TPU v7x, 768 devices: a whole 4x8x12 slice. The times are simulated.
768 devices in a mesh: row: 96 (over x, z, core), grp: 8 (over y).
Axes of the slice: x: 4, y: 8, z: 12, core: 2. Of those that a mesh axis runs over, the one named last changes fastest.
Arguments:
- source: bfloat16 [98304, 256], P(('row', 'grp')), may hold values from -0.5 to 0.5
- target: bfloat16 [98304, 256], P(('row', 'grp')), may hold values from -0.5 to 0.5
- pair_mask: int32 [96, 5], P('row'), may hold values from 0 to 1, as said below
Outputs:
- source_grad: float32 [98304, 256], P(('row', 'grp'))
- target_grad: float32 [98304, 256], P(('row', 'grp'))
Inputs may be any that keep to these rules, and one draw needn't show every extreme that they name: pair_mask[b, 2] = 1 for every block b: each source block is paired with the target block of the same index.
All inputs are finite; a program needn't handle non-finite values.
Results may differ from a plain program's by a relative error of at most 0.0035.
Values may be sent and summed in bfloat16 or wider, within the bound.
No kernel may reach another device: no remote copies, remote signals or barrier semaphores. Data moves between devices by JAX's collectives and lax.ppermute only.
A program may use at most 32 MiB of HBM per device.

v0:
```python
import jax
import jax.numpy as jnp
from jax import lax
from jax.sharding import PartitionSpec as P

ITERS = 3


EPS = 0.1
NEG = -1e30


def passed_along(block, axis, distance):
    devices = range(lax.axis_size(axis))
    route = [((i - distance) % len(devices), i) for i in devices]
    return lax.ppermute(block, axis, route)


def joined(shard, axis, combine):
    everything = jax.tree.map(lambda part: lax.all_gather(part, axis), shard)
    leading = jax.tree.map(lambda part: part[0], everything)

    def hop(k, so_far):
        return combine(so_far, jax.tree.map(lambda part: part[k], everything))

    return lax.fori_loop(1, lax.axis_size(axis), hop, leading)


def blend(earlier, later):
    highest = jnp.maximum(earlier[0], later[0])
    return (
        highest,
        earlier[1] * jnp.exp(earlier[0] - highest) + later[1] * jnp.exp(later[0] - highest),
    )


def pair_cost(rows_here, norms_here, window_span, window_norms):
    inner = jnp.einsum("ie,dje->dij", rows_here, window_span, preferred_element_type=jnp.float32)
    return norms_here[None, :, None] + window_norms[:, None, :] - 2.0 * inner


def shards(source, target, pair_mask):
    slot_count = pair_mask.shape[1]
    half_width = slot_count // 2
    slice_rows = source.shape[0]
    listed = pair_mask[0] == 1
    retain_mask = listed[:, None, None]
    gathered_rows = lax.all_gather(source, "grp", axis=0, tiled=True)
    pieces = []
    for slot_index in range(slot_count):
        if slot_index == half_width:
            pieces.append(target)
        else:
            pieces.append(passed_along(target, "row", half_width - slot_index))
    window_span = jnp.stack(pieces)
    block_norms = jnp.sum(jnp.square(gathered_rows.astype(jnp.float32)), axis=1)
    window_norms = jnp.sum(jnp.square(window_span.astype(jnp.float32)), axis=2)
    cost_tiles = pair_cost(gathered_rows, block_norms, window_span, window_norms)
    potentials = jnp.zeros((slot_count, slice_rows), jnp.float32)
    duals = jnp.zeros((gathered_rows.shape[0],), jnp.float32)
    for repeat_index in range(ITERS):
        scores = jnp.where(retain_mask, (potentials[:, None, :] - cost_tiles) / EPS, NEG)
        row_peak = jnp.max(scores, axis=(0, 2))
        row_sums = jnp.sum(jnp.exp(scores - row_peak[None, :, None]), axis=(0, 2))
        row_peak, row_sums = joined((row_peak, row_sums), "grp", blend)
        duals = -EPS * (row_peak + jnp.log(row_sums))
        scores = jnp.where(retain_mask, (duals[None, :, None] - cost_tiles) / EPS, NEG)
        col_peak = jnp.max(scores, axis=1)
        col_sums = jnp.sum(jnp.exp(scores - col_peak[:, None, :]), axis=1)
        nearby = {}
        for start_position in range(-2 * half_width, 2 * half_width + 1):
            if start_position == 0:
                nearby[start_position] = (col_peak, col_sums)
            else:
                nearby[start_position] = passed_along((col_peak, col_sums), "row", -start_position)
        new_rows = []
        for target_slot in range(slot_count):
            current = None
            for source_slot in range(slot_count):
                received = nearby[target_slot - source_slot]
                partial_value = (received[0][source_slot], received[1][source_slot])
                current = partial_value if current is None else blend(current, partial_value)
            new_rows.append(-EPS * (current[0] + jnp.log(current[1])))
        potentials = jnp.stack(new_rows)
    transport_plan = jnp.where(
        retain_mask,
        jnp.exp((duals[None, :, None] + potentials[:, None, :] - cost_tiles) / EPS),
        0.0,
    ).astype(jnp.bfloat16)
    row_mass = jnp.sum(transport_plan, axis=(0, 2), dtype=jnp.float32)
    carried_along = jnp.einsum(
        "buk,bka->ua", transport_plan, window_span, preferred_element_type=jnp.float32
    )
    source_grad = 2.0 * lax.psum_scatter(
        gathered_rows.astype(jnp.float32) * row_mass[:, None] - carried_along,
        "grp",
        scatter_dimension=0,
        tiled=True,
    )
    target_mass = jnp.sum(transport_plan, axis=1, dtype=jnp.float32)
    pulled_values = jnp.einsum(
        "nja,jq->naq", transport_plan, gathered_rows, preferred_element_type=jnp.float32
    )
    partials = window_span.astype(jnp.float32) * target_mass[:, :, None] - pulled_values
    collected = partials[half_width]
    for slot_index in range(slot_count):
        if slot_index != half_width:
            collected = collected + passed_along(
                partials[slot_index], "row", slot_index - half_width
            )
    target_grad = 2.0 * collected
    return (source_grad, target_grad)


def solution(mesh):
    placed = (P(("row", "grp"), None), P(("row", "grp"), None), P("row", None))
    return jax.shard_map(
        shards,
        mesh=mesh,
        in_specs=placed,
        out_specs=(P(("row", "grp"), None), P(("row", "grp"), None)),
        check_vma=False,
    )
```

profile of v0, /device:TPU:1, one launch (start us, length us, event | category | flops | bytes accessed | tf_op | source)
XLA Modules:
  0.0 447.7 jit_solution(16123128934436890702)
XLA Ops:
  7.2 5.4 %collective-permute-start.1 = (bf16[128,256]{1,0:T(8,128)(2,1)}, bf16[128,256]{1,0:T(8,128)(2,1)S(1)}, u32[]{:S(2)}, u32[]{:S(2)}) collective-permute-start(bf16[128,256]{1,0:T(8,128)(2,1)} %param.10), channel_id=1, source_target_pairs={{760,0},{0,8},{8,16},{16,24},{24,32},{32,40},{40,48},{48,56},{56,6... | collective-permute-start | bytes 196616 | tf_op jit(solution)/shard_map/ppermute | solution.py:16
  16.6 11.8 %collective-permute-start.3 = (bf16[128,256]{1,0:T(8,128)(2,1)}, bf16[128,256]{1,0:T(8,128)(2,1)S(1)}, u32[]{:S(2)}, u32[]{:S(2)}) collective-permute-start(bf16[128,256]{1,0:T(8,128)(2,1)} %param.10), channel_id=1, source_target_pairs={{16,0},{24,8},{32,16},{40,24},{48,32},{56,40},{64,48},{72,56},{80,... | collective-permute-start | bytes 196616 | tf_op jit(solution)/shard_map/ppermute | solution.py:16
  31.9 21.9 %all_gather.39 = bf16[1024,256]{1,0:T(8,128)(2,1)S(1)} all-gather(bf16[128,256]{1,0:T(8,128)(2,1)} %param.9), channel_id=1, replica_groups=mesh['row'=96,'grp'=8] {'grp'}, dimensions={0}, use_global_device_ids=true | all-gather | bytes 589824 | tf_op jit(solution)/shard_map/all_gather | solution.py:48
  55.9 18.3 %all-gather = f32[8192]{0:T(1024)S(1)} all-gather(f32[1024]{0:T(1024)S(1)} %get-tuple-element.456), channel_id=2, replica_groups=mesh['row'=96,'grp'=8] {'grp'}, dimensions={0}, use_global_device_ids=true | all-gather | bytes 36864 | tf_op jit(solution)/shard_map/all_gather | solution.py:20
  74.9 18.1 %all-gather.1 = f32[8192]{0:T(1024)S(1)} all-gather(f32[1024]{0:T(1024)S(1)} %exponential_reduce_fusion.5), channel_id=3, replica_groups=mesh['row'=96,'grp'=8] {'grp'}, dimensions={0}, use_global_device_ids=true | all-gather | bytes 36864 | tf_op jit(solution)/shard_map/all_gather | solution.py:20
  93.6 5.6 %while.51 = (s32[]{:T(128)}, f32[1024]{0:T(1024)S(1)}, f32[1024]{0:T(1024)S(1)}, f32[8,1024]{1,0:T(8,128)S(1)}, f32[8,1024]{1,0:T(8,128)}, /*index=5*/s32[]{:T(128)}, s32[]{:T(128)}, s32[]{:T(128)}) while((s32[]{:T(128)}, f32[1024]{0:T(1024)S(1)}, f32[1024]{0:T(1024)S(1)}, f32[8,1024]{1,0:T(8,128)S(1)}, f32[8,1024]{1,0:T(8,128)}, ...), condition=%wide.region_5.6_spmd, body=%wide.region_4.5_spmd.sunk | while | flops 6149 | bytes 41083 | solution.py:26
  104.1 22.6 %collective-permute-start.17 = (f32[5,128]{1,0:T(8,128)S(1)}, f32[5,128]{1,0:T(8,128)S(1)}, u32[]{:S(2)}, u32[]{:S(2)}) collective-permute-start(f32[5,128]{1,0:T(8,128)S(1)} %exponential_reduce_fusion.4), channel_id=1, source_target_pairs={{24,0},{32,8},{40,16},{48,24},{56,32},{64,40},{72,48},{80,56},{88,... | collective-permute-start | bytes 7688 | tf_op jit(solution)/shard_map/ppermute | solution.py:16
  139.9 4.3 collective-permute-start.11
  144.2 5.9 %collective-permute-start.10 = (f32[5,128]{1,0:T(8,128)S(1)}, f32[5,128]{1,0:T(8,128)S(1)}, u32[]{:S(2)}, u32[]{:S(2)}) collective-permute-start(f32[5,128]{1,0:T(8,128)S(1)} %exponential_reduce_fusion.4), channel_id=1, source_target_pairs={{744,0},{752,8},{760,16},{0,24},{8,32},{16,40},{24,48},{32,56},{40... | collective-permute-start | bytes 7688 | tf_op jit(solution)/shard_map/ppermute | solution.py:16
  175.9 18.1 %all-gather.2 = f32[8192]{0:T(1024)S(1)} all-gather(f32[1024]{0:T(1024)S(1)} %fusion.2), channel_id=4, replica_groups=mesh['row'=96,'grp'=8] {'grp'}, dimensions={0}, use_global_device_ids=true | all-gather | bytes 36864 | tf_op jit(solution)/shard_map/all_gather | solution.py:20
  194.0 18.1 %all-gather.3 = f32[8192]{0:T(1024)S(1)} all-gather(f32[1024]{0:T(1024)S(1)} %exponential_reduce_fusion.3), channel_id=5, replica_groups=mesh['row'=96,'grp'=8] {'grp'}, dimensions={0}, use_global_device_ids=true | all-gather | bytes 36864 | tf_op jit(solution)/shard_map/all_gather | solution.py:20
  212.7 5.6 %while.52 = (s32[]{:T(128)}, f32[1024]{0:T(1024)S(1)}, f32[1024]{0:T(1024)S(1)}, f32[8,1024]{1,0:T(8,128)S(1)}, f32[8,1024]{1,0:T(8,128)}, /*index=5*/s32[]{:T(128)}, s32[]{:T(128)}, s32[]{:T(128)}) while((s32[]{:T(128)}, f32[1024]{0:T(1024)S(1)}, f32[1024]{0:T(1024)S(1)}, f32[8,1024]{1,0:T(8,128)S(1)}, f32[8,1024]{1,0:T(8,128)}, ...), condition=%wide.region_11.12_spmd, body=%wide.region_10.11_spmd.sunk | while | flops 6149 | bytes 41083 | solution.py:26
  222.4 18.5 %collective-permute-start.33 = (f32[5,128]{1,0:T(8,128)S(1)}, f32[5,128]{1,0:T(8,128)S(1)}, u32[]{:S(2)}, u32[]{:S(2)}) collective-permute-start(f32[5,128]{1,0:T(8,128)S(1)} %exponential_reduce_fusion.2), channel_id=1, source_target_pairs={{24,0},{32,8},{40,16},{48,24},{56,32},{64,40},{72,48},{80,56},{88,... | collective-permute-start | bytes 7688 | tf_op jit(solution)/shard_map/ppermute | solution.py:16
  257.7 5.9 %collective-permute-start.26 = (f32[5,128]{1,0:T(8,128)S(1)}, f32[5,128]{1,0:T(8,128)S(1)}, u32[]{:S(2)}, u32[]{:S(2)}) collective-permute-start(f32[5,128]{1,0:T(8,128)S(1)} %exponential_reduce_fusion.2), channel_id=1, source_target_pairs={{744,0},{752,8},{760,16},{0,24},{8,32},{16,40},{24,48},{32,56},{40... | collective-permute-start | bytes 7688 | tf_op jit(solution)/shard_map/ppermute | solution.py:16
  283.9 4.2 collective-permute-done.22
  289.3 18.1 %all-gather.4 = f32[8192]{0:T(1024)S(1)} all-gather(f32[1024]{0:T(1024)S(1)} %fusion.4), channel_id=6, replica_groups=mesh['row'=96,'grp'=8] {'grp'}, dimensions={0}, use_global_device_ids=true | all-gather | bytes 36864 | tf_op jit(solution)/shard_map/all_gather | solution.py:20
  307.5 18.1 %all-gather.5 = f32[8192]{0:T(1024)S(1)} all-gather(f32[1024]{0:T(1024)S(1)} %exponential_reduce_fusion.1), channel_id=7, replica_groups=mesh['row'=96,'grp'=8] {'grp'}, dimensions={0}, use_global_device_ids=true | all-gather | bytes 36864 | tf_op jit(solution)/shard_map/all_gather | solution.py:20
  326.2 5.6 %while.53 = (s32[]{:T(128)}, f32[1024]{0:T(1024)S(1)}, f32[1024]{0:T(1024)S(1)}, f32[8,1024]{1,0:T(8,128)S(1)}, f32[8,1024]{1,0:T(8,128)}, /*index=5*/s32[]{:T(128)}, s32[]{:T(128)}, s32[]{:T(128)}) while((s32[]{:T(128)}, f32[1024]{0:T(1024)S(1)}, f32[1024]{0:T(1024)S(1)}, f32[8,1024]{1,0:T(8,128)S(1)}, f32[8,1024]{1,0:T(8,128)}, ...), condition=%wide.region_17.18_spmd, body=%wide.region_16.17_spmd.sunk | while | flops 6149 | bytes 41083 | solution.py:26
  336.3 18.5 %collective-permute-start.49 = (f32[5,128]{1,0:T(8,128)S(1)}, f32[5,128]{1,0:T(8,128)S(1)}, u32[]{:S(2)}, u32[]{:S(2)}) collective-permute-start(f32[5,128]{1,0:T(8,128)S(1)} %exponential_reduce_fusion), channel_id=1, source_target_pairs={{24,0},{32,8},{40,16},{48,24},{56,32},{64,40},{72,48},{80,56},{88,... | collective-permute-start | bytes 7688 | tf_op jit(solution)/shard_map/ppermute | solution.py:16
  367.1 4.5 %collective-permute-start.43 = (f32[5,128]{1,0:T(8,128)S(1)}, f32[5,128]{1,0:T(8,128)S(1)}, u32[]{:S(2)}, u32[]{:S(2)}) collective-permute-start(f32[5,128]{1,0:T(8,128)S(1)} %exponential_reduce_fusion), channel_id=1, source_target_pairs={{736,0},{744,8},{752,16},{760,24},{0,32},{8,40},{16,48},{24,56},{3... | collective-permute-start | bytes 7688 | tf_op jit(solution)/shard_map/ppermute | solution.py:16
  371.7 6.1 %collective-permute-start.42 = (f32[5,128]{1,0:T(8,128)S(1)}, f32[5,128]{1,0:T(8,128)S(1)}, u32[]{:S(2)}, u32[]{:S(2)}) collective-permute-start(f32[5,128]{1,0:T(8,128)S(1)} %exponential_reduce_fusion), channel_id=1, source_target_pairs={{744,0},{752,8},{760,16},{0,24},{8,32},{16,40},{24,48},{32,56},{40... | collective-permute-start | bytes 7688 | tf_op jit(solution)/shard_map/ppermute | solution.py:16
  397.9 4.4 collective-permute-done.38
  419.3 4.7 %collective-permute-done.53 = f32[128,256]{1,0:T(8,128)S(1)} collective-permute-done((f32[128,256]{1,0:T(8,128)S(1)}, f32[128,256]{1,0:T(8,128)S(1)}, u32[]{:S(2)}, u32[]{:S(2)}) %collective-permute-start.53) | collective-permute-done | bytes 131104 | tf_op jit(solution)/shard_map/ppermute | solution.py:16
  424.7 14.6 %reduce-scatter.2.cloned.1.call-done = f32[128,256]{1,0:T(8,128)} async-done(((f32[1024,256]{1,0:T(8,128)}), f32[128,256]{1,0:T(8,128)}) %reduce-scatter.2.cloned.1.call-update) | async-done | bytes 131088 | tf_op jit(solution)/shard_map/reduce_scatter | solution.py:94
  (204 shorter events, 170.3 us)
Async XLA Ops:
  7.2 432.1 %reduce-scatter.2.cloned.1.call-start = ((), (), s32[]{:S(2)}) async-start(), calls=%async_computation.1 | async-start | bytes 1179648 | tf_op jit(solution)/shard_map/reduce_scatter | solution.py:94
  7.2 46.8 %collective-permute-start.1 = (bf16[128,256]{1,0:T(8,128)(2,1)}, bf16[128,256]{1,0:T(8,128)(2,1)S(1)}, u32[]{:S(2)}, u32[]{:S(2)}) collective-permute-start(bf16[128,256]{1,0:T(8,128)(2,1)} %param.10), channel_id=1, source_target_pairs={{760,0},{0,8},{8,16},{16,24},{24,32},{32,40},{40,48},{48,56},{56,6... | collective-permute-start | bytes 196616 | tf_op jit(solution)/shard_map/ppermute | solution.py:16
  12.6 41.4 %collective-permute-start = (bf16[128,256]{1,0:T(8,128)(2,1)}, bf16[128,256]{1,0:T(8,128)(2,1)S(1)}, u32[]{:S(2)}, u32[]{:S(2)}) collective-permute-start(bf16[128,256]{1,0:T(8,128)(2,1)} %param.10), channel_id=1, source_target_pairs={{752,0},{760,8},{0,16},{8,24},{16,32},{24,40},{32,48},{40,56},{48,... | collective-permute-start | bytes 196616 | tf_op jit(solution)/shard_map/ppermute | solution.py:16
  16.6 38.3 %collective-permute-start.3 = (bf16[128,256]{1,0:T(8,128)(2,1)}, bf16[128,256]{1,0:T(8,128)(2,1)S(1)}, u32[]{:S(2)}, u32[]{:S(2)}) collective-permute-start(bf16[128,256]{1,0:T(8,128)(2,1)} %param.10), channel_id=1, source_target_pairs={{16,0},{24,8},{32,16},{40,24},{48,32},{56,40},{64,48},{72,56},{80,... | collective-permute-start | bytes 196616 | tf_op jit(solution)/shard_map/ppermute | solution.py:16
  28.4 26.5 %collective-permute-start.2 = (bf16[128,256]{1,0:T(8,128)(2,1)}, bf16[128,256]{1,0:T(8,128)(2,1)S(1)}, u32[]{:S(2)}, u32[]{:S(2)}) collective-permute-start(bf16[128,256]{1,0:T(8,128)(2,1)} %param.10), channel_id=1, source_target_pairs={{8,0},{16,8},{24,16},{32,24},{40,32},{48,40},{56,48},{64,56},{72,6... | collective-permute-start | bytes 196616 | tf_op jit(solution)/shard_map/ppermute | solution.py:16
  100.4 32.7 %collective-permute-start.19 = (f32[5,128]{1,0:T(8,128)S(1)}, f32[5,128]{1,0:T(8,128)S(1)}, u32[]{:S(2)}, u32[]{:S(2)}) collective-permute-start(f32[5,128]{1,0:T(8,128)S(1)} %exponential_reduce_fusion.4), channel_id=1, source_target_pairs={{32,0},{40,8},{48,16},{56,24},{64,32},{72,40},{80,48},{88,56},{96,... | collective-permute-start | bytes 7688 | tf_op jit(solution)/shard_map/ppermute | solution.py:16
  104.1 31.6 %collective-permute-start.17 = (f32[5,128]{1,0:T(8,128)S(1)}, f32[5,128]{1,0:T(8,128)S(1)}, u32[]{:S(2)}, u32[]{:S(2)}) collective-permute-start(f32[5,128]{1,0:T(8,128)S(1)} %exponential_reduce_fusion.4), channel_id=1, source_target_pairs={{24,0},{32,8},{40,16},{48,24},{56,32},{64,40},{72,48},{80,56},{88,... | collective-permute-start | bytes 7688 | tf_op jit(solution)/shard_map/ppermute | solution.py:16
  133.1 17.1 %collective-permute-start.16 = (f32[5,128]{1,0:T(8,128)S(1)}, f32[5,128]{1,0:T(8,128)S(1)}, u32[]{:S(2)}, u32[]{:S(2)}) collective-permute-start(f32[5,128]{1,0:T(8,128)S(1)} %fusion.1), channel_id=1, source_target_pairs={{24,0},{32,8},{40,16},{48,24},{56,32},{64,40},{72,48},{80,56},{88,... | collective-permute-start | bytes 7688 | tf_op jit(solution)/shard_map/ppermute | solution.py:16
  135.6 17.7 %collective-permute-start.14 = (f32[5,128]{1,0:T(8,128)S(1)}, f32[5,128]{1,0:T(8,128)S(1)}, u32[]{:S(2)}, u32[]{:S(2)}) collective-permute-start(f32[5,128]{1,0:T(8,128)S(1)} %fusion.1), channel_id=1, source_target_pairs={{16,0},{24,8},{32,16},{40,24},{48,32},{56,40},{64,48},{72,56},{80,... | collective-permute-start | bytes 7688 | tf_op jit(solution)/shard_map/ppermute | solution.py:16
  137.6 17.8 %collective-permute-start.12 = (f32[5,128]{1,0:T(8,128)S(1)}, f32[5,128]{1,0:T(8,128)S(1)}, u32[]{:S(2)}, u32[]{:S(2)}) collective-permute-start(f32[5,128]{1,0:T(8,128)S(1)} %fusion.1), channel_id=1, source_target_pairs={{8,0},{16,8},{24,16},{32,24},{40,32},{48,40},{56,48},{64,56},{72,6... | collective-permute-start | bytes 7688 | tf_op jit(solution)/shard_map/ppermute | solution.py:16
  139.9 34.8 %collective-permute-start.11 = (f32[5,128]{1,0:T(8,128)S(1)}, f32[5,128]{1,0:T(8,128)S(1)}, u32[]{:S(2)}, u32[]{:S(2)}) collective-permute-start(f32[5,128]{1,0:T(8,128)S(1)} %exponential_reduce_fusion.4), channel_id=1, source_target_pairs={{736,0},{744,8},{752,16},{760,24},{0,32},{8,40},{16,48},{24,56},{3... | collective-permute-start | bytes 7688 | tf_op jit(solution)/shard_map/ppermute | solution.py:16
  144.2 26.3 %collective-permute-start.10 = (f32[5,128]{1,0:T(8,128)S(1)}, f32[5,128]{1,0:T(8,128)S(1)}, u32[]{:S(2)}, u32[]{:S(2)}) collective-permute-start(f32[5,128]{1,0:T(8,128)S(1)} %exponential_reduce_fusion.4), channel_id=1, source_target_pairs={{744,0},{752,8},{760,16},{0,24},{8,32},{16,40},{24,48},{32,56},{40... | collective-permute-start | bytes 7688 | tf_op jit(solution)/shard_map/ppermute | solution.py:16
  219.5 27.5 %collective-permute-start.35 = (f32[5,128]{1,0:T(8,128)S(1)}, f32[5,128]{1,0:T(8,128)S(1)}, u32[]{:S(2)}, u32[]{:S(2)}) collective-permute-start(f32[5,128]{1,0:T(8,128)S(1)} %exponential_reduce_fusion.2), channel_id=1, source_target_pairs={{32,0},{40,8},{48,16},{56,24},{64,32},{72,40},{80,48},{88,56},{96,... | collective-permute-start | bytes 7688 | tf_op jit(solution)/shard_map/ppermute | solution.py:16
  222.4 26.6 %collective-permute-start.33 = (f32[5,128]{1,0:T(8,128)S(1)}, f32[5,128]{1,0:T(8,128)S(1)}, u32[]{:S(2)}, u32[]{:S(2)}) collective-permute-start(f32[5,128]{1,0:T(8,128)S(1)} %exponential_reduce_fusion.2), channel_id=1, source_target_pairs={{24,0},{32,8},{40,16},{48,24},{56,32},{64,40},{72,48},{80,56},{88,... | collective-permute-start | bytes 7688 | tf_op jit(solution)/shard_map/ppermute | solution.py:16
  249.0 18.1 %collective-permute-start.30 = (f32[5,128]{1,0:T(8,128)S(1)}, f32[5,128]{1,0:T(8,128)S(1)}, u32[]{:S(2)}, u32[]{:S(2)}) collective-permute-start(f32[5,128]{1,0:T(8,128)S(1)} %fusion.3), channel_id=1, source_target_pairs={{16,0},{24,8},{32,16},{40,24},{48,32},{56,40},{64,48},{72,56},{80,... | collective-permute-start | bytes 7688 | tf_op jit(solution)/shard_map/ppermute | solution.py:16
  252.5 17.1 %collective-permute-start.28 = (f32[5,128]{1,0:T(8,128)S(1)}, f32[5,128]{1,0:T(8,128)S(1)}, u32[]{:S(2)}, u32[]{:S(2)}) collective-permute-start(f32[5,128]{1,0:T(8,128)S(1)} %fusion.3), channel_id=1, source_target_pairs={{8,0},{16,8},{24,16},{32,24},{40,32},{48,40},{56,48},{64,56},{72,6... | collective-permute-start | bytes 7688 | tf_op jit(solution)/shard_map/ppermute | solution.py:16
  254.5 33.7 %collective-permute-start.27 = (f32[5,128]{1,0:T(8,128)S(1)}, f32[5,128]{1,0:T(8,128)S(1)}, u32[]{:S(2)}, u32[]{:S(2)}) collective-permute-start(f32[5,128]{1,0:T(8,128)S(1)} %exponential_reduce_fusion.2), channel_id=1, source_target_pairs={{736,0},{744,8},{752,16},{760,24},{0,32},{8,40},{16,48},{24,56},{3... | collective-permute-start | bytes 7688 | tf_op jit(solution)/shard_map/ppermute | solution.py:16
  257.7 26.2 %collective-permute-start.26 = (f32[5,128]{1,0:T(8,128)S(1)}, f32[5,128]{1,0:T(8,128)S(1)}, u32[]{:S(2)}, u32[]{:S(2)}) collective-permute-start(f32[5,128]{1,0:T(8,128)S(1)} %exponential_reduce_fusion.2), channel_id=1, source_target_pairs={{744,0},{752,8},{760,16},{0,24},{8,32},{16,40},{24,48},{32,56},{40... | collective-permute-start | bytes 7688 | tf_op jit(solution)/shard_map/ppermute | solution.py:16
  333.0 28.0 %collective-permute-start.51 = (f32[5,128]{1,0:T(8,128)S(1)}, f32[5,128]{1,0:T(8,128)S(1)}, u32[]{:S(2)}, u32[]{:S(2)}) collective-permute-start(f32[5,128]{1,0:T(8,128)S(1)} %exponential_reduce_fusion), channel_id=1, source_target_pairs={{32,0},{40,8},{48,16},{56,24},{64,32},{72,40},{80,48},{88,56},{96,... | collective-permute-start | bytes 7688 | tf_op jit(solution)/shard_map/ppermute | solution.py:16
  336.3 26.6 %collective-permute-start.49 = (f32[5,128]{1,0:T(8,128)S(1)}, f32[5,128]{1,0:T(8,128)S(1)}, u32[]{:S(2)}, u32[]{:S(2)}) collective-permute-start(f32[5,128]{1,0:T(8,128)S(1)} %exponential_reduce_fusion), channel_id=1, source_target_pairs={{24,0},{32,8},{40,16},{48,24},{56,32},{64,40},{72,48},{80,56},{88,... | collective-permute-start | bytes 7688 | tf_op jit(solution)/shard_map/ppermute | solution.py:16
  362.9 18.2 %collective-permute-start.46 = (f32[5,128]{1,0:T(8,128)S(1)}, f32[5,128]{1,0:T(8,128)S(1)}, u32[]{:S(2)}, u32[]{:S(2)}) collective-permute-start(f32[5,128]{1,0:T(8,128)S(1)} %fusion.5), channel_id=1, source_target_pairs={{16,0},{24,8},{32,16},{40,24},{48,32},{56,40},{64,48},{72,56},{80,... | collective-permute-start | bytes 7688 | tf_op jit(solution)/shard_map/ppermute | solution.py:16
  365.0 18.6 %collective-permute-start.44 = (f32[5,128]{1,0:T(8,128)S(1)}, f32[5,128]{1,0:T(8,128)S(1)}, u32[]{:S(2)}, u32[]{:S(2)}) collective-permute-start(f32[5,128]{1,0:T(8,128)S(1)} %fusion.5), channel_id=1, source_target_pairs={{8,0},{16,8},{24,16},{32,24},{40,32},{48,40},{56,48},{64,56},{72,6... | collective-permute-start | bytes 7688 | tf_op jit(solution)/shard_map/ppermute | solution.py:16
  367.1 35.2 %collective-permute-start.43 = (f32[5,128]{1,0:T(8,128)S(1)}, f32[5,128]{1,0:T(8,128)S(1)}, u32[]{:S(2)}, u32[]{:S(2)}) collective-permute-start(f32[5,128]{1,0:T(8,128)S(1)} %exponential_reduce_fusion), channel_id=1, source_target_pairs={{736,0},{744,8},{752,16},{760,24},{0,32},{8,40},{16,48},{24,56},{3... | collective-permute-start | bytes 7688 | tf_op jit(solution)/shard_map/ppermute | solution.py:16
  371.7 26.2 %collective-permute-start.42 = (f32[5,128]{1,0:T(8,128)S(1)}, f32[5,128]{1,0:T(8,128)S(1)}, u32[]{:S(2)}, u32[]{:S(2)}) collective-permute-start(f32[5,128]{1,0:T(8,128)S(1)} %exponential_reduce_fusion), channel_id=1, source_target_pairs={{744,0},{752,8},{760,16},{0,24},{8,32},{16,40},{24,48},{32,56},{40... | collective-permute-start | bytes 7688 | tf_op jit(solution)/shard_map/ppermute | solution.py:16
  (34 other events, 352.6 us)
Sparse Core Ops, SparseCore 0:
  406.2 33.0 reduce-scatter.1
where the time goes:
time: 454 us; the launch traced here: 448 us
  starting transfers between devices  229 us (50%)
  blocking collectives  131 us (29%)
  waiting for transfers between devices  37.1 us (8%)
  local copies, waits for them, and re-layouts  20.2 us (4%)
  between operations  15 us (3%)
  other arithmetic  11.4 us (3%)
    ppermute x56, starting transfers between devices, passed_along(): return lax.ppermute(block, axis, route)  229 us
    all_gather x6, blocking collectives, joined(): everything = jax.tree.map(lambda part: lax.all_gather(part, axis), shard)  109 us
    ppermute x56, waiting for transfers between devices, passed_along(): return lax.ppermute(block, axis, route)  22.5 us
    all_gather x1, blocking collectives, shards(): gathered_rows = lax.all_gather(source, 'grp', axis=0, tiled=True)  21.9 us
    dynamic_slice x21, local copies, waits for them, and re-layouts, hop(): return combine(so_far, jax.tree.map(lambda part: part[k], everything))  16.2 us
    reduce_scatter x1, waiting for transfers between devices, shards(): lax.psum_scatter(gathered_rows.astype(jnp.float32) * row_mass[:, None] -...  14.6 us
  transfers between devices with their start and end apart: 57, of which 8 were waited for; matrix products, arithmetic and copies ran while one was open for 1% of the time, Pallas kernels for 0%

commit v1 on v0

v1 whole, which is shorter than its diff:
```python
import functools
import math

import jax
import jax.numpy as jnp
from jax import lax
from jax.experimental import pallas as pl
from jax.experimental.pallas import tpu as pltpu
from jax.sharding import PartitionSpec as P

ITERS = 3
EPS = 0.1
NEG = -1e30
KAPPA = 1.0 / (EPS * math.log(2.0))
TWO_KAPPA = 2.0 * KAPPA
SAFE_SUM = 2.0 ** -60
LANES = 128
WINDOW = 5


def from_row(block, source_of):
    count = lax.axis_size("row")
    return lax.ppermute(block, "row", [(source_of(i), i) for i in range(count)])


def swap_mate(block):
    return from_row(block, lambda i: i ^ 1)


def shifted(block, distance):
    count = lax.axis_size("row")
    return from_row(block, lambda i: (i - distance) % count)


def from_chip(block, reach):
    count = lax.axis_size("row")

    def source_of(i):
        step = -2 * reach if i % 2 == 0 else 2 * reach
        return (i + step) % count

    return from_row(block, source_of)


def swap_cross(block):
    count = lax.axis_size("row")
    return from_row(block, lambda i: (i - 1 if i % 2 == 0 else i + 1) % count)


def gathered(shard):
    count = lax.axis_size("grp")
    copies = jnp.broadcast_to(shard[None], (count,) + shard.shape)
    return lax.all_to_all(copies, "grp", 0, 0, tiled=True).reshape(-1, shard.shape[1])


def lse2(a, b):
    top = jnp.maximum(a, b)
    return top + jnp.log2(jnp.exp2(a - top) + jnp.exp2(b - top))


def column_totals(partial, even):
    own, mate, cross, up, down = (partial[p] for p in range(WINDOW))
    none = jnp.full_like(own, NEG)
    six = jnp.where(
        even,
        jnp.stack([down, cross, own, mate, up, none]),
        jnp.stack([none, down, mate, own, cross, up]),
    )
    chip = lse2(six, swap_mate(six))
    near = from_chip(jnp.where(even, chip[2:6], chip[0:4]), 1)
    far = from_chip(jnp.where(even, chip[4:6], chip[0:2]), 2)
    blank = jnp.full_like(far, NEG)
    outer = jnp.where(
        even,
        jnp.concatenate([lse2(near[0:2], far), near[2:4], blank]),
        jnp.concatenate([blank, near[0:2], lse2(near[2:4], far)]),
    )
    total = lse2(chip, lse2(outer, swap_mate(outer)))
    return jnp.where(
        even,
        jnp.stack([total[2], total[3], total[1], total[4], total[0]]),
        jnp.stack([total[3], total[2], total[4], total[5], total[1]]),
    )


def dot_nt(a, b):
    return lax.dot_general(a, b, (((1,), (1,)), ((), ())), preferred_element_type=jnp.float32)


def step_kernel(first, listed, pot, rows, t0, t1, t2, t3, t4, sums_out, dual_out, bias, scores, peak, col):
    targets = (t0, t1, t2, t3, t4)
    count = rows.shape[0]
    tile = min(256, count)
    for p in range(WINDOW):
        if first:
            sq = jnp.square(targets[p][...].astype(jnp.float32))
            high = sq.astype(jnp.bfloat16)
            low = (sq - high.astype(jnp.float32)).astype(jnp.bfloat16)
            ones = jnp.ones((8, sq.shape[1]), jnp.bfloat16)
            row = -KAPPA * (dot_nt(ones, high) + dot_nt(ones, low))[0:1]
        else:
            row = pot[p : p + 1, :]
        bias[p : p + 1, :] = jnp.where(listed[p] == 1, row, NEG)

    peak[...] = jnp.full(peak.shape, NEG, jnp.float32)
    for p in range(WINDOW):

        def fill(c, carry, p=p):
            at = pl.multiple_of(c * tile, tile)
            inner = dot_nt(rows[...], targets[p][pl.ds(at, tile), :])
            block = inner * TWO_KAPPA + bias[p : p + 1, pl.ds(at, tile)]
            scores[:, pl.ds(pl.multiple_of(p * count + at, tile), tile)] = block
            best = peak[...]
            for q in range(tile // LANES):
                best = jnp.maximum(best, block[:, q * LANES : (q + 1) * LANES])
            peak[...] = best
            return carry

        lax.fori_loop(0, count // tile, fill, 0)

    col[...] = jnp.zeros(col.shape, jnp.float32)
    width = WINDOW * count // LANES

    def chunk(r, carry):
        here = pl.ds(pl.multiple_of(r * LANES, LANES), LANES)
        top = jnp.max(peak[here, :], axis=1, keepdims=True)
        acc = jnp.zeros((LANES, LANES), jnp.float32)
        for q in range(width):
            e = jnp.exp2(scores[here, q * LANES : (q + 1) * LANES] - top)
            scores[here, q * LANES : (q + 1) * LANES] = e
            acc = acc + e
        total = jnp.sum(acc, axis=1, keepdims=True)
        dual_out[here, :] = jnp.broadcast_to(-(top + jnp.log2(total)), (LANES, LANES))
        scale = jnp.broadcast_to(1.0 / total, (LANES, LANES))
        for q in range(width):
            e = scores[here, q * LANES : (q + 1) * LANES] * scale
            col[:, q * LANES : (q + 1) * LANES] += jnp.sum(e.reshape(LANES // 8, 8, LANES), axis=0)
        return carry

    lax.fori_loop(0, count // LANES, chunk, 0)

    sums_out[...] = jnp.full(sums_out.shape, NEG, jnp.float32)
    for p in range(WINDOW):
        total = jnp.sum(col[:, p * count : (p + 1) * count], axis=0, keepdims=True)
        safe = jnp.min(total) >= SAFE_SUM
        usable = listed[p] == 1

        @pl.when(jnp.logical_and(usable, safe))
        def _(p=p, total=total):
            sums_out[p : p + 1, :] = jnp.log2(total) - bias[p : p + 1, :]

        @pl.when(jnp.logical_and(usable, jnp.logical_not(safe)))
        def _(p=p):
            def value(r):
                here = pl.ds(pl.multiple_of(r * LANES, LANES), LANES)
                return dot_nt(rows[here, :], targets[p][...]) * TWO_KAPPA + dual_out[here, 0:1]

            def find(r, best):
                return jnp.maximum(best, jnp.max(value(r), axis=0, keepdims=True))

            best = lax.fori_loop(0, count // LANES, find, jnp.full((1, count), NEG, jnp.float32))

            def add(r, acc):
                return acc + jnp.sum(jnp.exp2(value(r) - best), axis=0, keepdims=True)

            acc = lax.fori_loop(0, count // LANES, add, jnp.zeros((1, count), jnp.float32))
            sums_out[p : p + 1, :] = best + jnp.log2(acc)


def step(first, listed, pot, rows, targets):
    count, width = rows.shape
    vmem = pl.BlockSpec(memory_space=pltpu.VMEM)
    pairs = WINDOW * count * count
    return pl.pallas_call(
        functools.partial(step_kernel, first),
        out_shape=(
            jax.ShapeDtypeStruct((8, count), jnp.float32),
            jax.ShapeDtypeStruct((count, LANES), jnp.float32),
        ),
        in_specs=[pl.BlockSpec(memory_space=pltpu.SMEM)] + [vmem] * 7,
        out_specs=(vmem, vmem),
        scratch_shapes=[
            pltpu.VMEM((8, count), jnp.float32),
            pltpu.VMEM((count, WINDOW * count), jnp.float32),
            pltpu.VMEM((count, LANES), jnp.float32),
            pltpu.VMEM((8, WINDOW * count), jnp.float32),
        ],
        compiler_params=pltpu.CompilerParams(vmem_limit_bytes=44 * 1024 * 1024),
        cost_estimate=pl.CostEstimate(
            flops=2 * pairs * width, bytes_accessed=12 * count * width, transcendentals=pairs
        ),
        name="sinkhorn_step",
    )(listed, pot, rows, *targets)


def grad_kernel(scal, pot, dual, mine, rows, t0, t1, t2, t3, t4, source_out, o0, o1, o2, o3, o4):
    targets = (t0, t1, t2, t3, t4)
    outs = (o0, o1, o2, o3, o4)
    count = rows.shape[0]
    at = pl.multiple_of(scal[WINDOW] * LANES, LANES)
    here = pl.ds(at, LANES)
    own_dual = dual[here, 0:1]
    dual_row = jnp.concatenate(
        [dual[r * LANES : (r + 1) * LANES, :].T[0:1, :] for r in range(count // LANES)], axis=1
    )
    mass = jnp.zeros((LANES, 1), jnp.float32)
    carried = jnp.zeros((LANES, rows.shape[1]), jnp.float32)
    for p in range(WINDOW):
        bias = jnp.where(scal[p] == 1, pot[p : p + 1, :], NEG)
        weight = jnp.exp2(dot_nt(mine[...], targets[p][...]) * TWO_KAPPA + (own_dual + bias))
        weight = weight.astype(jnp.bfloat16)
        mass = mass + jnp.sum(weight.astype(jnp.float32), axis=1, keepdims=True)
        carried = carried + jnp.dot(weight, targets[p][...], preferred_element_type=jnp.float32)
    source_out[...] = 2.0 * (mine[...].astype(jnp.float32) * mass - carried)

    for p in range(WINDOW):
        bias = jnp.where(scal[p] == 1, pot[p : p + 1, here], NEG)
        bias = jnp.broadcast_to(bias, (LANES, LANES)).T[:, 0:1]
        some = targets[p][here, :]
        weight = jnp.exp2(dot_nt(some, rows[...]) * TWO_KAPPA + (dual_row + bias))
        weight = weight.astype(jnp.bfloat16)
        mass = jnp.sum(weight.astype(jnp.float32), axis=1, keepdims=True)
        pulled = jnp.dot(weight, rows[...], preferred_element_type=jnp.float32)
        outs[p][...] = some.astype(jnp.float32) * mass - pulled


def gradients(scal, pot, dual, mine, rows, targets):
    count, width = rows.shape
    vmem = pl.BlockSpec(memory_space=pltpu.VMEM)
    part = jax.ShapeDtypeStruct((LANES, width), jnp.float32)
    pairs = 2 * WINDOW * count * LANES
    return pl.pallas_call(
        grad_kernel,
        out_shape=(part,) * (1 + WINDOW),
        in_specs=[pl.BlockSpec(memory_space=pltpu.SMEM)] + [vmem] * 9,
        out_specs=(vmem,) * (1 + WINDOW),
        compiler_params=pltpu.CompilerParams(vmem_limit_bytes=44 * 1024 * 1024),
        cost_estimate=pl.CostEstimate(
            flops=4 * pairs * width, bytes_accessed=16 * count * width, transcendentals=pairs
        ),
        name="plan_gradients",
    )(scal, pot, dual, mine, rows, *targets)


def shards(source, target, pair_mask):
    even = lax.axis_index("row") % 2 == 0
    own = gathered(target)
    above = shifted(own, -2)
    below = shifted(own, 2)
    mate = swap_mate(own)
    cross = swap_mate(jnp.where(even, above, below))
    rows = gathered(source)
    targets = (own, mate, cross, above, below)
    mask = pair_mask[0]
    listed = jnp.where(even, mask[jnp.array([2, 3, 1, 4, 0])], mask[jnp.array([2, 1, 3, 4, 0])])
    pot = jnp.zeros((WINDOW, own.shape[0]), jnp.float32)
    dual = None
    for k in range(ITERS):
        partial, dual = step(k == 0, listed, pot, rows, targets)
        pot = -column_totals(partial, even)
    scal = jnp.concatenate([listed, lax.axis_index("grp").astype(jnp.int32)[None]])
    source_grad, part_own, part_mate, part_cross, part_above, part_below = gradients(
        scal, pot, dual, source, rows, targets
    )
    total = (
        part_own
        + swap_mate(part_mate)
        + swap_cross(part_cross)
        + shifted(part_above, 2)
        + shifted(part_below, -2)
    )
    return source_grad, 2.0 * total


def solution(mesh):
    placed = (P(("row", "grp"), None), P(("row", "grp"), None), P("row", None))
    return jax.shard_map(
        shards,
        mesh=mesh,
        in_specs=placed,
        out_specs=(P(("row", "grp"), None), P(("row", "grp"), None)),
        check_vma=False,
    )
```

time: 454 us -> 250 us (0.55)
  blocking collectives: 131 us -> 19.8 us
  starting transfers between devices: 229 us -> 153 us
  Pallas kernels: 0 us -> 51.5 us
  waiting for transfers between devices: 37.1 us -> 12.2 us
  local copies, waits for them, and re-layouts: 20.2 us -> 5.28 us
  between operations: 15 us -> 1.17 us
  other arithmetic: 11.4 us -> 2.37 us
    all_gather x7 -> x0, blocking collectives: 131 us -> none  [the longest x6 109 us: joined(): everything = jax.tree.map(lambda part: lax.all_gather(part, axis), shard)]
    ppermute x56 -> x20, starting transfers between devices: 229 us -> 150 us  [from_row(): return lax.ppermute(block, 'row', [(source_of(i), i) for i in range(count)])]
    pallas_call x0 -> x4, Pallas kernels: none -> 51.5 us  [the longest x3 47.6 us: step(): pl.pallas_call(functools.partial(step_kernel, first), out_shape=(jax.Shap...]
    all_to_all x0 -> x1, blocking collectives: none -> 19.8 us  [gathered(): lax.all_to_all(copies, 'grp', 0, 0, tiled=True).reshape(-1, shard.shape[1])]
    dynamic_slice x21 -> x0, local copies, waits for them, and re-layouts: 16.2 us -> none  [hop(): return combine(so_far, jax.tree.map(lambda part: part[k], everything))]
    reduce_scatter x1 -> x0, waiting for transfers between devices: 14.6 us -> none  [shards(): lax.psum_scatter(gathered_rows.astype(jnp.float32) * row_mass[:, None] -...]
    ppermute x56 -> x20, waiting for transfers between devices: 22.5 us -> 9.53 us  [from_row(): return lax.ppermute(block, 'row', [(source_of(i), i) for i in range(count)])]
    reduce_sum x9 -> x0, other arithmetic: 5.64 us -> none  [the longest x3 2.25 us: shards(): col_sums = jnp.sum(jnp.exp(scores - col_peak[:, None, :]), axis=1)]
  transfers between devices with their start and end apart: 57 -> 21, of which waited for: 8 -> 12; matrix products, arithmetic and copies ran while one was open for 1% -> 1% of each run, Pallas kernels for 0% -> 0%
where the time goes in v1:
time: 250 us; the launch traced here: 246 us
  starting transfers between devices  153 us (61%)
  Pallas kernels  51.5 us (21%)
  blocking collectives  19.8 us (8%)
  waiting for transfers between devices  12.2 us (5%)
  local copies, waits for them, and re-layouts  5.28 us (2%)
    ppermute x20, starting transfers between devices, from_row(): return lax.ppermute(block, 'row', [(source_of(i), i) for i in range(count)])  150 us
    pallas_call x3, Pallas kernels, step(): pl.pallas_call(functools.partial(step_kernel, first), out_shape=(jax.Shap...  47.6 us
    all_to_all x1, blocking collectives, gathered(): lax.all_to_all(copies, 'grp', 0, 0, tiled=True).reshape(-1, shard.shape[1])  19.8 us
    ppermute x20, waiting for transfers between devices, from_row(): return lax.ppermute(block, 'row', [(source_of(i), i) for i in range(count)])  9.53 us
  transfers between devices with their start and end apart: 21, of which 12 were waited for; matrix products, arithmetic and copies ran while one was open for 1% of the time, Pallas kernels for 0%

profile of v1, /device:TPU:1, one launch (start us, length us, event | category | flops | bytes accessed | tf_op | source)
XLA Modules:
  0.0 245.6 jit_solution(10191250889326519262)
XLA Ops:
  1.5 19.8 %all_to_all.10 = bf16[8,128,256]{2,1,0:T(8,128)(2,1)S(1)} all-to-all(bf16[8,128,256]{2,1,0:T(8,128)(2,1)S(1)} %broadcast_in_dim.29), channel_id=1, replica_groups=mesh['row'=96,'grp'=8] {'grp'}, dimensions={0} | all-to-all | bytes 1048576 | tf_op jit(solution)/shard_map/all_to_all | solution.py:53
  21.3 7.8 %collective-permute-start.2 = (bf16[1024,256]{1,0:T(8,128)(2,1)S(1)}, bf16[1024,256]{1,0:T(8,128)(2,1)S(1)}, u32[]{:S(2)}, u32[]{:S(2)}) collective-permute-start(bf16[1024,256]{1,0:T(8,128)(2,1)S(1)} %bitcast.6), channel_id=1, source_target_pairs={{752,0},{760,8},{0,16},{8,24},{16,32},{24,40},{32,48},{40,56},{48,... | collective-permute-start | bytes 1572872 | tf_op jit(solution)/shard_map/ppermute | solution.py:23
  29.1 14.4 %collective-permute-start.1 = (bf16[1024,256]{1,0:T(8,128)(2,1)S(1)}, bf16[1024,256]{1,0:T(8,128)(2,1)S(1)}, u32[]{:S(2)}, u32[]{:S(2)}) collective-permute-start(bf16[1024,256]{1,0:T(8,128)(2,1)S(1)} %bitcast.7), channel_id=1, source_target_pairs={{16,0},{24,8},{32,16},{40,24},{48,32},{56,40},{64,48},{72,56},{80,... | collective-permute-start | bytes 1572872 | tf_op jit(solution)/shard_map/ppermute | solution.py:23
  44.4 3.5 %all-to-all-start = ((bf16[8,128,256]{2,1,0:T(8,128)(2,1)}), bf16[8,128,256]{2,1,0:T(8,128)(2,1)S(1)}, u32[]{:S(2)}, u32[]{:S(2)}) async-start(bf16[8,128,256]{2,1,0:T(8,128)(2,1)} %broadcast_in_dim.28), calls=%async_computation | async-start | bytes 1048576 | tf_op jit(solution)/shard_map/all_to_all | solution.py:53
  47.9 4.6 %collective-permute-start = (bf16[1024,256]{1,0:T(8,128)(2,1)S(1)}, bf16[1024,256]{1,0:T(8,128)(2,1)S(1)}, u32[]{:S(2)}, u32[]{:S(2)}) collective-permute-start(bf16[1024,256]{1,0:T(8,128)(2,1)S(1)} %bitcast.8), channel_id=1, source_target_pairs={{8,0},{0,8},{24,16},{16,24},{40,32},{32,40},{56,48},{48,56},{72,64... | collective-permute-start | bytes 1572872 | tf_op jit(solution)/shard_map/ppermute | solution.py:23
  53.5 5.0 %collective-permute-start.3 = (bf16[1024,256]{1,0:T(8,128)(2,1)}, bf16[1024,256]{1,0:T(8,128)(2,1)S(1)}, u32[]{:S(2)}, u32[]{:S(2)}) collective-permute-start(bf16[1024,256]{1,0:T(8,128)(2,1)} %broadcast_select_fusion), channel_id=1, source_target_pairs={{8,0},{0,8},{24,16},{16,24},{40,32},{32,40},{56,48},{48,56},{72,64... | collective-permute-start | bytes 1572872 | tf_op jit(solution)/shard_map/ppermute | solution.py:23
  59.8 2.7 %all-to-all-done = bf16[8,128,256]{2,1,0:T(8,128)(2,1)S(1)} async-done(((bf16[8,128,256]{2,1,0:T(8,128)(2,1)}), bf16[8,128,256]{2,1,0:T(8,128)(2,1)S(1)}, u32[]{:S(2)}, u32[]{:S(2)}) %all-to-all-start) | async-done | bytes 524320 | tf_op jit(solution)/shard_map/all_to_all | solution.py:53
  62.5 20.6 %sinkhorn_step.3 = (f32[8,1024]{1,0:T(8,128)S(1)}, f32[1024,128]{1,0:T(8,128)}) custom-call(s32[5]{0:T(128)S(1)} %broadcast_select_fusion.4.listed, f32[5,1024]{1,0:T(8,128)S(1)} %broadcast_in_dim.27.pot, bf16[1024,256]{1,0:T(8,128)(2,1)S(1)} %bitcast.13, bf16[1024,256]{1,0:T(8,128)(2,1)S(1)} %bitcast.9, bf16[1024,256]{1,0:T(8,128)(2,1)S(1)} %collective-permute-done.t1, ...), custom_call_target="tpu_custom_call" | custom-call | flops 2684354560 | bytes 3145728 | tf_op jit(solution)/shard_map/sinkhorn_step/pallas_call | solution.py:174
  83.2 5.7 %collective-permute-start.4 = (f32[6,1024]{1,0:T(8,128)S(1)}, f32[6,1024]{1,0:T(8,128)S(1)}, u32[]{:S(2)}, u32[]{:S(2)}) collective-permute-start(f32[6,1024]{1,0:T(8,128)S(1)} %broadcast_select_fusion.3), channel_id=1, source_target_pairs={{8,0},{0,8},{24,16},{16,24},{40,32},{32,40},{56,48},{48,56},{72,64... | collective-permute-start | bytes 73736 | tf_op jit(solution)/shard_map/ppermute | solution.py:23
  89.8 8.6 %collective-permute-start.5 = (f32[4,1024]{1,0:T(4,128)S(1)}, f32[4,1024]{1,0:T(4,128)S(1)}, u32[]{:S(2)}, u32[]{:S(2)}) collective-permute-start(f32[4,1024]{1,0:T(4,128)S(1)} %slice_select_fusion.2), channel_id=1, source_target_pairs={{752,0},{24,8},{0,16},{40,24},{16,32},{56,40},{32,48},{72,56},{48,... | collective-permute-start | bytes 49160 | tf_op jit(solution)/shard_map/ppermute | solution.py:23
  98.4 14.1 %collective-permute-start.6 = (f32[2,1024]{1,0:T(2,128)S(1)}, f32[2,1024]{1,0:T(2,128)S(1)}, u32[]{:S(2)}, u32[]{:S(2)}) collective-permute-start(f32[2,1024]{1,0:T(2,128)S(1)} %slice_select_fusion.5), channel_id=1, source_target_pairs={{736,0},{40,8},{752,16},{56,24},{0,32},{72,40},{16,48},{88,56},{32... | collective-permute-start | bytes 24584 | tf_op jit(solution)/shard_map/ppermute | solution.py:23
  113.5 2.9 %collective-permute-start.7 = (f32[6,1024]{1,0:T(8,128)S(1)}, f32[6,1024]{1,0:T(8,128)S(1)}, u32[]{:S(2)}, u32[]{:S(2)}) collective-permute-start(f32[6,1024]{1,0:T(8,128)S(1)} %fusion.1), channel_id=1, source_target_pairs={{8,0},{0,8},{24,16},{16,24},{40,32},{32,40},{56,48},{48,56},{72,64... | collective-permute-start | bytes 73736 | tf_op jit(solution)/shard_map/ppermute | solution.py:23
  117.4 13.9 %sinkhorn_step.4 = (f32[8,1024]{1,0:T(8,128)S(1)}, f32[1024,128]{1,0:T(8,128)}) custom-call(s32[5]{0:T(128)S(1)} %broadcast_select_fusion.4.listed, f32[5,1024]{1,0:T(8,128)S(1)} %fusion.6.pot, bf16[1024,256]{1,0:T(8,128)(2,1)S(1)} %bitcast.14, bf16[1024,256]{1,0:T(8,128)(2,1)S(1)} %bitcast.10, bf16[1024,256]{1,0:T(8,128)(2,1)S(1)} %collective-permute-done.t1, ...), custom_call_target="tpu_custom_call" | custom-call | flops 2684354560 | bytes 3145728 | tf_op jit(solution)/shard_map/sinkhorn_step/pallas_call | solution.py:174
  131.4 2.2 collective-permute-start.8
  134.6 12.2 %collective-permute-start.9 = (f32[4,1024]{1,0:T(4,128)S(1)}, f32[4,1024]{1,0:T(4,128)S(1)}, u32[]{:S(2)}, u32[]{:S(2)}) collective-permute-start(f32[4,1024]{1,0:T(4,128)S(1)} %slice_select_fusion.1), channel_id=1, source_target_pairs={{752,0},{24,8},{0,16},{40,24},{16,32},{56,40},{32,48},{72,56},{48,... | collective-permute-start | bytes 49160 | tf_op jit(solution)/shard_map/ppermute | solution.py:23
  146.8 20.8 %collective-permute-start.10 = (f32[2,1024]{1,0:T(2,128)S(1)}, f32[2,1024]{1,0:T(2,128)S(1)}, u32[]{:S(2)}, u32[]{:S(2)}) collective-permute-start(f32[2,1024]{1,0:T(2,128)S(1)} %slice_select_fusion.4), channel_id=1, source_target_pairs={{736,0},{40,8},{752,16},{56,24},{0,32},{72,40},{16,48},{88,56},{32... | collective-permute-start | bytes 24584 | tf_op jit(solution)/shard_map/ppermute | solution.py:23
  171.7 13.1 %sinkhorn_step.5 = (f32[8,1024]{1,0:T(8,128)S(1)}, f32[1024,128]{1,0:T(8,128)S(1)}) custom-call(s32[5]{0:T(128)S(1)} %broadcast_select_fusion.4.listed, f32[5,1024]{1,0:T(8,128)S(1)} %fusion.7.pot, bf16[1024,256]{1,0:T(8,128)(2,1)S(1)} %bitcast.15, bf16[1024,256]{1,0:T(8,128)(2,1)S(1)} %bitcast.11, bf16[1024,256]{1,0:T(8,128)(2,1)S(1)} %collective-permute-done.t1, ...), custom_call_target="tpu_custom_call" | custom-call | flops 2684354560 | bytes 3145728 | tf_op jit(solution)/shard_map/sinkhorn_step/pallas_call | solution.py:174
  188.9 10.2 %collective-permute-start.13 = (f32[4,1024]{1,0:T(4,128)S(1)}, f32[4,1024]{1,0:T(4,128)S(1)}, u32[]{:S(2)}, u32[]{:S(2)}) collective-permute-start(f32[4,1024]{1,0:T(4,128)S(1)} %slice_select_fusion), channel_id=1, source_target_pairs={{752,0},{24,8},{0,16},{40,24},{16,32},{56,40},{32,48},{72,56},{48,... | collective-permute-start | bytes 49160 | tf_op jit(solution)/shard_map/ppermute | solution.py:23
  199.2 20.4 %collective-permute-start.14 = (f32[2,1024]{1,0:T(2,128)S(1)}, f32[2,1024]{1,0:T(2,128)S(1)}, u32[]{:S(2)}, u32[]{:S(2)}) collective-permute-start(f32[2,1024]{1,0:T(2,128)S(1)} %slice_select_fusion.3), channel_id=1, source_target_pairs={{736,0},{40,8},{752,16},{56,24},{0,32},{72,40},{16,48},{88,56},{32... | collective-permute-start | bytes 24584 | tf_op jit(solution)/shard_map/ppermute | solution.py:23
  220.5 3.2 %collective-permute-start.15 = (f32[6,1024]{1,0:T(8,128)S(1)}, f32[6,1024]{1,0:T(8,128)S(1)}, u32[]{:S(2)}, u32[]{:S(2)}) collective-permute-start(f32[6,1024]{1,0:T(8,128)S(1)} %fusion.5), channel_id=1, source_target_pairs={{8,0},{0,8},{24,16},{16,24},{40,32},{32,40},{56,48},{48,56},{72,64... | collective-permute-start | bytes 73736 | tf_op jit(solution)/shard_map/ppermute | solution.py:23
  225.7 3.9 %plan_gradients.1 = (f32[128,256]{1,0:T(8,128)}, f32[128,256]{1,0:T(8,128)S(1)}, f32[128,256]{1,0:T(8,128)S(1)}, f32[128,256]{1,0:T(8,128)S(1)}, f32[128,256]{1,0:T(8,128)S(1)}, /*index=5*/f32[128,256]{1,0:T(8,128)S(1)}) custom-call(s32[6]{0:T(128)S(1)} %pad_add_fusion.scal, f32[5,1024]{1,0:T(8,128)S(1)} %fusion.8.pot, f32[1024,128]{1,0:T(8,128)S(1)} %copy-done.3, ...), custom_call_target="tpu_custom_call" | custom-call | flops 1342177280 | bytes 4194304 | tf_op jit(solution)/shard_map/plan_gradients/pallas_call | solution.py:232
  229.6 2.2 collective-permute-start.16
  231.8 2.5 %collective-permute-start.17 = (f32[128,256]{1,0:T(8,128)S(1)}, f32[128,256]{1,0:T(8,128)S(1)}, u32[]{:S(2)}, u32[]{:S(2)}) collective-permute-start(f32[128,256]{1,0:T(8,128)S(1)} %get-tuple-element.19), channel_id=1, source_target_pairs={{760,0},{16,8},{8,16},{32,24},{24,32},{48,40},{40,48},{64,56},{56,... | collective-permute-start | bytes 393224 | tf_op jit(solution)/shard_map/ppermute | solution.py:23
  236.2 6.7 %collective-permute-start.19 = (f32[128,256]{1,0:T(8,128)S(1)}, f32[128,256]{1,0:T(8,128)S(1)}, u32[]{:S(2)}, u32[]{:S(2)}) collective-permute-start(f32[128,256]{1,0:T(8,128)S(1)} %get-tuple-element.21), channel_id=1, source_target_pairs={{16,0},{24,8},{32,16},{40,24},{48,32},{56,40},{64,48},{72,56},{80,... | collective-permute-start | bytes 393224 | tf_op jit(solution)/shard_map/ppermute | solution.py:23
  (90 shorter events, 23.3 us)
Async XLA Ops:
  0.6 57.8 %copy-start = (s32[1,5]{1,0:T(1,128)S(1)}, s32[1,5]{1,0:T(1,128)}, u32[]{:S(2)}) copy-start(s32[1,5]{1,0:T(1,128)} %param.7) | copy-start | bytes 64
  1.5 42.0 %copy-start.1 = (bf16[128,256]{1,0:T(8,128)(2,1)S(1)}, bf16[128,256]{1,0:T(8,128)(2,1)}, u32[]{:S(2)}) copy-start(bf16[128,256]{1,0:T(8,128)(2,1)} %mine.1) | copy-start | bytes 196612
  21.3 31.2 %collective-permute-start.2 = (bf16[1024,256]{1,0:T(8,128)(2,1)S(1)}, bf16[1024,256]{1,0:T(8,128)(2,1)S(1)}, u32[]{:S(2)}, u32[]{:S(2)}) collective-permute-start(bf16[1024,256]{1,0:T(8,128)(2,1)S(1)} %bitcast.6), channel_id=1, source_target_pairs={{752,0},{760,8},{0,16},{8,24},{16,32},{24,40},{32,48},{40,56},{48,... | collective-permute-start | bytes 1572872 | tf_op jit(solution)/shard_map/ppermute | solution.py:23
  29.1 23.5 %collective-permute-start.1 = (bf16[1024,256]{1,0:T(8,128)(2,1)S(1)}, bf16[1024,256]{1,0:T(8,128)(2,1)S(1)}, u32[]{:S(2)}, u32[]{:S(2)}) collective-permute-start(bf16[1024,256]{1,0:T(8,128)(2,1)S(1)} %bitcast.7), channel_id=1, source_target_pairs={{16,0},{24,8},{32,16},{40,24},{48,32},{56,40},{64,48},{72,56},{80,... | collective-permute-start | bytes 1572872 | tf_op jit(solution)/shard_map/ppermute | solution.py:23
  44.4 18.1 %all-to-all-start = ((bf16[8,128,256]{2,1,0:T(8,128)(2,1)}), bf16[8,128,256]{2,1,0:T(8,128)(2,1)S(1)}, u32[]{:S(2)}, u32[]{:S(2)}) async-start(bf16[8,128,256]{2,1,0:T(8,128)(2,1)} %broadcast_in_dim.28), calls=%async_computation | async-start | bytes 1048576 | tf_op jit(solution)/shard_map/all_to_all | solution.py:53
  47.9 10.5 %copy-start.5 = (s32[5]{0:T(128)S(1)}, s32[5]{0:T(128)}, u32[]{:S(2)}) copy-start(s32[5]{0:T(128)} %constant.55) | copy-start | bytes 64
  47.9 14.6 %collective-permute-start = (bf16[1024,256]{1,0:T(8,128)(2,1)S(1)}, bf16[1024,256]{1,0:T(8,128)(2,1)S(1)}, u32[]{:S(2)}, u32[]{:S(2)}) collective-permute-start(bf16[1024,256]{1,0:T(8,128)(2,1)S(1)} %bitcast.8), channel_id=1, source_target_pairs={{8,0},{0,8},{24,16},{16,24},{40,32},{32,40},{56,48},{48,56},{72,64... | collective-permute-start | bytes 1572872 | tf_op jit(solution)/shard_map/ppermute | solution.py:23
  53.5 9.0 %collective-permute-start.3 = (bf16[1024,256]{1,0:T(8,128)(2,1)}, bf16[1024,256]{1,0:T(8,128)(2,1)S(1)}, u32[]{:S(2)}, u32[]{:S(2)}) collective-permute-start(bf16[1024,256]{1,0:T(8,128)(2,1)} %broadcast_select_fusion), channel_id=1, source_target_pairs={{8,0},{0,8},{24,16},{16,24},{40,32},{32,40},{56,48},{48,56},{72,64... | collective-permute-start | bytes 1572872 | tf_op jit(solution)/shard_map/ppermute | solution.py:23
  83.2 6.5 %collective-permute-start.4 = (f32[6,1024]{1,0:T(8,128)S(1)}, f32[6,1024]{1,0:T(8,128)S(1)}, u32[]{:S(2)}, u32[]{:S(2)}) collective-permute-start(f32[6,1024]{1,0:T(8,128)S(1)} %broadcast_select_fusion.3), channel_id=1, source_target_pairs={{8,0},{0,8},{24,16},{16,24},{40,32},{32,40},{56,48},{48,56},{72,64... | collective-permute-start | bytes 73736 | tf_op jit(solution)/shard_map/ppermute | solution.py:23
  89.8 23.5 %collective-permute-start.5 = (f32[4,1024]{1,0:T(4,128)S(1)}, f32[4,1024]{1,0:T(4,128)S(1)}, u32[]{:S(2)}, u32[]{:S(2)}) collective-permute-start(f32[4,1024]{1,0:T(4,128)S(1)} %slice_select_fusion.2), channel_id=1, source_target_pairs={{752,0},{24,8},{0,16},{40,24},{16,32},{56,40},{32,48},{72,56},{48,... | collective-permute-start | bytes 49160 | tf_op jit(solution)/shard_map/ppermute | solution.py:23
  98.4 14.9 %collective-permute-start.6 = (f32[2,1024]{1,0:T(2,128)S(1)}, f32[2,1024]{1,0:T(2,128)S(1)}, u32[]{:S(2)}, u32[]{:S(2)}) collective-permute-start(f32[2,1024]{1,0:T(2,128)S(1)} %slice_select_fusion.5), channel_id=1, source_target_pairs={{736,0},{40,8},{752,16},{56,24},{0,32},{72,40},{16,48},{88,56},{32... | collective-permute-start | bytes 24584 | tf_op jit(solution)/shard_map/ppermute | solution.py:23
  113.5 3.8 %collective-permute-start.7 = (f32[6,1024]{1,0:T(8,128)S(1)}, f32[6,1024]{1,0:T(8,128)S(1)}, u32[]{:S(2)}, u32[]{:S(2)}) collective-permute-start(f32[6,1024]{1,0:T(8,128)S(1)} %fusion.1), channel_id=1, source_target_pairs={{8,0},{0,8},{24,16},{16,24},{40,32},{32,40},{56,48},{48,56},{72,64... | collective-permute-start | bytes 73736 | tf_op jit(solution)/shard_map/ppermute | solution.py:23
  131.4 3.1 %collective-permute-start.8 = (f32[6,1024]{1,0:T(8,128)S(1)}, f32[6,1024]{1,0:T(8,128)S(1)}, u32[]{:S(2)}, u32[]{:S(2)}) collective-permute-start(f32[6,1024]{1,0:T(8,128)S(1)} %broadcast_select_fusion.2), channel_id=1, source_target_pairs={{8,0},{0,8},{24,16},{16,24},{40,32},{32,40},{56,48},{48,56},{72,64... | collective-permute-start | bytes 73736 | tf_op jit(solution)/shard_map/ppermute | solution.py:23
  134.6 33.8 %collective-permute-start.9 = (f32[4,1024]{1,0:T(4,128)S(1)}, f32[4,1024]{1,0:T(4,128)S(1)}, u32[]{:S(2)}, u32[]{:S(2)}) collective-permute-start(f32[4,1024]{1,0:T(4,128)S(1)} %slice_select_fusion.1), channel_id=1, source_target_pairs={{752,0},{24,8},{0,16},{40,24},{16,32},{56,40},{32,48},{72,56},{48,... | collective-permute-start | bytes 49160 | tf_op jit(solution)/shard_map/ppermute | solution.py:23
  146.8 21.6 %collective-permute-start.10 = (f32[2,1024]{1,0:T(2,128)S(1)}, f32[2,1024]{1,0:T(2,128)S(1)}, u32[]{:S(2)}, u32[]{:S(2)}) collective-permute-start(f32[2,1024]{1,0:T(2,128)S(1)} %slice_select_fusion.4), channel_id=1, source_target_pairs={{736,0},{40,8},{752,16},{56,24},{0,32},{72,40},{16,48},{88,56},{32... | collective-permute-start | bytes 24584 | tf_op jit(solution)/shard_map/ppermute | solution.py:23
  168.5 3.1 %collective-permute-start.11 = (f32[6,1024]{1,0:T(8,128)S(1)}, f32[6,1024]{1,0:T(8,128)S(1)}, u32[]{:S(2)}, u32[]{:S(2)}) collective-permute-start(f32[6,1024]{1,0:T(8,128)S(1)} %fusion.3), channel_id=1, source_target_pairs={{8,0},{0,8},{24,16},{16,24},{40,32},{32,40},{56,48},{48,56},{72,64... | collective-permute-start | bytes 73736 | tf_op jit(solution)/shard_map/ppermute | solution.py:23
  185.8 3.1 %collective-permute-start.12 = (f32[6,1024]{1,0:T(8,128)S(1)}, f32[6,1024]{1,0:T(8,128)S(1)}, u32[]{:S(2)}, u32[]{:S(2)}) collective-permute-start(f32[6,1024]{1,0:T(8,128)S(1)} %broadcast_select_fusion.1), channel_id=1, source_target_pairs={{8,0},{0,8},{24,16},{16,24},{40,32},{32,40},{56,48},{48,56},{72,64... | collective-permute-start | bytes 73736 | tf_op jit(solution)/shard_map/ppermute | solution.py:23
  188.9 31.5 %collective-permute-start.13 = (f32[4,1024]{1,0:T(4,128)S(1)}, f32[4,1024]{1,0:T(4,128)S(1)}, u32[]{:S(2)}, u32[]{:S(2)}) collective-permute-start(f32[4,1024]{1,0:T(4,128)S(1)} %slice_select_fusion), channel_id=1, source_target_pairs={{752,0},{24,8},{0,16},{40,24},{16,32},{56,40},{32,48},{72,56},{48,... | collective-permute-start | bytes 49160 | tf_op jit(solution)/shard_map/ppermute | solution.py:23
  199.2 21.2 %collective-permute-start.14 = (f32[2,1024]{1,0:T(2,128)S(1)}, f32[2,1024]{1,0:T(2,128)S(1)}, u32[]{:S(2)}, u32[]{:S(2)}) collective-permute-start(f32[2,1024]{1,0:T(2,128)S(1)} %slice_select_fusion.3), channel_id=1, source_target_pairs={{736,0},{40,8},{752,16},{56,24},{0,32},{72,40},{16,48},{88,56},{32... | collective-permute-start | bytes 24584 | tf_op jit(solution)/shard_map/ppermute | solution.py:23
  220.5 4.0 %collective-permute-start.15 = (f32[6,1024]{1,0:T(8,128)S(1)}, f32[6,1024]{1,0:T(8,128)S(1)}, u32[]{:S(2)}, u32[]{:S(2)}) collective-permute-start(f32[6,1024]{1,0:T(8,128)S(1)} %fusion.5), channel_id=1, source_target_pairs={{8,0},{0,8},{24,16},{16,24},{40,32},{32,40},{56,48},{48,56},{72,64... | collective-permute-start | bytes 73736 | tf_op jit(solution)/shard_map/ppermute | solution.py:23
  229.6 13.4 %collective-permute-start.16 = (f32[128,256]{1,0:T(8,128)S(1)}, f32[128,256]{1,0:T(8,128)S(1)}, u32[]{:S(2)}, u32[]{:S(2)}) collective-permute-start(f32[128,256]{1,0:T(8,128)S(1)} %get-tuple-element.18), channel_id=1, source_target_pairs={{8,0},{0,8},{24,16},{16,24},{40,32},{32,40},{56,48},{48,56},{72,64... | collective-permute-start | bytes 393224 | tf_op jit(solution)/shard_map/ppermute | solution.py:23
  231.8 11.1 %collective-permute-start.17 = (f32[128,256]{1,0:T(8,128)S(1)}, f32[128,256]{1,0:T(8,128)S(1)}, u32[]{:S(2)}, u32[]{:S(2)}) collective-permute-start(f32[128,256]{1,0:T(8,128)S(1)} %get-tuple-element.19), channel_id=1, source_target_pairs={{760,0},{16,8},{8,16},{32,24},{24,32},{48,40},{40,48},{64,56},{56,... | collective-permute-start | bytes 393224 | tf_op jit(solution)/shard_map/ppermute | solution.py:23
  234.3 9.0 %collective-permute-start.18 = (f32[128,256]{1,0:T(8,128)S(1)}, f32[128,256]{1,0:T(8,128)S(1)}, u32[]{:S(2)}, u32[]{:S(2)}) collective-permute-start(f32[128,256]{1,0:T(8,128)S(1)} %get-tuple-element.20), channel_id=1, source_target_pairs={{752,0},{760,8},{0,16},{8,24},{16,32},{24,40},{32,48},{40,56},{48,... | collective-permute-start | bytes 393224 | tf_op jit(solution)/shard_map/ppermute | solution.py:23
  236.2 8.6 %collective-permute-start.19 = (f32[128,256]{1,0:T(8,128)S(1)}, f32[128,256]{1,0:T(8,128)S(1)}, u32[]{:S(2)}, u32[]{:S(2)}) collective-permute-start(f32[128,256]{1,0:T(8,128)S(1)} %get-tuple-element.21), channel_id=1, source_target_pairs={{16,0},{24,8},{32,16},{40,24},{48,32},{56,40},{64,48},{72,56},{80,... | collective-permute-start | bytes 393224 | tf_op jit(solution)/shard_map/ppermute | solution.py:23
  (3 other events, 2.5 us)

commit v2 on v1

--- a/solution.py
+++ b/solution.py
@@ -14,6 +14,9 @@
 KAPPA = 1.0 / (EPS * math.log(2.0))
 TWO_KAPPA = 2.0 * KAPPA
 SAFE_SUM = 2.0 ** -60
+SAFE_ROW = 2.0 ** -28
+SAFE_SHIFT = 60.0
+SCOPED = 16 * 1024 * 1024
 LANES = 128
 WINDOW = 5
 
@@ -87,110 +90,254 @@
     return lax.dot_general(a, b, (((1,), (1,)), ((), ())), preferred_element_type=jnp.float32)
 
 
-def step_kernel(first, listed, pot, rows, t0, t1, t2, t3, t4, sums_out, dual_out, bias, scores, peak, col):
+def exact_columns(rows, target, dual):
+    count = rows.shape[0]
+
+    def value(r):
+        here = pl.ds(pl.multiple_of(r * LANES, LANES), LANES)
+        return dot_nt(rows[here, :], target[...]) * TWO_KAPPA + dual[here, 0:1]
+
+    def find(r, best):
+        return jnp.maximum(best, jnp.max(value(r), axis=0, keepdims=True))
+
+    best = lax.fori_loop(0, count // LANES, find, jnp.full((1, count), NEG, jnp.float32))
+
+    def add(r, acc):
+        return acc + jnp.sum(jnp.exp2(value(r) - best), axis=0, keepdims=True)
+
+    acc = lax.fori_loop(0, count // LANES, add, jnp.zeros((1, count), jnp.float32))
+    return best + jnp.log2(acc)
+
+
+def put_columns(listed, base, col, sums_out, fine):
+    count = sums_out.shape[1]
+    sums_out[...] = jnp.full(sums_out.shape, NEG, jnp.float32)
+    for p in range(WINDOW):
+        sums = jnp.sum(col[:, p * count : (p + 1) * count], axis=0, keepdims=True)
+        taken = listed[p] == 1
+        sums_out[p : p + 1, :] = jnp.where(taken, jnp.log2(sums) - base[p : p + 1, :], NEG)
+        good = jnp.where(jnp.logical_or(jnp.logical_not(taken), sums >= SAFE_SUM), 1.0, 0.0)
+        for q in range(count // LANES):
+            fine = jnp.minimum(fine, good[:, q * LANES : (q + 1) * LANES])
+    return jnp.min(fine) > 0.5
+
+
+def put_exact_columns(listed, fetch, dual, sums_out):
+    for p in range(WINDOW):
+
+        @pl.when(listed[p] == 1)
+        def _(p=p):
+            sums_out[p : p + 1, :] = exact_columns(*fetch(p), dual)
+
+
+def add_columns(entries, here, scale, col, width):
+    for q in range(width):
+        e = entries[here, q * LANES : (q + 1) * LANES] * scale
+        col[:, q * LANES : (q + 1) * LANES] += jnp.sum(e.reshape(LANES // 8, 8, LANES), axis=0)
+
+
+def first_kernel(listed, rows, t0, t1, t2, t3, t4, entries, sums_out, top_out, base, dual, peak, col):
     targets = (t0, t1, t2, t3, t4)
     count = rows.shape[0]
-    tile = min(256, count)
-    for p in range(WINDOW):
-        if first:
-            sq = jnp.square(targets[p][...].astype(jnp.float32))
-            high = sq.astype(jnp.bfloat16)
-            low = (sq - high.astype(jnp.float32)).astype(jnp.bfloat16)
-            ones = jnp.ones((8, sq.shape[1]), jnp.bfloat16)
-            row = -KAPPA * (dot_nt(ones, high) + dot_nt(ones, low))[0:1]
-        else:
-            row = pot[p : p + 1, :]
-        bias[p : p + 1, :] = jnp.where(listed[p] == 1, row, NEG)
-
+    base[...] = jnp.zeros(base.shape, jnp.float32)
     peak[...] = jnp.full(peak.shape, NEG, jnp.float32)
     for p in range(WINDOW):
-
-        def fill(c, carry, p=p):
-            at = pl.multiple_of(c * tile, tile)
-            inner = dot_nt(rows[...], targets[p][pl.ds(at, tile), :])
-            block = inner * TWO_KAPPA + bias[p : p + 1, pl.ds(at, tile)]
-            scores[:, pl.ds(pl.multiple_of(p * count + at, tile), tile)] = block
-            best = peak[...]
-            for q in range(tile // LANES):
-                best = jnp.maximum(best, block[:, q * LANES : (q + 1) * LANES])
-            peak[...] = best
-            return carry
-
-        lax.fori_loop(0, count // tile, fill, 0)
+        sq = jnp.square(targets[p][...].astype(jnp.float32))
+        sq = sum(sq[:, q * LANES : (q + 1) * LANES] for q in range(sq.shape[1] // LANES))
+        bias = jnp.concatenate(
+            [
+                jnp.sum(sq[r * LANES : (r + 1) * LANES, :].T, axis=0, keepdims=True)
+                for r in range(count // LANES)
+            ],
+            axis=1,
+        )
+        bias = -KAPPA * bias
+        bias = jnp.where(listed[p] == 1, bias, NEG)
+        base[p : p + 1, :] = bias
+
+        block = dot_nt(rows[...], targets[p][...]) * TWO_KAPPA + bias
+        entries[:, p * count : (p + 1) * count] = block
+        best = peak[...]
+        for q in range(count // LANES):
+            best = jnp.maximum(best, block[:, q * LANES : (q + 1) * LANES])
+        peak[...] = best
 
     col[...] = jnp.zeros(col.shape, jnp.float32)
     width = WINDOW * count // LANES
 
-    def chunk(r, carry):
-        here = pl.ds(pl.multiple_of(r * LANES, LANES), LANES)
-        top = jnp.max(peak[here, :], axis=1, keepdims=True)
+    def rows_of(r):
+        return pl.ds(pl.multiple_of(r * LANES, LANES), LANES)
+
+    def exponentials(r, meanwhile):
+        here = rows_of(r)
+        top = jnp.broadcast_to(jnp.max(peak[here, :], axis=1, keepdims=True), (LANES, LANES))
         acc = jnp.zeros((LANES, LANES), jnp.float32)
         for q in range(width):
-            e = jnp.exp2(scores[here, q * LANES : (q + 1) * LANES] - top)
-            scores[here, q * LANES : (q + 1) * LANES] = e
+            e = jnp.exp2(entries[here, q * LANES : (q + 1) * LANES] - top)
+            entries[here, q * LANES : (q + 1) * LANES] = e
             acc = acc + e
-        total = jnp.sum(acc, axis=1, keepdims=True)
-        dual_out[here, :] = jnp.broadcast_to(-(top + jnp.log2(total)), (LANES, LANES))
-        scale = jnp.broadcast_to(1.0 / total, (LANES, LANES))
+        total = jnp.broadcast_to(jnp.sum(acc, axis=1, keepdims=True), (LANES, LANES))
+        meanwhile()
+        top_out[here, :] = top
+        dual[here, :] = -(top + jnp.log2(total))
+        peak[here, :] = 1.0 / total
+
+    def columns(r):
+        add_columns(entries, rows_of(r), peak[rows_of(r), :], col, width)
+
+    def both(r, carry):
+        exponentials(r, lambda: columns(r - 1))
+        return carry
+
+    exponentials(0, lambda: None)
+    lax.fori_loop(1, count // LANES, both, 0)
+    columns(count // LANES - 1)
+    fine = put_columns(listed, base, col, sums_out, jnp.ones((1, LANES), jnp.float32))
+
+    @pl.when(jnp.logical_not(fine))
+    def _():
+        put_exact_columns(listed, lambda p: (rows, targets[p]), dual, sums_out)
+
+
+def later_kernel(
+    listed, entries, pot, base, top, rows_far, t0, t1, t2, t3, t4, sums_out, dual_out, gain, col, low, total, rows, target
+):
+    targets = (t0, t1, t2, t3, t4)
+    count = rows.shape[0]
+
+    def fetch(p):
+        pltpu.sync_copy(rows_far, rows)
+        pltpu.sync_copy(targets[p], target)
+        return rows, target
+
+    col[...] = jnp.zeros(col.shape, jnp.float32)
+    width = WINDOW * count // LANES
+    worst = jnp.zeros((1, count), jnp.float32)
+    for p in range(WINDOW):
+        taken = listed[p] == 1
+        shift = jnp.where(taken, pot[p : p + 1, :] - base[p : p + 1, :], 0.0)
+        worst = jnp.maximum(worst, jnp.abs(shift))
+        gain[:, p * count : (p + 1) * count] = jnp.broadcast_to(
+            jnp.where(taken, jnp.exp2(shift), 0.0), (8, count)
+        )
+    low[...] = jnp.full(low.shape, 1.0, jnp.float32)
+
+    def rows_of(r):
+        return pl.ds(pl.multiple_of(r * LANES, LANES), LANES)
+
+    def weigh(r, meanwhile):
+        here = rows_of(r)
+        acc = jnp.zeros((LANES, LANES), jnp.float32)
         for q in range(width):
-            e = scores[here, q * LANES : (q + 1) * LANES] * scale
-            col[:, q * LANES : (q + 1) * LANES] += jnp.sum(e.reshape(LANES // 8, 8, LANES), axis=0)
+            at = slice(q * LANES, (q + 1) * LANES)
+            acc = acc + entries[here, at] * gain[0:1, at]
+        mass = jnp.broadcast_to(jnp.sum(acc, axis=1, keepdims=True), (LANES, LANES))
+        meanwhile()
+        low[...] = jnp.minimum(low[...], mass)
+        dual_out[here, :] = -(top[here, :] + jnp.log2(mass))
+        total[here, :] = 1.0 / mass
+
+    def columns(r):
+        add_columns(entries, rows_of(r), total[rows_of(r), :], col, width)
+
+    def both(r, carry):
+        weigh(r, lambda: columns(r - 1))
         return carry
 
-    lax.fori_loop(0, count // LANES, chunk, 0)
-
-    sums_out[...] = jnp.full(sums_out.shape, NEG, jnp.float32)
-    for p in range(WINDOW):
-        total = jnp.sum(col[:, p * count : (p + 1) * count], axis=0, keepdims=True)
-        safe = jnp.min(total) >= SAFE_SUM
-        usable = listed[p] == 1
-
-        @pl.when(jnp.logical_and(usable, safe))
-        def _(p=p, total=total):
-            sums_out[p : p + 1, :] = jnp.log2(total) - bias[p : p + 1, :]
-
-        @pl.when(jnp.logical_and(usable, jnp.logical_not(safe)))
-        def _(p=p):
-            def value(r):
+    weigh(0, lambda: None)
+    lax.fori_loop(1, count // LANES, both, 0)
+    columns(count // LANES - 1)
+    fine = jnp.where(jnp.min(low[...], axis=0, keepdims=True) >= SAFE_ROW, 1.0, 0.0)
+    for q in range(count // LANES):
+        fine = jnp.minimum(fine, jnp.where(worst[:, q * LANES : (q + 1) * LANES] <= SAFE_SHIFT, 1.0, 0.0))
+    fine = put_columns(listed, base, col, sums_out, fine)
+
+    @pl.when(jnp.logical_not(fine))
+    def _():
+        def value(p, here):
+            bias = jnp.where(listed[p] == 1, pot[p : p + 1, :], NEG)
+            return dot_nt(rows[here, :], target[...]) * TWO_KAPPA + bias
+
+        dual_out[...] = jnp.full(dual_out.shape, NEG, jnp.float32)
+        for p in range(WINDOW):
+            fetch(p)
+
+            def find(r, carry, p=p):
                 here = pl.ds(pl.multiple_of(r * LANES, LANES), LANES)
-                return dot_nt(rows[here, :], targets[p][...]) * TWO_KAPPA + dual_out[here, 0:1]
-
-            def find(r, best):
-                return jnp.maximum(best, jnp.max(value(r), axis=0, keepdims=True))
-
-            best = lax.fori_loop(0, count // LANES, find, jnp.full((1, count), NEG, jnp.float32))
-
-            def add(r, acc):
-                return acc + jnp.sum(jnp.exp2(value(r) - best), axis=0, keepdims=True)
-
-            acc = lax.fori_loop(0, count // LANES, add, jnp.zeros((1, count), jnp.float32))
-            sums_out[p : p + 1, :] = best + jnp.log2(acc)
-
-
-def step(first, listed, pot, rows, targets):
+                best = jnp.max(value(p, here), axis=1, keepdims=True)
+                dual_out[here, :] = jnp.maximum(dual_out[here, :], best)
+                return carry
+
+            lax.fori_loop(0, count // LANES, find, 0)
+        total[...] = jnp.zeros(total.shape, jnp.float32)
+        for p in range(WINDOW):
+            fetch(p)
+
+            def add(r, carry, p=p):
+                here = pl.ds(pl.multiple_of(r * LANES, LANES), LANES)
+                e = jnp.exp2(value(p, here) - dual_out[here, 0:1])
+                total[here, :] += jnp.sum(e, axis=1, keepdims=True)
+                return carry
+
+            lax.fori_loop(0, count // LANES, add, 0)
+        dual_out[...] = -(dual_out[...] + jnp.log2(total[...]))
+
+        put_exact_columns(listed, fetch, dual_out, sums_out)
+
+
+VMEM = pl.BlockSpec(memory_space=pltpu.VMEM)
+ANY = pl.BlockSpec(memory_space=pl.ANY)
+SMEM = pl.BlockSpec(memory_space=pltpu.SMEM)
+
+
+def first_step(listed, rows, targets):
     count, width = rows.shape
-    vmem = pl.BlockSpec(memory_space=pltpu.VMEM)
     pairs = WINDOW * count * count
+    row = jax.ShapeDtypeStruct((8, count), jnp.float32)
+    column = jax.ShapeDtypeStruct((count, LANES), jnp.float32)
     return pl.pallas_call(
-        functools.partial(step_kernel, first),
-        out_shape=(
-            jax.ShapeDtypeStruct((8, count), jnp.float32),
-            jax.ShapeDtypeStruct((count, LANES), jnp.float32),
-        ),
-        in_specs=[pl.BlockSpec(memory_space=pltpu.SMEM)] + [vmem] * 7,
-        out_specs=(vmem, vmem),
+        first_kernel,
+        out_shape=(pltpu.VMEM((count, WINDOW * count), jnp.float32), row, column, row),
+        in_specs=[SMEM] + [VMEM] * 6,
+        out_specs=(VMEM,) * 4,
         scratch_shapes=[
-            pltpu.VMEM((8, count), jnp.float32),
-            pltpu.VMEM((count, WINDOW * count), jnp.float32),
+            pltpu.VMEM((count, LANES), jnp.float32),
             pltpu.VMEM((count, LANES), jnp.float32),
             pltpu.VMEM((8, WINDOW * count), jnp.float32),
         ],
-        compiler_params=pltpu.CompilerParams(vmem_limit_bytes=44 * 1024 * 1024),
+        compiler_params=pltpu.CompilerParams(vmem_limit_bytes=SCOPED),
         cost_estimate=pl.CostEstimate(
             flops=2 * pairs * width, bytes_accessed=12 * count * width, transcendentals=pairs
         ),
-        name="sinkhorn_step",
-    )(listed, pot, rows, *targets)
+        name="first_step",
+    )(listed, rows, *targets)
+
+
+def later_step(listed, entries, pot, base, top, rows, targets):
+    count, width = rows.shape
+    pairs = WINDOW * count * count
+    row = jax.ShapeDtypeStruct((8, count), jnp.float32)
+    column = jax.ShapeDtypeStruct((count, LANES), jnp.float32)
+    entries = pltpu.with_memory_space_constraint(entries, pltpu.VMEM)
+    return pl.pallas_call(
+        later_kernel,
+        out_shape=(row, column),
+        in_specs=[SMEM] + [VMEM] * 4 + [ANY] * 6,
+        out_specs=(VMEM, VMEM),
+        scratch_shapes=[
+            pltpu.VMEM((8, WINDOW * count), jnp.float32),
+            pltpu.VMEM((8, WINDOW * count), jnp.float32),
+            pltpu.VMEM((LANES, LANES), jnp.float32),
+            pltpu.VMEM((count, LANES), jnp.float32),
+            pltpu.VMEM((count, width), jnp.bfloat16),
+            pltpu.VMEM((count, width), jnp.bfloat16),
+        ],
+        compiler_params=pltpu.CompilerParams(vmem_limit_bytes=SCOPED),
+        cost_estimate=pl.CostEstimate(
+            flops=4 * pairs, bytes_accessed=12 * count * width, transcendentals=0
+        ),
+        name="later_step",
+    )(listed, entries, pot, base, top, rows, *targets)
 
 
 def grad_kernel(scal, pot, dual, mine, rows, t0, t1, t2, t3, t4, source_out, o0, o1, o2, o3, o4):
@@ -226,15 +373,14 @@
 
 def gradients(scal, pot, dual, mine, rows, targets):
     count, width = rows.shape
-    vmem = pl.BlockSpec(memory_space=pltpu.VMEM)
     part = jax.ShapeDtypeStruct((LANES, width), jnp.float32)
     pairs = 2 * WINDOW * count * LANES
     return pl.pallas_call(
         grad_kernel,
         out_shape=(part,) * (1 + WINDOW),
-        in_specs=[pl.BlockSpec(memory_space=pltpu.SMEM)] + [vmem] * 9,
-        out_specs=(vmem,) * (1 + WINDOW),
-        compiler_params=pltpu.CompilerParams(vmem_limit_bytes=44 * 1024 * 1024),
+        in_specs=[SMEM] + [VMEM] * 9,
+        out_specs=(VMEM,) * (1 + WINDOW),
+        compiler_params=pltpu.CompilerParams(vmem_limit_bytes=SCOPED),
         cost_estimate=pl.CostEstimate(
             flops=4 * pairs * width, bytes_accessed=16 * count * width, transcendentals=pairs
         ),
@@ -253,10 +399,10 @@
     targets = (own, mate, cross, above, below)
     mask = pair_mask[0]
     listed = jnp.where(even, mask[jnp.array([2, 3, 1, 4, 0])], mask[jnp.array([2, 1, 3, 4, 0])])
-    pot = jnp.zeros((WINDOW, own.shape[0]), jnp.float32)
-    dual = None
-    for k in range(ITERS):
-        partial, dual = step(k == 0, listed, pot, rows, targets)
+    entries, partial, top, base = first_step(listed, rows, targets)
+    pot = -column_totals(partial, even)
+    for _ in range(ITERS - 1):
+        partial, dual = later_step(listed, entries, pot, base, top, rows, targets)
         pot = -column_totals(partial, even)
     scal = jnp.concatenate([listed, lax.axis_index("grp").astype(jnp.int32)[None]])
     source_grad, part_own, part_mate, part_cross, part_above, part_below = gradients(

time: 250 us -> 325 us (1.30)
  Pallas kernels: 51.5 us -> 120 us
  local copies, waits for them, and re-layouts: 5.28 us -> 29.9 us
  starting transfers between devices: 153 us -> 136 us
    pallas_call x4, Pallas kernels: 51.5 us -> 120 us  [the longest x2 97 us: later_step(): pl.pallas_call(later_kernel, out_shape=(row, column), in_specs=[SMEM] + [...]
    unnamed x12 -> x20, local copies, waits for them, and re-layouts: 1.86 us -> 25.6 us
    ppermute x20, starting transfers between devices: 150 us -> 133 us  [from_row(): return lax.ppermute(block, 'row', [(source_of(i), i) for i in range(count)])]
  transfers between devices with their start and end apart: 21 -> 21, of which waited for: 12 -> 12; matrix products, arithmetic and copies ran while one was open for 1% -> 2% of each run, Pallas kernels for 0% -> 0%
where the time goes in v2:
time: 325 us; the launch traced here: 322 us
  starting transfers between devices  136 us (42%)
  Pallas kernels  120 us (37%)
  local copies, waits for them, and re-layouts  29.9 us (9%)
  blocking collectives  19.7 us (6%)
  waiting for transfers between devices  11.4 us (4%)
  other arithmetic  3.67 us (1%)
    ppermute x20, starting transfers between devices, from_row(): return lax.ppermute(block, 'row', [(source_of(i), i) for i in range(count)])  133 us
    pallas_call x2, Pallas kernels, later_step(): pl.pallas_call(later_kernel, out_shape=(row, column), in_specs=[SMEM] + [...  97 us
    unnamed x20, local copies, waits for them, and re-layouts  25.6 us
    all_to_all x1, blocking collectives, gathered(): lax.all_to_all(copies, 'grp', 0, 0, tiled=True).reshape(-1, shard.shape[1])  19.7 us
    pallas_call x1, Pallas kernels, first_step(): pl.pallas_call(first_kernel, out_shape=(pltpu.VMEM((count, WINDOW * count...  19.5 us
    ppermute x20, waiting for transfers between devices, from_row(): return lax.ppermute(block, 'row', [(source_of(i), i) for i in range(count)])  9.19 us
  transfers between devices with their start and end apart: 21, of which 12 were waited for; matrix products, arithmetic and copies ran while one was open for 2% of the time, Pallas kernels for 0%

profile of v2, /device:TPU:1, one launch (start us, length us, event | category | flops | bytes accessed | tf_op | source)
XLA Modules:
  0.0 322.1 jit_solution(126647185820849916)
XLA Ops:
  1.5 19.7 %all_to_all.10 = bf16[8,128,256]{2,1,0:T(8,128)(2,1)S(1)} all-to-all(bf16[8,128,256]{2,1,0:T(8,128)(2,1)S(1)} %broadcast_in_dim.25), channel_id=1, replica_groups=mesh['row'=96,'grp'=8] {'grp'}, dimensions={0} | all-to-all | bytes 1048576 | tf_op jit(solution)/shard_map/all_to_all | solution.py:56
  21.2 7.8 %collective-permute-start.2 = (bf16[1024,256]{1,0:T(8,128)(2,1)S(1)}, bf16[1024,256]{1,0:T(8,128)(2,1)S(1)}, u32[]{:S(2)}, u32[]{:S(2)}) collective-permute-start(bf16[1024,256]{1,0:T(8,128)(2,1)S(1)} %bitcast.6), channel_id=1, source_target_pairs={{752,0},{760,8},{0,16},{8,24},{16,32},{24,40},{32,48},{40,56},{48,... | collective-permute-start | bytes 1572872 | tf_op jit(solution)/shard_map/ppermute | solution.py:26
  29.0 14.4 %collective-permute-start.1 = (bf16[1024,256]{1,0:T(8,128)(2,1)S(1)}, bf16[1024,256]{1,0:T(8,128)(2,1)S(1)}, u32[]{:S(2)}, u32[]{:S(2)}) collective-permute-start(bf16[1024,256]{1,0:T(8,128)(2,1)S(1)} %bitcast.7), channel_id=1, source_target_pairs={{16,0},{24,8},{32,16},{40,24},{48,32},{56,40},{64,48},{72,56},{80,... | collective-permute-start | bytes 1572872 | tf_op jit(solution)/shard_map/ppermute | solution.py:26
  45.1 3.5 %all-to-all-start = ((bf16[8,128,256]{2,1,0:T(8,128)(2,1)}), bf16[8,128,256]{2,1,0:T(8,128)(2,1)S(1)}, u32[]{:S(2)}, u32[]{:S(2)}) async-start(bf16[8,128,256]{2,1,0:T(8,128)(2,1)} %broadcast_in_dim.24), calls=%async_computation | async-start | bytes 1048576 | tf_op jit(solution)/shard_map/all_to_all | solution.py:56
  48.6 4.6 %collective-permute-start = (bf16[1024,256]{1,0:T(8,128)(2,1)S(1)}, bf16[1024,256]{1,0:T(8,128)(2,1)S(1)}, u32[]{:S(2)}, u32[]{:S(2)}) collective-permute-start(bf16[1024,256]{1,0:T(8,128)(2,1)S(1)} %bitcast.8), channel_id=1, source_target_pairs={{8,0},{0,8},{24,16},{16,24},{40,32},{32,40},{56,48},{48,56},{72,64... | collective-permute-start | bytes 1572872 | tf_op jit(solution)/shard_map/ppermute | solution.py:26
  54.1 4.1 %collective-permute-start.3 = (bf16[1024,256]{1,0:T(8,128)(2,1)}, bf16[1024,256]{1,0:T(8,128)(2,1)S(1)}, u32[]{:S(2)}, u32[]{:S(2)}) collective-permute-start(bf16[1024,256]{1,0:T(8,128)(2,1)} %broadcast_select_fusion), channel_id=1, source_target_pairs={{8,0},{0,8},{24,16},{16,24},{40,32},{32,40},{56,48},{48,56},{72,64... | collective-permute-start | bytes 1572872 | tf_op jit(solution)/shard_map/ppermute | solution.py:26
  63.2 19.5 %first_step.1 = (f32[1024,5120]{1,0:T(8,128)S(1)}, f32[8,1024]{1,0:T(8,128)S(1)}, f32[1024,128]{1,0:T(8,128)S(1)}, f32[8,1024]{1,0:T(8,128)S(1)}) custom-call(s32[5]{0:T(128)S(1)} %broadcast_select_fusion.4.listed, bf16[1024,256]{1,0:T(8,128)(2,1)S(1)} %bitcast.13, bf16[1024,256]{1,0:T(8,128)(2,1)S(1)} %bitcast.9, ...), custom_call_target="tpu_custom_call" | custom-call | flops 2684354560 | bytes 3145728 | tf_op jit(solution)/shard_map/first_step/pallas_call | solution.py:298
  82.6 7.0 %copy-done.1 = f32[1024,5120]{1,0:T(8,128)} copy-done((f32[1024,5120]{1,0:T(8,128)}, f32[1024,5120]{1,0:T(8,128)S(1)}, u32[]{:S(2)}) %copy-start.1) | copy-done | bytes 20971544
  90.5 16.1 %collective-permute-start.4 = (f32[6,1024]{1,0:T(8,128)S(1)}, f32[6,1024]{1,0:T(8,128)S(1)}, u32[]{:S(2)}, u32[]{:S(2)}) collective-permute-start(f32[6,1024]{1,0:T(8,128)S(1)} %broadcast_select_fusion.3), channel_id=1, source_target_pairs={{8,0},{0,8},{24,16},{16,24},{40,32},{32,40},{56,48},{48,56},{72,64... | collective-permute-start | bytes 73736 | tf_op jit(solution)/shard_map/ppermute | solution.py:26
  109.5 4.8 %collective-permute-start.6 = (f32[2,1024]{1,0:T(2,128)S(1)}, f32[2,1024]{1,0:T(2,128)S(1)}, u32[]{:S(2)}, u32[]{:S(2)}) collective-permute-start(f32[2,1024]{1,0:T(2,128)S(1)} %slice_select_fusion.5), channel_id=1, source_target_pairs={{736,0},{40,8},{752,16},{56,24},{0,32},{72,40},{16,48},{88,56},{32... | collective-permute-start | bytes 24584 | tf_op jit(solution)/shard_map/ppermute | solution.py:26
  115.2 6.4 %collective-permute-start.7 = (f32[6,1024]{1,0:T(8,128)S(1)}, f32[6,1024]{1,0:T(8,128)S(1)}, u32[]{:S(2)}, u32[]{:S(2)}) collective-permute-start(f32[6,1024]{1,0:T(8,128)S(1)} %fusion.1), channel_id=1, source_target_pairs={{8,0},{0,8},{24,16},{16,24},{40,32},{32,40},{56,48},{48,56},{72,64... | collective-permute-start | bytes 73736 | tf_op jit(solution)/shard_map/ppermute | solution.py:26
  122.6 7.0 %copy-done.2 = f32[1024,5120]{1,0:T(8,128)S(1)} copy-done((f32[1024,5120]{1,0:T(8,128)S(1)}, f32[1024,5120]{1,0:T(8,128)}, u32[]{:S(2)}) %copy-start.2) | copy-done | bytes 20971544
  130.6 49.1 %later_step.2 = (f32[8,1024]{1,0:T(8,128)S(1)}, f32[1024,128]{1,0:T(8,128)}) custom-call(s32[5]{0:T(128)S(1)} %broadcast_select_fusion.4.listed, f32[1024,5120]{1,0:T(8,128)S(1)} %copy-done.2, f32[5,1024]{1,0:T(8,128)S(1)} %fusion.6.pot, f32[8,1024]{1,0:T(8,128)S(1)} %get-tuple-element.17.base, f32[1024,128]{1,0:T(8,128)S(1)} %copy-done.5, ...), custom_call_target="tpu_custom_call" | custom-call | flops 20971520 | bytes 3145728 | tf_op jit(solution)/shard_map/later_step/pallas_call | solution.py:322
  179.8 12.8 %collective-permute-start.8 = (f32[6,1024]{1,0:T(8,128)S(1)}, f32[6,1024]{1,0:T(8,128)S(1)}, u32[]{:S(2)}, u32[]{:S(2)}) collective-permute-start(f32[6,1024]{1,0:T(8,128)S(1)} %broadcast_select_fusion.2), channel_id=1, source_target_pairs={{8,0},{0,8},{24,16},{16,24},{40,32},{32,40},{56,48},{48,56},{72,64... | collective-permute-start | bytes 73736 | tf_op jit(solution)/shard_map/ppermute | solution.py:26
  195.5 9.3 %collective-permute-start.10 = (f32[2,1024]{1,0:T(2,128)S(1)}, f32[2,1024]{1,0:T(2,128)S(1)}, u32[]{:S(2)}, u32[]{:S(2)}) collective-permute-start(f32[2,1024]{1,0:T(2,128)S(1)} %slice_select_fusion.4), channel_id=1, source_target_pairs={{736,0},{40,8},{752,16},{56,24},{0,32},{72,40},{16,48},{88,56},{32... | collective-permute-start | bytes 24584 | tf_op jit(solution)/shard_map/ppermute | solution.py:26
  205.7 3.2 collective-permute-start.11
  209.9 7.0 %copy-done.3 = f32[1024,5120]{1,0:T(8,128)S(1)} copy-done((f32[1024,5120]{1,0:T(8,128)S(1)}, f32[1024,5120]{1,0:T(8,128)}, u32[]{:S(2)}) %copy-start.3) | copy-done | bytes 20971544
  217.9 47.9 %later_step.3 = (f32[8,1024]{1,0:T(8,128)S(1)}, f32[1024,128]{1,0:T(8,128)S(1)}) custom-call(s32[5]{0:T(128)S(1)} %broadcast_select_fusion.4.listed, f32[1024,5120]{1,0:T(8,128)S(1)} %copy-done.3, f32[5,1024]{1,0:T(8,128)S(1)} %fusion.7.pot, f32[8,1024]{1,0:T(8,128)S(1)} %get-tuple-element.17.base, f32[1024,128]{1,0:T(8,128)S(1)} %copy-done.6, ...), custom_call_target="tpu_custom_call" | custom-call | flops 20971520 | bytes 3145728 | tf_op jit(solution)/shard_map/later_step/pallas_call | solution.py:322
  266.7 12.8 %collective-permute-start.12 = (f32[6,1024]{1,0:T(8,128)S(1)}, f32[6,1024]{1,0:T(8,128)S(1)}, u32[]{:S(2)}, u32[]{:S(2)}) collective-permute-start(f32[6,1024]{1,0:T(8,128)S(1)} %broadcast_select_fusion.1), channel_id=1, source_target_pairs={{8,0},{0,8},{24,16},{16,24},{40,32},{32,40},{56,48},{48,56},{72,64... | collective-permute-start | bytes 73736 | tf_op jit(solution)/shard_map/ppermute | solution.py:26
  282.3 12.2 %collective-permute-start.14 = (f32[2,1024]{1,0:T(2,128)S(1)}, f32[2,1024]{1,0:T(2,128)S(1)}, u32[]{:S(2)}, u32[]{:S(2)}) collective-permute-start(f32[2,1024]{1,0:T(2,128)S(1)} %slice_select_fusion.3), channel_id=1, source_target_pairs={{736,0},{40,8},{752,16},{56,24},{0,32},{72,40},{16,48},{88,56},{32... | collective-permute-start | bytes 24584 | tf_op jit(solution)/shard_map/ppermute | solution.py:26
  295.4 3.2 collective-permute-start.15
  300.6 3.9 %plan_gradients.1 = (f32[128,256]{1,0:T(8,128)}, f32[128,256]{1,0:T(8,128)S(1)}, f32[128,256]{1,0:T(8,128)S(1)}, f32[128,256]{1,0:T(8,128)S(1)}, f32[128,256]{1,0:T(8,128)S(1)}, /*index=5*/f32[128,256]{1,0:T(8,128)S(1)}) custom-call(s32[6]{0:T(128)S(1)} %pad_add_fusion.scal, f32[5,1024]{1,0:T(8,128)S(1)} %fusion.8.pot, f32[1024,128]{1,0:T(8,128)S(1)} %copy-done.9, ...), custom_call_target="tpu_custom_call" | custom-call | flops 1342177280 | bytes 4194304 | tf_op jit(solution)/shard_map/plan_gradients/pallas_call | solution.py:378
  306.7 4.1 %collective-permute-start.17 = (f32[128,256]{1,0:T(8,128)S(1)}, f32[128,256]{1,0:T(8,128)S(1)}, u32[]{:S(2)}, u32[]{:S(2)}) collective-permute-start(f32[128,256]{1,0:T(8,128)S(1)} %get-tuple-element.25), channel_id=1, source_target_pairs={{760,0},{16,8},{8,16},{32,24},{24,32},{48,40},{40,48},{64,56},{56,... | collective-permute-start | bytes 393224 | tf_op jit(solution)/shard_map/ppermute | solution.py:26
  312.8 6.7 %collective-permute-start.19 = (f32[128,256]{1,0:T(8,128)S(1)}, f32[128,256]{1,0:T(8,128)S(1)}, u32[]{:S(2)}, u32[]{:S(2)}) collective-permute-start(f32[128,256]{1,0:T(8,128)S(1)} %get-tuple-element.27), channel_id=1, source_target_pairs={{16,0},{24,8},{32,16},{40,24},{48,32},{56,40},{64,48},{72,56},{80,... | collective-permute-start | bytes 393224 | tf_op jit(solution)/shard_map/ppermute | solution.py:26
  (97 shorter events, 34.0 us)
Async XLA Ops:
  0.6 58.3 %copy-start = (s32[1,5]{1,0:T(1,128)S(1)}, s32[1,5]{1,0:T(1,128)}, u32[]{:S(2)}) copy-start(s32[1,5]{1,0:T(1,128)} %param.7) | copy-start | bytes 64
  21.2 32.1 %collective-permute-start.2 = (bf16[1024,256]{1,0:T(8,128)(2,1)S(1)}, bf16[1024,256]{1,0:T(8,128)(2,1)S(1)}, u32[]{:S(2)}, u32[]{:S(2)}) collective-permute-start(bf16[1024,256]{1,0:T(8,128)(2,1)S(1)} %bitcast.6), channel_id=1, source_target_pairs={{752,0},{760,8},{0,16},{8,24},{16,32},{24,40},{32,48},{40,56},{48,... | collective-permute-start | bytes 1572872 | tf_op jit(solution)/shard_map/ppermute | solution.py:26
  29.0 24.3 %collective-permute-start.1 = (bf16[1024,256]{1,0:T(8,128)(2,1)S(1)}, bf16[1024,256]{1,0:T(8,128)(2,1)S(1)}, u32[]{:S(2)}, u32[]{:S(2)}) collective-permute-start(bf16[1024,256]{1,0:T(8,128)(2,1)S(1)} %bitcast.7), channel_id=1, source_target_pairs={{16,0},{24,8},{32,16},{40,24},{48,32},{56,40},{64,48},{72,56},{80,... | collective-permute-start | bytes 1572872 | tf_op jit(solution)/shard_map/ppermute | solution.py:26
  45.1 18.1 %all-to-all-start = ((bf16[8,128,256]{2,1,0:T(8,128)(2,1)}), bf16[8,128,256]{2,1,0:T(8,128)(2,1)S(1)}, u32[]{:S(2)}, u32[]{:S(2)}) async-start(bf16[8,128,256]{2,1,0:T(8,128)(2,1)} %broadcast_in_dim.24), calls=%async_computation | async-start | bytes 1048576 | tf_op jit(solution)/shard_map/all_to_all | solution.py:56
  48.6 14.6 %collective-permute-start = (bf16[1024,256]{1,0:T(8,128)(2,1)S(1)}, bf16[1024,256]{1,0:T(8,128)(2,1)S(1)}, u32[]{:S(2)}, u32[]{:S(2)}) collective-permute-start(bf16[1024,256]{1,0:T(8,128)(2,1)S(1)} %bitcast.8), channel_id=1, source_target_pairs={{8,0},{0,8},{24,16},{16,24},{40,32},{32,40},{56,48},{48,56},{72,64... | collective-permute-start | bytes 1572872 | tf_op jit(solution)/shard_map/ppermute | solution.py:26
  54.1 9.0 %collective-permute-start.3 = (bf16[1024,256]{1,0:T(8,128)(2,1)}, bf16[1024,256]{1,0:T(8,128)(2,1)S(1)}, u32[]{:S(2)}, u32[]{:S(2)}) collective-permute-start(bf16[1024,256]{1,0:T(8,128)(2,1)} %broadcast_select_fusion), channel_id=1, source_target_pairs={{8,0},{0,8},{24,16},{16,24},{40,32},{32,40},{56,48},{48,56},{72,64... | collective-permute-start | bytes 1572872 | tf_op jit(solution)/shard_map/ppermute | solution.py:26
  82.6 7.0 %copy-start.1 = (f32[1024,5120]{1,0:T(8,128)}, f32[1024,5120]{1,0:T(8,128)S(1)}, u32[]{:S(2)}) copy-start(f32[1024,5120]{1,0:T(8,128)S(1)} %get-tuple-element.15.entries) | copy-start | bytes 62914564
  90.5 16.9 %collective-permute-start.4 = (f32[6,1024]{1,0:T(8,128)S(1)}, f32[6,1024]{1,0:T(8,128)S(1)}, u32[]{:S(2)}, u32[]{:S(2)}) collective-permute-start(f32[6,1024]{1,0:T(8,128)S(1)} %broadcast_select_fusion.3), channel_id=1, source_target_pairs={{8,0},{0,8},{24,16},{16,24},{40,32},{32,40},{56,48},{48,56},{72,64... | collective-permute-start | bytes 73736 | tf_op jit(solution)/shard_map/ppermute | solution.py:26
  107.5 7.6 %collective-permute-start.5 = (f32[4,1024]{1,0:T(4,128)S(1)}, f32[4,1024]{1,0:T(4,128)S(1)}, u32[]{:S(2)}, u32[]{:S(2)}) collective-permute-start(f32[4,1024]{1,0:T(4,128)S(1)} %slice_select_fusion.2), channel_id=1, source_target_pairs={{752,0},{24,8},{0,16},{40,24},{16,32},{56,40},{32,48},{72,56},{48,... | collective-permute-start | bytes 49160 | tf_op jit(solution)/shard_map/ppermute | solution.py:26
  109.5 5.6 %collective-permute-start.6 = (f32[2,1024]{1,0:T(2,128)S(1)}, f32[2,1024]{1,0:T(2,128)S(1)}, u32[]{:S(2)}, u32[]{:S(2)}) collective-permute-start(f32[2,1024]{1,0:T(2,128)S(1)} %slice_select_fusion.5), channel_id=1, source_target_pairs={{736,0},{40,8},{752,16},{56,24},{0,32},{72,40},{16,48},{88,56},{32... | collective-permute-start | bytes 24584 | tf_op jit(solution)/shard_map/ppermute | solution.py:26
  115.2 7.2 %collective-permute-start.7 = (f32[6,1024]{1,0:T(8,128)S(1)}, f32[6,1024]{1,0:T(8,128)S(1)}, u32[]{:S(2)}, u32[]{:S(2)}) collective-permute-start(f32[6,1024]{1,0:T(8,128)S(1)} %fusion.1), channel_id=1, source_target_pairs={{8,0},{0,8},{24,16},{16,24},{40,32},{32,40},{56,48},{48,56},{72,64... | collective-permute-start | bytes 73736 | tf_op jit(solution)/shard_map/ppermute | solution.py:26
  130.6 169.0 %copy-start.7 = (bf16[128,256]{1,0:T(8,128)(2,1)S(1)}, bf16[128,256]{1,0:T(8,128)(2,1)}, u32[]{:S(2)}) copy-start(bf16[128,256]{1,0:T(8,128)(2,1)} %mine.1) | copy-start | bytes 196612
  179.8 13.7 %collective-permute-start.8 = (f32[6,1024]{1,0:T(8,128)S(1)}, f32[6,1024]{1,0:T(8,128)S(1)}, u32[]{:S(2)}, u32[]{:S(2)}) collective-permute-start(f32[6,1024]{1,0:T(8,128)S(1)} %broadcast_select_fusion.2), channel_id=1, source_target_pairs={{8,0},{0,8},{24,16},{16,24},{40,32},{32,40},{56,48},{48,56},{72,64... | collective-permute-start | bytes 73736 | tf_op jit(solution)/shard_map/ppermute | solution.py:26
  193.5 12.0 %collective-permute-start.9 = (f32[4,1024]{1,0:T(4,128)S(1)}, f32[4,1024]{1,0:T(4,128)S(1)}, u32[]{:S(2)}, u32[]{:S(2)}) collective-permute-start(f32[4,1024]{1,0:T(4,128)S(1)} %slice_select_fusion.1), channel_id=1, source_target_pairs={{752,0},{24,8},{0,16},{40,24},{16,32},{56,40},{32,48},{72,56},{48,... | collective-permute-start | bytes 49160 | tf_op jit(solution)/shard_map/ppermute | solution.py:26
  195.5 10.1 %collective-permute-start.10 = (f32[2,1024]{1,0:T(2,128)S(1)}, f32[2,1024]{1,0:T(2,128)S(1)}, u32[]{:S(2)}, u32[]{:S(2)}) collective-permute-start(f32[2,1024]{1,0:T(2,128)S(1)} %slice_select_fusion.4), channel_id=1, source_target_pairs={{736,0},{40,8},{752,16},{56,24},{0,32},{72,40},{16,48},{88,56},{32... | collective-permute-start | bytes 24584 | tf_op jit(solution)/shard_map/ppermute | solution.py:26
  205.7 4.0 %collective-permute-start.11 = (f32[6,1024]{1,0:T(8,128)S(1)}, f32[6,1024]{1,0:T(8,128)S(1)}, u32[]{:S(2)}, u32[]{:S(2)}) collective-permute-start(f32[6,1024]{1,0:T(8,128)S(1)} %fusion.3), channel_id=1, source_target_pairs={{8,0},{0,8},{24,16},{16,24},{40,32},{32,40},{56,48},{48,56},{72,64... | collective-permute-start | bytes 73736 | tf_op jit(solution)/shard_map/ppermute | solution.py:26
  266.7 13.6 %collective-permute-start.12 = (f32[6,1024]{1,0:T(8,128)S(1)}, f32[6,1024]{1,0:T(8,128)S(1)}, u32[]{:S(2)}, u32[]{:S(2)}) collective-permute-start(f32[6,1024]{1,0:T(8,128)S(1)} %broadcast_select_fusion.1), channel_id=1, source_target_pairs={{8,0},{0,8},{24,16},{16,24},{40,32},{32,40},{56,48},{48,56},{72,64... | collective-permute-start | bytes 73736 | tf_op jit(solution)/shard_map/ppermute | solution.py:26
  280.4 14.9 %collective-permute-start.13 = (f32[4,1024]{1,0:T(4,128)S(1)}, f32[4,1024]{1,0:T(4,128)S(1)}, u32[]{:S(2)}, u32[]{:S(2)}) collective-permute-start(f32[4,1024]{1,0:T(4,128)S(1)} %slice_select_fusion), channel_id=1, source_target_pairs={{752,0},{24,8},{0,16},{40,24},{16,32},{56,40},{32,48},{72,56},{48,... | collective-permute-start | bytes 49160 | tf_op jit(solution)/shard_map/ppermute | solution.py:26
  282.3 13.0 %collective-permute-start.14 = (f32[2,1024]{1,0:T(2,128)S(1)}, f32[2,1024]{1,0:T(2,128)S(1)}, u32[]{:S(2)}, u32[]{:S(2)}) collective-permute-start(f32[2,1024]{1,0:T(2,128)S(1)} %slice_select_fusion.3), channel_id=1, source_target_pairs={{736,0},{40,8},{752,16},{56,24},{0,32},{72,40},{16,48},{88,56},{32... | collective-permute-start | bytes 24584 | tf_op jit(solution)/shard_map/ppermute | solution.py:26
  295.4 4.0 %collective-permute-start.15 = (f32[6,1024]{1,0:T(8,128)S(1)}, f32[6,1024]{1,0:T(8,128)S(1)}, u32[]{:S(2)}, u32[]{:S(2)}) collective-permute-start(f32[6,1024]{1,0:T(8,128)S(1)} %fusion.5), channel_id=1, source_target_pairs={{8,0},{0,8},{24,16},{16,24},{40,32},{32,40},{56,48},{48,56},{72,64... | collective-permute-start | bytes 73736 | tf_op jit(solution)/shard_map/ppermute | solution.py:26
  304.5 15.0 %collective-permute-start.16 = (f32[128,256]{1,0:T(8,128)S(1)}, f32[128,256]{1,0:T(8,128)S(1)}, u32[]{:S(2)}, u32[]{:S(2)}) collective-permute-start(f32[128,256]{1,0:T(8,128)S(1)} %get-tuple-element.24), channel_id=1, source_target_pairs={{8,0},{0,8},{24,16},{16,24},{40,32},{32,40},{56,48},{48,56},{72,64... | collective-permute-start | bytes 393224 | tf_op jit(solution)/shard_map/ppermute | solution.py:26
  306.7 12.8 %collective-permute-start.17 = (f32[128,256]{1,0:T(8,128)S(1)}, f32[128,256]{1,0:T(8,128)S(1)}, u32[]{:S(2)}, u32[]{:S(2)}) collective-permute-start(f32[128,256]{1,0:T(8,128)S(1)} %get-tuple-element.25), channel_id=1, source_target_pairs={{760,0},{16,8},{8,16},{32,24},{24,32},{48,40},{40,48},{64,56},{56,... | collective-permute-start | bytes 393224 | tf_op jit(solution)/shard_map/ppermute | solution.py:26
  310.9 9.0 %collective-permute-start.18 = (f32[128,256]{1,0:T(8,128)S(1)}, f32[128,256]{1,0:T(8,128)S(1)}, u32[]{:S(2)}, u32[]{:S(2)}) collective-permute-start(f32[128,256]{1,0:T(8,128)S(1)} %get-tuple-element.26), channel_id=1, source_target_pairs={{752,0},{760,8},{0,16},{8,24},{16,32},{24,40},{32,48},{40,56},{48,... | collective-permute-start | bytes 393224 | tf_op jit(solution)/shard_map/ppermute | solution.py:26
  312.8 8.6 %collective-permute-start.19 = (f32[128,256]{1,0:T(8,128)S(1)}, f32[128,256]{1,0:T(8,128)S(1)}, u32[]{:S(2)}, u32[]{:S(2)}) collective-permute-start(f32[128,256]{1,0:T(8,128)S(1)} %get-tuple-element.27), channel_id=1, source_target_pairs={{16,0},{24,8},{32,16},{40,24},{48,32},{56,40},{64,48},{72,56},{80,... | collective-permute-start | bytes 393224 | tf_op jit(solution)/shard_map/ppermute | solution.py:26
  (7 other events, 18.7 us)

commit v3 on v2

--- a/solution.py
+++ b/solution.py
@@ -35,19 +35,18 @@
     return from_row(block, lambda i: (i - distance) % count)
 
 
-def from_chip(block, reach):
+def swap_chips(block, second):
     count = lax.axis_size("row")
 
     def source_of(i):
-        step = -2 * reach if i % 2 == 0 else 2 * reach
-        return (i + step) % count
+        chip, core = divmod(i, 2)
+        reach = 1 + core
+        up = (chip // reach) % 2 == 0
+        if second:
+            up = not up
+        return (i + 2 * reach if up else i - 2 * reach) % count
 
     return from_row(block, source_of)
-
-
-def swap_cross(block):
-    count = lax.axis_size("row")
-    return from_row(block, lambda i: (i - 1 if i % 2 == 0 else i + 1) % count)
 
 
 def gathered(shard):
@@ -61,29 +60,46 @@
     return top + jnp.log2(jnp.exp2(a - top) + jnp.exp2(b - top))
 
 
-def column_totals(partial, even):
-    own, mate, cross, up, down = (partial[p] for p in range(WINDOW))
-    none = jnp.full_like(own, NEG)
-    six = jnp.where(
-        even,
-        jnp.stack([down, cross, own, mate, up, none]),
-        jnp.stack([none, down, mate, own, cross, up]),
-    )
-    chip = lse2(six, swap_mate(six))
-    near = from_chip(jnp.where(even, chip[2:6], chip[0:4]), 1)
-    far = from_chip(jnp.where(even, chip[4:6], chip[0:2]), 2)
-    blank = jnp.full_like(far, NEG)
+def column_totals(partial, row, extra=False):
+    even = row % 2 == 0
+    up = (row // 2) // (1 + row % 2) % 2 == 0
+    count = 2 if extra else 0
+    other = swap_mate(partial[: 6 + count])
+    chip = lse2(partial[:6], other[:6])
+    to_above, to_below = chip[2:6], chip[0:4]
+    if count:
+        mine = partial[6:8]
+        here = jnp.where(
+            even, jnp.concatenate([mine, other[6:]]), jnp.concatenate([other[6:], mine])
+        )
+        to_above = jnp.concatenate([to_above, here])
+        to_below = jnp.concatenate([to_below, here])
+    one = swap_chips(jnp.where(up, to_above, to_below), False)
+    two = swap_chips(jnp.where(up, to_below, to_above), True)
+    above = jnp.where(up, one, two)
+    below = jnp.where(up, two, one)
+    blank = jnp.full_like(above[0:2], NEG)
     outer = jnp.where(
         even,
-        jnp.concatenate([lse2(near[0:2], far), near[2:4], blank]),
-        jnp.concatenate([blank, near[0:2], lse2(near[2:4], far)]),
+        jnp.concatenate([below[0:2], lse2(below[2:4], above[0:2]), above[2:4]]),
+        jnp.concatenate([below[2:4], blank, above[0:2]]),
     )
-    total = lse2(chip, lse2(outer, swap_mate(outer)))
-    return jnp.where(
-        even,
-        jnp.stack([total[2], total[3], total[1], total[4], total[0]]),
-        jnp.stack([total[3], total[2], total[4], total[5], total[1]]),
-    )
+    sent = jnp.concatenate([outer, below[4:], above[4:]]) if count else outer
+    got = swap_mate(sent)
+    total = lse2(chip, lse2(outer, got[:6]))
+
+    def placed(rows):
+        return jnp.where(
+            even,
+            jnp.stack([rows[2], rows[3], rows[1], rows[4], rows[0]]),
+            jnp.stack([rows[3], rows[2], rows[4], rows[5], rows[1]]),
+        )
+
+    if not count:
+        return placed(total)
+    near = jnp.where(even, sent[6:], got[6:])
+    around = jnp.concatenate([near[:4], here, near[4:]]).reshape(6, count, -1)
+    return placed(total), placed(around)
 
 
 def dot_nt(a, b):
@@ -109,25 +125,39 @@
     return best + jnp.log2(acc)
 
 
-def put_columns(listed, base, col, sums_out, fine):
+def is_even():
+    return lax.rem(lax.axis_index("row"), 2) == 0
+
+
+def place(p):
+    low, high = ((2, 3), (3, 2), (1, 4), (4, 5), (0, 1))[p]
+    return pl.ds(jnp.where(is_even(), low, high), 1)
+
+
+def is_listed(mask, p):
+    low, high = ((2, 2), (3, 1), (1, 3), (4, 4), (0, 0))[p]
+    return mask[0, jnp.where(is_even(), low, high)] == 1
+
+
+def put_columns(mask, base, col, sums_out, fine):
     count = sums_out.shape[1]
     sums_out[...] = jnp.full(sums_out.shape, NEG, jnp.float32)
     for p in range(WINDOW):
         sums = jnp.sum(col[:, p * count : (p + 1) * count], axis=0, keepdims=True)
-        taken = listed[p] == 1
-        sums_out[p : p + 1, :] = jnp.where(taken, jnp.log2(sums) - base[p : p + 1, :], NEG)
+        taken = is_listed(mask, p)
+        sums_out[place(p), :] = jnp.where(taken, jnp.log2(sums) - base[p : p + 1, :], NEG)
         good = jnp.where(jnp.logical_or(jnp.logical_not(taken), sums >= SAFE_SUM), 1.0, 0.0)
         for q in range(count // LANES):
             fine = jnp.minimum(fine, good[:, q * LANES : (q + 1) * LANES])
     return jnp.min(fine) > 0.5
 
 
-def put_exact_columns(listed, fetch, dual, sums_out):
-    for p in range(WINDOW):
-
-        @pl.when(listed[p] == 1)
+def put_exact_columns(mask, fetch, dual, sums_out):
+    for p in range(WINDOW):
+
+        @pl.when(is_listed(mask, p))
         def _(p=p):
-            sums_out[p : p + 1, :] = exact_columns(*fetch(p), dual)
+            sums_out[place(p), :] = exact_columns(*fetch(p), dual)
 
 
 def add_columns(entries, here, scale, col, width):
@@ -136,7 +166,7 @@
         col[:, q * LANES : (q + 1) * LANES] += jnp.sum(e.reshape(LANES // 8, 8, LANES), axis=0)
 
 
-def first_kernel(listed, rows, t0, t1, t2, t3, t4, entries, sums_out, top_out, base, dual, peak, col):
+def first_kernel(mask, rows, t0, t1, t2, t3, t4, entries, sums_out, top_out, base, dual, peak, col):
     targets = (t0, t1, t2, t3, t4)
     count = rows.shape[0]
     base[...] = jnp.zeros(base.shape, jnp.float32)
@@ -152,7 +182,7 @@
             axis=1,
         )
         bias = -KAPPA * bias
-        bias = jnp.where(listed[p] == 1, bias, NEG)
+        bias = jnp.where(is_listed(mask, p), bias, NEG)
         base[p : p + 1, :] = bias
 
         block = dot_nt(rows[...], targets[p][...]) * TWO_KAPPA + bias
@@ -192,15 +222,15 @@
     exponentials(0, lambda: None)
     lax.fori_loop(1, count // LANES, both, 0)
     columns(count // LANES - 1)
-    fine = put_columns(listed, base, col, sums_out, jnp.ones((1, LANES), jnp.float32))
+    fine = put_columns(mask, base, col, sums_out, jnp.ones((1, LANES), jnp.float32))
 
     @pl.when(jnp.logical_not(fine))
     def _():
-        put_exact_columns(listed, lambda p: (rows, targets[p]), dual, sums_out)
+        put_exact_columns(mask, lambda p: (rows, targets[p]), dual, sums_out)
 
 
 def later_kernel(
-    listed, entries, pot, base, top, rows_far, t0, t1, t2, t3, t4, sums_out, dual_out, gain, col, low, total, rows, target
+    mask, entries, pot, base, top, rows_far, t0, t1, t2, t3, t4, sums_out, dual_out, gain, col, low, total, rows, target
 ):
     targets = (t0, t1, t2, t3, t4)
     count = rows.shape[0]
@@ -214,7 +244,7 @@
     width = WINDOW * count // LANES
     worst = jnp.zeros((1, count), jnp.float32)
     for p in range(WINDOW):
-        taken = listed[p] == 1
+        taken = is_listed(mask, p)
         shift = jnp.where(taken, pot[p : p + 1, :] - base[p : p + 1, :], 0.0)
         worst = jnp.maximum(worst, jnp.abs(shift))
         gain[:, p * count : (p + 1) * count] = jnp.broadcast_to(
@@ -250,12 +280,12 @@
     fine = jnp.where(jnp.min(low[...], axis=0, keepdims=True) >= SAFE_ROW, 1.0, 0.0)
     for q in range(count // LANES):
         fine = jnp.minimum(fine, jnp.where(worst[:, q * LANES : (q + 1) * LANES] <= SAFE_SHIFT, 1.0, 0.0))
-    fine = put_columns(listed, base, col, sums_out, fine)
+    fine = put_columns(mask, base, col, sums_out, fine)
 
     @pl.when(jnp.logical_not(fine))
     def _():
         def value(p, here):
-            bias = jnp.where(listed[p] == 1, pot[p : p + 1, :], NEG)
+            bias = jnp.where(is_listed(mask, p), pot[p : p + 1, :], NEG)
             return dot_nt(rows[here, :], target[...]) * TWO_KAPPA + bias
 
         dual_out[...] = jnp.full(dual_out.shape, NEG, jnp.float32)
@@ -282,7 +312,16 @@
             lax.fori_loop(0, count // LANES, add, 0)
         dual_out[...] = -(dual_out[...] + jnp.log2(total[...]))
 
-        put_exact_columns(listed, fetch, dual_out, sums_out)
+        put_exact_columns(mask, fetch, dual_out, sums_out)
+
+    for r in range(count // LANES):
+        here = slice(r * LANES, (r + 1) * LANES)
+        sums_out[6:7, here] = dual_out[here, :].T[0:1, :]
+    lane = lax.broadcasted_iota(jnp.int32, (1, LANES), 1)
+    pairs = jnp.zeros((1, LANES), jnp.float32)
+    for k in range(WINDOW):
+        pairs = jnp.where(lane == k, mask[0, k].astype(jnp.float32), pairs)
+    sums_out[7:8, 0:LANES] = pairs
 
 
 VMEM = pl.BlockSpec(memory_space=pltpu.VMEM)
@@ -290,7 +329,7 @@
 SMEM = pl.BlockSpec(memory_space=pltpu.SMEM)
 
 
-def first_step(listed, rows, targets):
+def first_step(mask, rows, targets):
     count, width = rows.shape
     pairs = WINDOW * count * count
     row = jax.ShapeDtypeStruct((8, count), jnp.float32)
@@ -310,10 +349,10 @@
             flops=2 * pairs * width, bytes_accessed=12 * count * width, transcendentals=pairs
         ),
         name="first_step",
-    )(listed, rows, *targets)
-
-
-def later_step(listed, entries, pot, base, top, rows, targets):
+    )(mask, rows, *targets)
+
+
+def later_step(mask, entries, pot, base, top, rows, targets):
     count, width = rows.shape
     pairs = WINDOW * count * count
     row = jax.ShapeDtypeStruct((8, count), jnp.float32)
@@ -337,85 +376,89 @@
             flops=4 * pairs, bytes_accessed=12 * count * width, transcendentals=0
         ),
         name="later_step",
-    )(listed, entries, pot, base, top, rows, *targets)
-
-
-def grad_kernel(scal, pot, dual, mine, rows, t0, t1, t2, t3, t4, source_out, o0, o1, o2, o3, o4):
+    )(mask, entries, pot, base, top, rows, *targets)
+
+
+def grad_kernel(
+    mask, pot, dual, around, mine, own, t0, t1, t2, t3, t4, x0, x1, x2, x3, x4, source_out, target_out
+):
     targets = (t0, t1, t2, t3, t4)
-    outs = (o0, o1, o2, o3, o4)
-    count = rows.shape[0]
-    at = pl.multiple_of(scal[WINDOW] * LANES, LANES)
-    here = pl.ds(at, LANES)
-    own_dual = dual[here, 0:1]
-    dual_row = jnp.concatenate(
-        [dual[r * LANES : (r + 1) * LANES, :].T[0:1, :] for r in range(count // LANES)], axis=1
-    )
+    sources = (x0, x1, x2, x3, x4)
+    width = own.shape[1]
+    here = pl.ds(pl.multiple_of(lax.axis_index("grp") * LANES, LANES), LANES)
+    dual_column = dual[here, 0:1]
     mass = jnp.zeros((LANES, 1), jnp.float32)
-    carried = jnp.zeros((LANES, rows.shape[1]), jnp.float32)
-    for p in range(WINDOW):
-        bias = jnp.where(scal[p] == 1, pot[p : p + 1, :], NEG)
-        weight = jnp.exp2(dot_nt(mine[...], targets[p][...]) * TWO_KAPPA + (own_dual + bias))
+    carried = jnp.zeros((LANES, width), jnp.float32)
+    for p in range(WINDOW):
+        bias = jnp.where(is_listed(mask, p), pot[p : p + 1, :], NEG)
+        weight = jnp.exp2(dot_nt(mine[...], targets[p][...]) * TWO_KAPPA + (dual_column + bias))
         weight = weight.astype(jnp.bfloat16)
         mass = mass + jnp.sum(weight.astype(jnp.float32), axis=1, keepdims=True)
         carried = carried + jnp.dot(weight, targets[p][...], preferred_element_type=jnp.float32)
     source_out[...] = 2.0 * (mine[...].astype(jnp.float32) * mass - carried)
 
-    for p in range(WINDOW):
-        bias = jnp.where(scal[p] == 1, pot[p : p + 1, here], NEG)
-        bias = jnp.broadcast_to(bias, (LANES, LANES)).T[:, 0:1]
-        some = targets[p][here, :]
-        weight = jnp.exp2(dot_nt(some, rows[...]) * TWO_KAPPA + (dual_row + bias))
+    bias = jnp.broadcast_to(pot[0:1, here], (LANES, LANES)).T[:, 0:1]
+    lane = lax.broadcasted_iota(jnp.int32, (1, LANES), 1)
+    mass = jnp.zeros((LANES, 1), jnp.float32)
+    pulled = jnp.zeros((LANES, width), jnp.float32)
+    for p in range(WINDOW):
+        low, high = ((2, 2), (1, 3), (3, 1), (0, 0), (4, 4))[p]
+        slot = jnp.where(is_even(), low, high)
+        taken = jnp.max(jnp.where(lane == slot, around[p, 1:2, 0:LANES], 0.0), axis=1, keepdims=True)
+        shift = jnp.where(taken > 0.5, around[p, 0:1, :], NEG) + bias
+        weight = jnp.exp2(dot_nt(own[...], sources[p][...]) * TWO_KAPPA + shift)
         weight = weight.astype(jnp.bfloat16)
-        mass = jnp.sum(weight.astype(jnp.float32), axis=1, keepdims=True)
-        pulled = jnp.dot(weight, rows[...], preferred_element_type=jnp.float32)
-        outs[p][...] = some.astype(jnp.float32) * mass - pulled
-
-
-def gradients(scal, pot, dual, mine, rows, targets):
-    count, width = rows.shape
+        mass = mass + jnp.sum(weight.astype(jnp.float32), axis=1, keepdims=True)
+        pulled = pulled + jnp.dot(weight, sources[p][...], preferred_element_type=jnp.float32)
+    target_out[...] = 2.0 * (own[...].astype(jnp.float32) * mass - pulled)
+
+
+def gradients(mask, pot, dual, around, mine, own, targets, sources):
+    width = mine.shape[1]
+    count = sources[0].shape[0]
     part = jax.ShapeDtypeStruct((LANES, width), jnp.float32)
     pairs = 2 * WINDOW * count * LANES
     return pl.pallas_call(
         grad_kernel,
-        out_shape=(part,) * (1 + WINDOW),
-        in_specs=[SMEM] + [VMEM] * 9,
-        out_specs=(VMEM,) * (1 + WINDOW),
+        out_shape=(part, part),
+        in_specs=[SMEM] + [VMEM] * 15,
+        out_specs=(VMEM, VMEM),
         compiler_params=pltpu.CompilerParams(vmem_limit_bytes=SCOPED),
         cost_estimate=pl.CostEstimate(
-            flops=4 * pairs * width, bytes_accessed=16 * count * width, transcendentals=pairs
+            flops=4 * pairs * width, bytes_accessed=20 * count * width, transcendentals=pairs
         ),
         name="plan_gradients",
-    )(scal, pot, dual, mine, rows, *targets)
+    )(mask, pot, dual, around, mine, own, *targets, *sources)
+
+
+def neighbours(block, even):
+    above = shifted(block, -2)
+    below = shifted(block, 2)
+    mate = swap_mate(block)
+    cross = swap_mate(jnp.where(even, above, below))
+    return block, mate, cross, above, below
 
 
 def shards(source, target, pair_mask):
-    even = lax.axis_index("row") % 2 == 0
-    own = gathered(target)
-    above = shifted(own, -2)
-    below = shifted(own, 2)
-    mate = swap_mate(own)
+    row = lax.axis_index("row")
+    even = row % 2 == 0
+    targets = neighbours(gathered(target), even)
+    rows = gathered(source)
+    entries, partial, top, base = first_step(pair_mask, rows, targets)
+    above = shifted(rows, -2)
+    below = shifted(rows, 2)
+    mate = swap_mate(rows)
+    partial, above, below, mate = lax.optimization_barrier((partial, above, below, mate))
     cross = swap_mate(jnp.where(even, above, below))
-    rows = gathered(source)
-    targets = (own, mate, cross, above, below)
-    mask = pair_mask[0]
-    listed = jnp.where(even, mask[jnp.array([2, 3, 1, 4, 0])], mask[jnp.array([2, 1, 3, 4, 0])])
-    entries, partial, top, base = first_step(listed, rows, targets)
-    pot = -column_totals(partial, even)
-    for _ in range(ITERS - 1):
-        partial, dual = later_step(listed, entries, pot, base, top, rows, targets)
-        pot = -column_totals(partial, even)
-    scal = jnp.concatenate([listed, lax.axis_index("grp").astype(jnp.int32)[None]])
-    source_grad, part_own, part_mate, part_cross, part_above, part_below = gradients(
-        scal, pot, dual, source, rows, targets
-    )
-    total = (
-        part_own
-        + swap_mate(part_mate)
-        + swap_cross(part_cross)
-        + shifted(part_above, 2)
-        + shifted(part_below, -2)
-    )
-    return source_grad, 2.0 * total
+    pot = -column_totals(partial, row)
+    pot, cross = lax.optimization_barrier((pot, cross))
+    sources = (rows, mate, cross, above, below)
+    for _ in range(ITERS - 2):
+        partial, dual = later_step(pair_mask, entries, pot, base, top, rows, targets)
+        pot = -column_totals(partial, row)
+    partial, dual = later_step(pair_mask, entries, pot, base, top, rows, targets)
+    total, around = column_totals(partial, row, True)
+    return gradients(pair_mask, -total, dual, around, source, target, targets, sources)
 
 
 def solution(mesh):

time: 325 us -> 311 us (0.957)
  Pallas kernels: 120 us -> 103 us
  waiting for transfers between devices: 11.4 us -> 20.9 us
  local copies, waits for them, and re-layouts: 29.9 us -> 22.3 us
  starting transfers between devices: 136 us -> 140 us
    pallas_call x2, Pallas kernels: 97 us -> 85 us  [later_step(): pl.pallas_call(later_kernel, out_shape=(row, column), in_specs=[SMEM] + [...]
    ppermute x20, waiting for transfers between devices: 9.19 us -> 16 us  [from_row(): return lax.ppermute(block, 'row', [(source_of(i), i) for i in range(count)])]
    unnamed x20 -> x35, local copies, waits for them, and re-layouts: 25.6 us -> 19.6 us
    pallas_call x1, Pallas kernels: 19.5 us -> 13.9 us  [first_step(): pl.pallas_call(first_kernel, out_shape=(pltpu.VMEM((count, WINDOW * count...]
    ppermute x20, starting transfers between devices: 133 us -> 136 us  [from_row(): return lax.ppermute(block, 'row', [(source_of(i), i) for i in range(count)])]
  transfers between devices with their start and end apart: 21 -> 21, of which waited for: 12 -> 10; matrix products, arithmetic and copies ran while one was open for 2% -> 1% of each run, Pallas kernels for 0% -> 4%
where the time goes in v3:
time: 311 us; the launch traced here: 309 us
  starting transfers between devices  140 us (45%)
  Pallas kernels  103 us (33%)
  local copies, waits for them, and re-layouts  22.3 us (7%)
  waiting for transfers between devices  20.9 us (7%)
  blocking collectives  19.7 us (6%)
    ppermute x20, starting transfers between devices, from_row(): return lax.ppermute(block, 'row', [(source_of(i), i) for i in range(count)])  136 us
    pallas_call x2, Pallas kernels, later_step(): pl.pallas_call(later_kernel, out_shape=(row, column), in_specs=[SMEM] + [...  85 us
    all_to_all x1, blocking collectives, gathered(): lax.all_to_all(copies, 'grp', 0, 0, tiled=True).reshape(-1, shard.shape[1])  19.7 us
    unnamed x35, local copies, waits for them, and re-layouts  19.6 us
    ppermute x20, waiting for transfers between devices, from_row(): return lax.ppermute(block, 'row', [(source_of(i), i) for i in range(count)])  16 us
    pallas_call x1, Pallas kernels, first_step(): pl.pallas_call(first_kernel, out_shape=(pltpu.VMEM((count, WINDOW * count...  13.9 us
  transfers between devices with their start and end apart: 21, of which 10 were waited for; matrix products, arithmetic and copies ran while one was open for 1% of the time, Pallas kernels for 4%

profile of v3, /device:TPU:1, one launch (start us, length us, event | category | flops | bytes accessed | tf_op | source)
XLA Modules:
  0.0 309.4 jit_solution(2554101543497859466)
XLA Ops:
  1.5 19.7 %all_to_all.10 = bf16[8,128,256]{2,1,0:T(8,128)(2,1)S(1)} all-to-all(bf16[8,128,256]{2,1,0:T(8,128)(2,1)S(1)} %broadcast_in_dim.5), channel_id=1, replica_groups=mesh['row'=96,'grp'=8] {'grp'}, dimensions={0} | all-to-all | bytes 1048576 | tf_op jit(solution)/shard_map/all_to_all | solution.py:55
  21.2 7.8 %collective-permute-start.2 = (bf16[1024,256]{1,0:T(8,128)(2,1)S(1)}, bf16[1024,256]{1,0:T(8,128)(2,1)S(1)}, u32[]{:S(2)}, u32[]{:S(2)}) collective-permute-start(bf16[1024,256]{1,0:T(8,128)(2,1)S(1)} %bitcast.36), channel_id=1, source_target_pairs={{752,0},{760,8},{0,16},{8,24},{16,32},{24,40},{32,48},{40,56},{48,... | collective-permute-start | bytes 1572872 | tf_op jit(solution)/shard_map/ppermute | solution.py:26
  28.9 14.4 %collective-permute-start.1 = (bf16[1024,256]{1,0:T(8,128)(2,1)S(1)}, bf16[1024,256]{1,0:T(8,128)(2,1)S(1)}, u32[]{:S(2)}, u32[]{:S(2)}) collective-permute-start(bf16[1024,256]{1,0:T(8,128)(2,1)S(1)} %bitcast.37), channel_id=1, source_target_pairs={{16,0},{24,8},{32,16},{40,24},{48,32},{56,40},{64,48},{72,56},{80,... | collective-permute-start | bytes 1572872 | tf_op jit(solution)/shard_map/ppermute | solution.py:26
  45.1 3.5 %all-to-all-start = ((bf16[8,128,256]{2,1,0:T(8,128)(2,1)}), bf16[8,128,256]{2,1,0:T(8,128)(2,1)S(1)}, u32[]{:S(2)}, u32[]{:S(2)}) async-start(bf16[8,128,256]{2,1,0:T(8,128)(2,1)} %broadcast_in_dim.4), calls=%async_computation | async-start | bytes 1048576 | tf_op jit(solution)/shard_map/all_to_all | solution.py:55
  48.6 4.6 %collective-permute-start = (bf16[1024,256]{1,0:T(8,128)(2,1)S(1)}, bf16[1024,256]{1,0:T(8,128)(2,1)S(1)}, u32[]{:S(2)}, u32[]{:S(2)}) collective-permute-start(bf16[1024,256]{1,0:T(8,128)(2,1)S(1)} %bitcast.38), channel_id=1, source_target_pairs={{8,0},{0,8},{24,16},{16,24},{40,32},{32,40},{56,48},{48,56},{72,64... | collective-permute-start | bytes 1572872 | tf_op jit(solution)/shard_map/ppermute | solution.py:26
  54.1 4.1 %collective-permute-start.3 = (bf16[1024,256]{1,0:T(8,128)(2,1)}, bf16[1024,256]{1,0:T(8,128)(2,1)S(1)}, u32[]{:S(2)}, u32[]{:S(2)}) collective-permute-start(bf16[1024,256]{1,0:T(8,128)(2,1)} %broadcast_select_fusion.1), channel_id=1, source_target_pairs={{8,0},{0,8},{24,16},{16,24},{40,32},{32,40},{56,48},{48,56},{72,64... | collective-permute-start | bytes 1572872 | tf_op jit(solution)/shard_map/ppermute | solution.py:26
  58.3 4.9 %all-to-all-done = bf16[8,128,256]{2,1,0:T(8,128)(2,1)S(1)} async-done(((bf16[8,128,256]{2,1,0:T(8,128)(2,1)}), bf16[8,128,256]{2,1,0:T(8,128)(2,1)S(1)}, u32[]{:S(2)}, u32[]{:S(2)}) %all-to-all-start) | async-done | bytes 524320 | tf_op jit(solution)/shard_map/all_to_all | solution.py:55
  63.1 5.7 %collective-permute-start.6 = (bf16[1024,256]{1,0:T(8,128)(2,1)S(1)}, bf16[1024,256]{1,0:T(8,128)(2,1)S(1)}, u32[]{:S(2)}, u32[]{:S(2)}) collective-permute-start(bf16[1024,256]{1,0:T(8,128)(2,1)S(1)} %bitcast.43), channel_id=1, source_target_pairs={{8,0},{0,8},{24,16},{16,24},{40,32},{32,40},{56,48},{48,56},{72,64... | collective-permute-start | bytes 1572872 | tf_op jit(solution)/shard_map/ppermute | solution.py:26
  70.8 6.7 %collective-permute-start.4 = (bf16[1024,256]{1,0:T(8,128)(2,1)S(1)}, bf16[1024,256]{1,0:T(8,128)(2,1)S(1)}, u32[]{:S(2)}, u32[]{:S(2)}) collective-permute-start(bf16[1024,256]{1,0:T(8,128)(2,1)S(1)} %bitcast.45), channel_id=1, source_target_pairs={{16,0},{24,8},{32,16},{40,24},{48,32},{56,40},{64,48},{72,56},{80,... | collective-permute-start | bytes 1572872 | tf_op jit(solution)/shard_map/ppermute | solution.py:26
  78.1 13.9 %first_step.1 = (f32[1024,5120]{1,0:T(8,128)S(1)}, f32[8,1024]{1,0:T(8,128)S(1)}, f32[1024,128]{1,0:T(8,128)S(1)}, f32[8,1024]{1,0:T(8,128)S(1)}) custom-call(s32[1,5]{1,0:T(1,128)S(1)} %copy-done.12, bf16[1024,256]{1,0:T(8,128)(2,1)S(1)} %bitcast.46, bf16[1024,256]{1,0:T(8,128)(2,1)S(1)} %bitcast.39, bf16[1024,256]{1,0:T(8,128)(2,1)S(1)} %collective-permute-done.t1, ...), custom_call_target="tpu_custom_call" | custom-call | flops 2684354560 | bytes 3145728 | tf_op jit(solution)/shard_map/first_step/pallas_call | solution.py:337
  92.1 7.0 %copy-done = f32[1024,5120]{1,0:T(8,128)} copy-done((f32[1024,5120]{1,0:T(8,128)}, f32[1024,5120]{1,0:T(8,128)S(1)}, u32[]{:S(2)}) %copy-start) | copy-done | bytes 20971544
  102.3 2.5 collective-permute-start.7
  105.6 20.6 %collective-permute-start.8 = (f32[4,1024]{1,0:T(4,128)S(1)}, f32[4,1024]{1,0:T(4,128)S(1)}, u32[]{:S(2)}, u32[]{:S(2)}) collective-permute-start(f32[4,1024]{1,0:T(4,128)S(1)} %get-tuple-element.72), channel_id=1, source_target_pairs={{752,0},{744,8},{32,16},{760,24},{16,32},{72,40},{64,48},{88,56},{... | collective-permute-start | bytes 49160 | tf_op jit(solution)/shard_map/ppermute | solution.py:26
  128.3 3.4 %collective-permute-done.9 = f32[4,1024]{1,0:T(4,128)S(1)} collective-permute-done((f32[4,1024]{1,0:T(4,128)S(1)}, f32[4,1024]{1,0:T(4,128)S(1)}, u32[]{:S(2)}, u32[]{:S(2)}) %collective-permute-start.9) | collective-permute-done | bytes 16416 | tf_op jit(solution)/shard_map/ppermute | solution.py:26
  134.8 2.4 collective-permute-start.11
  138.7 7.0 %copy-done.1 = f32[1024,5120]{1,0:T(8,128)S(1)} copy-done((f32[1024,5120]{1,0:T(8,128)S(1)}, f32[1024,5120]{1,0:T(8,128)}, u32[]{:S(2)}) %copy-start.1) | copy-done | bytes 20971544
  147.4 43.0 %later_step.2 = (f32[8,1024]{1,0:T(8,128)S(1)}, f32[1024,128]{1,0:T(8,128)}) custom-call(s32[1,5]{1,0:T(1,128)S(1)} %copy-done.13, f32[1024,5120]{1,0:T(8,128)S(1)} %copy-done.1, f32[5,1024]{1,0:T(8,128)S(1)} %fusion.pot, f32[8,1024]{1,0:T(8,128)S(1)} %get-tuple-element.21.base, f32[1024,128]{1,0:T(8,128)S(1)} %copy-done.3, bf16[1024,256]{1,0:T(8,128)(2,1)S(1)} %bitcast.47, ...), custom_call_target="tpu_custom_call" | custom-call | flops 20971520 | bytes 3145728 | tf_op jit(solution)/shard_map/later_step/pallas_call | solution.py:361
  193.6 24.4 %collective-permute-start.13 = (f32[4,1024]{1,0:T(4,128)S(1)}, f32[4,1024]{1,0:T(4,128)S(1)}, u32[]{:S(2)}, u32[]{:S(2)}) collective-permute-start(f32[4,1024]{1,0:T(4,128)S(1)} %get-tuple-element.61), channel_id=1, source_target_pairs={{752,0},{744,8},{32,16},{760,24},{16,32},{72,40},{64,48},{88,56},{... | collective-permute-start | bytes 49160 | tf_op jit(solution)/shard_map/ppermute | solution.py:26
  219.9 3.4 %collective-permute-done.14 = f32[4,1024]{1,0:T(4,128)S(1)} collective-permute-done((f32[4,1024]{1,0:T(4,128)S(1)}, f32[4,1024]{1,0:T(4,128)S(1)}, u32[]{:S(2)}, u32[]{:S(2)}) %collective-permute-start.14) | collective-permute-done | bytes 16416 | tf_op jit(solution)/shard_map/ppermute | solution.py:26
  226.7 42.0 %later_step.3 = (f32[8,1024]{1,0:T(8,128)S(1)}, f32[1024,128]{1,0:T(8,128)S(1)}) custom-call(s32[1,5]{1,0:T(1,128)S(1)} %copy-done.13, f32[1024,5120]{1,0:T(8,128)S(1)} %copy-done.1, f32[5,1024]{1,0:T(8,128)S(1)} %fusion.1.pot, f32[8,1024]{1,0:T(8,128)S(1)} %get-tuple-element.21.base, f32[1024,128]{1,0:T(8,128)S(1)} %copy-done.3, ...), custom_call_target="tpu_custom_call" | custom-call | flops 20971520 | bytes 3145728 | tf_op jit(solution)/shard_map/later_step/pallas_call | solution.py:361
  271.9 24.4 %collective-permute-start.17 = (f32[8,1024]{1,0:T(8,128)S(1)}, f32[8,1024]{1,0:T(8,128)S(1)}, u32[]{:S(2)}, u32[]{:S(2)}) collective-permute-start(f32[8,1024]{1,0:T(8,128)S(1)} %get-tuple-element.30), channel_id=1, source_target_pairs={{752,0},{744,8},{32,16},{760,24},{16,32},{72,40},{64,48},{88,56},{... | collective-permute-start | bytes 98312 | tf_op jit(solution)/shard_map/ppermute | solution.py:26
  296.4 2.7 collective-permute-start.18
  299.1 2.8 collective-permute-done.18
  305.6 3.9 %plan_gradients.1 = (f32[128,256]{1,0:T(8,128)}, f32[128,256]{1,0:T(8,128)}) custom-call(s32[1,5]{1,0:T(1,128)S(1)} %copy-done.14, f32[5,1024]{1,0:T(8,128)S(1)} %fusion.2.pot, f32[1024,128]{1,0:T(8,128)S(1)} %get-tuple-element.25.dual, f32[5,2,1024]{2,1,0:T(2,128)S(1)} %broadcast_select_fusion.2.around, bf16[128,256]{1,0:T(8,128)(2,1)S(1)} %copy-done.10, ...), custom_call_target="tpu_custom_call" | custom-call | flops 1342177280 | bytes 5242880 | tf_op jit(solution)/shard_map/plan_gradients/pallas_call | solution.py:421
  (100 shorter events, 33.5 us)
Async XLA Ops:
  21.2 32.1 %collective-permute-start.2 = (bf16[1024,256]{1,0:T(8,128)(2,1)S(1)}, bf16[1024,256]{1,0:T(8,128)(2,1)S(1)}, u32[]{:S(2)}, u32[]{:S(2)}) collective-permute-start(bf16[1024,256]{1,0:T(8,128)(2,1)S(1)} %bitcast.36), channel_id=1, source_target_pairs={{752,0},{760,8},{0,16},{8,24},{16,32},{24,40},{32,48},{40,56},{48,... | collective-permute-start | bytes 1572872 | tf_op jit(solution)/shard_map/ppermute | solution.py:26
  28.9 24.3 %collective-permute-start.1 = (bf16[1024,256]{1,0:T(8,128)(2,1)S(1)}, bf16[1024,256]{1,0:T(8,128)(2,1)S(1)}, u32[]{:S(2)}, u32[]{:S(2)}) collective-permute-start(bf16[1024,256]{1,0:T(8,128)(2,1)S(1)} %bitcast.37), channel_id=1, source_target_pairs={{16,0},{24,8},{32,16},{40,24},{48,32},{56,40},{64,48},{72,56},{80,... | collective-permute-start | bytes 1572872 | tf_op jit(solution)/shard_map/ppermute | solution.py:26
  45.1 18.1 %all-to-all-start = ((bf16[8,128,256]{2,1,0:T(8,128)(2,1)}), bf16[8,128,256]{2,1,0:T(8,128)(2,1)S(1)}, u32[]{:S(2)}, u32[]{:S(2)}) async-start(bf16[8,128,256]{2,1,0:T(8,128)(2,1)} %broadcast_in_dim.4), calls=%async_computation | async-start | bytes 1048576 | tf_op jit(solution)/shard_map/all_to_all | solution.py:55
  48.6 28.9 %collective-permute-start = (bf16[1024,256]{1,0:T(8,128)(2,1)S(1)}, bf16[1024,256]{1,0:T(8,128)(2,1)S(1)}, u32[]{:S(2)}, u32[]{:S(2)}) collective-permute-start(bf16[1024,256]{1,0:T(8,128)(2,1)S(1)} %bitcast.38), channel_id=1, source_target_pairs={{8,0},{0,8},{24,16},{16,24},{40,32},{32,40},{56,48},{48,56},{72,64... | collective-permute-start | bytes 1572872 | tf_op jit(solution)/shard_map/ppermute | solution.py:26
  54.1 23.3 %collective-permute-start.3 = (bf16[1024,256]{1,0:T(8,128)(2,1)}, bf16[1024,256]{1,0:T(8,128)(2,1)S(1)}, u32[]{:S(2)}, u32[]{:S(2)}) collective-permute-start(bf16[1024,256]{1,0:T(8,128)(2,1)} %broadcast_select_fusion.1), channel_id=1, source_target_pairs={{8,0},{0,8},{24,16},{16,24},{40,32},{32,40},{56,48},{48,56},{72,64... | collective-permute-start | bytes 1572872 | tf_op jit(solution)/shard_map/ppermute | solution.py:26
  63.1 36.7 %collective-permute-start.6 = (bf16[1024,256]{1,0:T(8,128)(2,1)S(1)}, bf16[1024,256]{1,0:T(8,128)(2,1)S(1)}, u32[]{:S(2)}, u32[]{:S(2)}) collective-permute-start(bf16[1024,256]{1,0:T(8,128)(2,1)S(1)} %bitcast.43), channel_id=1, source_target_pairs={{8,0},{0,8},{24,16},{16,24},{40,32},{32,40},{56,48},{48,56},{72,64... | collective-permute-start | bytes 1572872 | tf_op jit(solution)/shard_map/ppermute | solution.py:26
  68.8 31.8 %collective-permute-start.5 = (bf16[1024,256]{1,0:T(8,128)(2,1)S(1)}, bf16[1024,256]{1,0:T(8,128)(2,1)S(1)}, u32[]{:S(2)}, u32[]{:S(2)}) collective-permute-start(bf16[1024,256]{1,0:T(8,128)(2,1)S(1)} %bitcast.44), channel_id=1, source_target_pairs={{752,0},{760,8},{0,16},{8,24},{16,32},{24,40},{32,48},{40,56},{48,... | collective-permute-start | bytes 1572872 | tf_op jit(solution)/shard_map/ppermute | solution.py:26
  70.8 29.9 %collective-permute-start.4 = (bf16[1024,256]{1,0:T(8,128)(2,1)S(1)}, bf16[1024,256]{1,0:T(8,128)(2,1)S(1)}, u32[]{:S(2)}, u32[]{:S(2)}) collective-permute-start(bf16[1024,256]{1,0:T(8,128)(2,1)S(1)} %bitcast.45), channel_id=1, source_target_pairs={{16,0},{24,8},{32,16},{40,24},{48,32},{56,40},{64,48},{72,56},{80,... | collective-permute-start | bytes 1572872 | tf_op jit(solution)/shard_map/ppermute | solution.py:26
  102.3 3.3 %collective-permute-start.7 = (f32[6,1024]{1,0:T(8,128)S(1)}, f32[6,1024]{1,0:T(8,128)S(1)}, u32[]{:S(2)}, u32[]{:S(2)}) collective-permute-start(f32[6,1024]{1,0:T(8,128)S(1)} %bitcast.50), channel_id=1, source_target_pairs={{8,0},{0,8},{24,16},{16,24},{40,32},{32,40},{56,48},{48,56},{72,64... | collective-permute-start | bytes 73736 | tf_op jit(solution)/shard_map/ppermute | solution.py:26
  105.6 22.7 %collective-permute-start.8 = (f32[4,1024]{1,0:T(4,128)S(1)}, f32[4,1024]{1,0:T(4,128)S(1)}, u32[]{:S(2)}, u32[]{:S(2)}) collective-permute-start(f32[4,1024]{1,0:T(4,128)S(1)} %get-tuple-element.72), channel_id=1, source_target_pairs={{752,0},{744,8},{32,16},{760,24},{16,32},{72,40},{64,48},{88,56},{... | collective-permute-start | bytes 49160 | tf_op jit(solution)/shard_map/ppermute | solution.py:26
  126.3 5.4 %collective-permute-start.9 = (f32[4,1024]{1,0:T(4,128)S(1)}, f32[4,1024]{1,0:T(4,128)S(1)}, u32[]{:S(2)}, u32[]{:S(2)}) collective-permute-start(f32[4,1024]{1,0:T(4,128)S(1)} %get-tuple-element.73), channel_id=1, source_target_pairs={{16,0},{40,8},{0,16},{56,24},{48,32},{8,40},{32,48},{24,56},{80,64... | collective-permute-start | bytes 49160 | tf_op jit(solution)/shard_map/ppermute | solution.py:26
  131.8 5.4 %collective-permute-start.10 = (f32[6,1024]{1,0:T(8,128)S(1)}, f32[6,1024]{1,0:T(8,128)S(1)}, u32[]{:S(2)}, u32[]{:S(2)}) collective-permute-start(f32[6,1024]{1,0:T(8,128)S(1)} %maximum_select_fusion), channel_id=1, source_target_pairs={{8,0},{0,8},{24,16},{16,24},{40,32},{32,40},{56,48},{48,56},{72,64... | collective-permute-start | bytes 73736 | tf_op jit(solution)/shard_map/ppermute | solution.py:26
  134.8 3.9 %collective-permute-start.11 = (bf16[1024,256]{1,0:T(8,128)(2,1)S(1)}, bf16[1024,256]{1,0:T(8,128)(2,1)S(1)}, u32[]{:S(2)}, u32[]{:S(2)}) collective-permute-start(bf16[1024,256]{1,0:T(8,128)(2,1)S(1)} %broadcast_select_fusion), channel_id=1, source_target_pairs={{8,0},{0,8},{24,16},{16,24},{40,32},{32,40},{56,48},{48,56},{72,64... | collective-permute-start | bytes 1572872 | tf_op jit(solution)/shard_map/ppermute | solution.py:26
  147.4 158.1 %copy-start.10 = (bf16[128,256]{1,0:T(8,128)(2,1)S(1)}, bf16[128,256]{1,0:T(8,128)(2,1)}, u32[]{:S(2)}) copy-start(bf16[128,256]{1,0:T(8,128)(2,1)} %mine.1) | copy-start | bytes 196612
  147.4 158.1 %copy-start.11 = (bf16[128,256]{1,0:T(8,128)(2,1)S(1)}, bf16[128,256]{1,0:T(8,128)(2,1)}, u32[]{:S(2)}) copy-start(bf16[128,256]{1,0:T(8,128)(2,1)} %own.1) | copy-start | bytes 196612
  147.4 158.1 %copy-start.14 = (s32[1,5]{1,0:T(1,128)S(1)}, s32[1,5]{1,0:T(1,128)}, u32[]{:S(2)}) copy-start(s32[1,5]{1,0:T(1,128)} %mask.7) | copy-start | bytes 64
  190.4 3.1 %collective-permute-start.12 = (f32[6,1024]{1,0:T(8,128)S(1)}, f32[6,1024]{1,0:T(8,128)S(1)}, u32[]{:S(2)}, u32[]{:S(2)}) collective-permute-start(f32[6,1024]{1,0:T(8,128)S(1)} %bitcast.51), channel_id=1, source_target_pairs={{8,0},{0,8},{24,16},{16,24},{40,32},{32,40},{56,48},{48,56},{72,64... | collective-permute-start | bytes 73736 | tf_op jit(solution)/shard_map/ppermute | solution.py:26
  193.6 26.3 %collective-permute-start.13 = (f32[4,1024]{1,0:T(4,128)S(1)}, f32[4,1024]{1,0:T(4,128)S(1)}, u32[]{:S(2)}, u32[]{:S(2)}) collective-permute-start(f32[4,1024]{1,0:T(4,128)S(1)} %get-tuple-element.61), channel_id=1, source_target_pairs={{752,0},{744,8},{32,16},{760,24},{16,32},{72,40},{64,48},{88,56},{... | collective-permute-start | bytes 49160 | tf_op jit(solution)/shard_map/ppermute | solution.py:26
  218.0 5.4 %collective-permute-start.14 = (f32[4,1024]{1,0:T(4,128)S(1)}, f32[4,1024]{1,0:T(4,128)S(1)}, u32[]{:S(2)}, u32[]{:S(2)}) collective-permute-start(f32[4,1024]{1,0:T(4,128)S(1)} %get-tuple-element.62), channel_id=1, source_target_pairs={{16,0},{40,8},{0,16},{56,24},{48,32},{8,40},{32,48},{24,56},{80,64... | collective-permute-start | bytes 49160 | tf_op jit(solution)/shard_map/ppermute | solution.py:26
  223.5 3.1 collective-permute-start.15
  268.7 3.1 %collective-permute-start.16 = (f32[8,1024]{1,0:T(8,128)S(1)}, f32[8,1024]{1,0:T(8,128)S(1)}, u32[]{:S(2)}, u32[]{:S(2)}) collective-permute-start(f32[8,1024]{1,0:T(8,128)S(1)} %get-tuple-element.24), channel_id=1, source_target_pairs={{8,0},{0,8},{24,16},{16,24},{40,32},{32,40},{56,48},{48,56},{72,64... | collective-permute-start | bytes 98312 | tf_op jit(solution)/shard_map/ppermute | solution.py:26
  271.9 27.1 %collective-permute-start.17 = (f32[8,1024]{1,0:T(8,128)S(1)}, f32[8,1024]{1,0:T(8,128)S(1)}, u32[]{:S(2)}, u32[]{:S(2)}) collective-permute-start(f32[8,1024]{1,0:T(8,128)S(1)} %get-tuple-element.30), channel_id=1, source_target_pairs={{752,0},{744,8},{32,16},{760,24},{16,32},{72,40},{64,48},{88,56},{... | collective-permute-start | bytes 98312 | tf_op jit(solution)/shard_map/ppermute | solution.py:26
  296.4 5.6 %collective-permute-start.18 = (f32[8,1024]{1,0:T(8,128)S(1)}, f32[8,1024]{1,0:T(8,128)S(1)}, u32[]{:S(2)}, u32[]{:S(2)}) collective-permute-start(f32[8,1024]{1,0:T(8,128)S(1)} %get-tuple-element.31), channel_id=1, source_target_pairs={{16,0},{40,8},{0,16},{56,24},{48,32},{8,40},{32,48},{24,56},{80,64... | collective-permute-start | bytes 98312 | tf_op jit(solution)/shard_map/ppermute | solution.py:26
  302.1 3.1 %collective-permute-start.19 = (f32[14,1024]{1,0:T(8,128)S(1)}, f32[14,1024]{1,0:T(8,128)S(1)}, u32[]{:S(2)}, u32[]{:S(2)}) collective-permute-start(f32[14,1024]{1,0:T(8,128)S(1)} %pad_maximum_fusion), channel_id=1, source_target_pairs={{8,0},{0,8},{24,16},{16,24},{40,32},{32,40},{56,48},{48,56},{72,64... | collective-permute-start | bytes 172040 | tf_op jit(solution)/shard_map/ppermute | solution.py:26
  (12 other events, 493.9 us)

commit v4 on v3

--- a/solution.py
+++ b/solution.py
@@ -8,7 +8,6 @@
 from jax.experimental.pallas import tpu as pltpu
 from jax.sharding import PartitionSpec as P
 
-ITERS = 3
 EPS = 0.1
 NEG = -1e30
 KAPPA = 1.0 / (EPS * math.log(2.0))
@@ -60,12 +59,12 @@
     return top + jnp.log2(jnp.exp2(a - top) + jnp.exp2(b - top))
 
 
-def column_totals(partial, row, extra=False):
-    even = row % 2 == 0
-    up = (row // 2) // (1 + row % 2) % 2 == 0
+def column_totals(partial, even, up, extra=False, cargo=None, movers=(), late=False):
     count = 2 if extra else 0
     other = swap_mate(partial[: 6 + count])
     chip = lse2(partial[:6], other[:6])
+    if movers:
+        chip, cargo = lax.optimization_barrier((chip, cargo))
     to_above, to_below = chip[2:6], chip[0:4]
     if count:
         mine = partial[6:8]
@@ -87,6 +86,10 @@
     sent = jnp.concatenate([outer, below[4:], above[4:]]) if count else outer
     got = swap_mate(sent)
     total = lse2(chip, lse2(outer, got[:6]))
+    if movers:
+        moved = [move(*cargo) for move in movers]
+        if not late:
+            total, moved = lax.optimization_barrier((total, moved))
 
     def placed(rows):
         return jnp.where(
@@ -95,6 +98,8 @@
             jnp.stack([rows[3], rows[2], rows[4], rows[5], rows[1]]),
         )
 
+    if movers:
+        return placed(total), moved
     if not count:
         return placed(total)
     near = jnp.where(even, sent[6:], got[6:])
@@ -442,22 +447,26 @@
 def shards(source, target, pair_mask):
     row = lax.axis_index("row")
     even = row % 2 == 0
+    up = (row // 2) // (1 + row % 2) % 2 == 0
     targets = neighbours(gathered(target), even)
     rows = gathered(source)
+    rows, even, up = lax.optimization_barrier((rows, even, up))
     entries, partial, top, base = first_step(pair_mask, rows, targets)
-    above = shifted(rows, -2)
-    below = shifted(rows, 2)
-    mate = swap_mate(rows)
-    partial, above, below, mate = lax.optimization_barrier((partial, above, below, mate))
-    cross = swap_mate(jnp.where(even, above, below))
-    pot = -column_totals(partial, row)
-    pot, cross = lax.optimization_barrier((pot, cross))
+    total, (above, below) = column_totals(
+        partial, even, up, False, (rows,), (lambda x: shifted(x, -2), lambda x: shifted(x, 2)), True
+    )
+    partial, dual = later_step(pair_mask, entries, -total, base, top, rows, targets)
+    total, (mate, cross) = column_totals(
+        partial,
+        even,
+        up,
+        False,
+        (rows, above, below),
+        (lambda x, a, b: swap_mate(x), lambda x, a, b: swap_mate(jnp.where(even, a, b))),
+    )
+    partial, dual = later_step(pair_mask, entries, -total, base, top, rows, targets)
+    total, around = column_totals(partial, even, up, True)
     sources = (rows, mate, cross, above, below)
-    for _ in range(ITERS - 2):
-        partial, dual = later_step(pair_mask, entries, pot, base, top, rows, targets)
-        pot = -column_totals(partial, row)
-    partial, dual = later_step(pair_mask, entries, pot, base, top, rows, targets)
-    total, around = column_totals(partial, row, True)
     return gradients(pair_mask, -total, dual, around, source, target, targets, sources)
 
 

time: 311 us -> 292 us (0.939)
  local copies, waits for them, and re-layouts: 22.3 us -> 3.48 us
    unnamed x35 -> x11, local copies, waits for them, and re-layouts: 19.6 us -> 0.73 us
  transfers between devices with their start and end apart: 21 -> 21, of which waited for: 10 -> 9; matrix products, arithmetic and copies ran while one was open for 1% -> 1% of each run, Pallas kernels for 4% -> 15%
where the time goes in v4:
time: 292 us; the launch traced here: 291 us
  starting transfers between devices  141 us (48%)
  Pallas kernels  105 us (36%)
  blocking collectives  19.7 us (7%)
  waiting for transfers between devices  18.9 us (6%)
  local copies, waits for them, and re-layouts  3.48 us (1%)
    ppermute x20, starting transfers between devices, from_row(): return lax.ppermute(block, 'row', [(source_of(i), i) for i in range(count)])  137 us
    pallas_call x2, Pallas kernels, later_step(): pl.pallas_call(later_kernel, out_shape=(row, column), in_specs=[SMEM] + [...  86.7 us
    all_to_all x1, blocking collectives, gathered(): lax.all_to_all(copies, 'grp', 0, 0, tiled=True).reshape(-1, shard.shape[1])  19.7 us
    pallas_call x1, Pallas kernels, first_step(): pl.pallas_call(first_kernel, out_shape=(pltpu.VMEM((count, WINDOW * count...  14.2 us
    ppermute x20, waiting for transfers between devices, from_row(): return lax.ppermute(block, 'row', [(source_of(i), i) for i in range(count)])  14.1 us
  transfers between devices with their start and end apart: 21, of which 9 were waited for; matrix products, arithmetic and copies ran while one was open for 1% of the time, Pallas kernels for 15%

profile of v4, /device:TPU:1, one launch (start us, length us, event | category | flops | bytes accessed | tf_op | source)
XLA Modules:
  0.0 290.8 jit_solution(10219989587158562823)
XLA Ops:
  1.5 19.7 %all_to_all.10 = bf16[8,128,256]{2,1,0:T(8,128)(2,1)S(1)} all-to-all(bf16[8,128,256]{2,1,0:T(8,128)(2,1)S(1)} %broadcast_in_dim.5), channel_id=1, replica_groups=mesh['row'=96,'grp'=8] {'grp'}, dimensions={0} | all-to-all | bytes 1048576 | tf_op jit(solution)/shard_map/all_to_all | solution.py:54
  21.2 7.8 %collective-permute-start.2 = (bf16[1024,256]{1,0:T(8,128)(2,1)S(1)}, bf16[1024,256]{1,0:T(8,128)(2,1)S(1)}, u32[]{:S(2)}, u32[]{:S(2)}) collective-permute-start(bf16[1024,256]{1,0:T(8,128)(2,1)S(1)} %bitcast.36), channel_id=1, source_target_pairs={{752,0},{760,8},{0,16},{8,24},{16,32},{24,40},{32,48},{40,56},{48,... | collective-permute-start | bytes 1572872 | tf_op jit(solution)/shard_map/ppermute | solution.py:25
  28.9 14.4 %collective-permute-start.1 = (bf16[1024,256]{1,0:T(8,128)(2,1)S(1)}, bf16[1024,256]{1,0:T(8,128)(2,1)S(1)}, u32[]{:S(2)}, u32[]{:S(2)}) collective-permute-start(bf16[1024,256]{1,0:T(8,128)(2,1)S(1)} %bitcast.37), channel_id=1, source_target_pairs={{16,0},{24,8},{32,16},{40,24},{48,32},{56,40},{64,48},{72,56},{80,... | collective-permute-start | bytes 1572872 | tf_op jit(solution)/shard_map/ppermute | solution.py:25
  45.0 3.5 %all-to-all-start = ((bf16[8,128,256]{2,1,0:T(8,128)(2,1)}), bf16[8,128,256]{2,1,0:T(8,128)(2,1)S(1)}, u32[]{:S(2)}, u32[]{:S(2)}) async-start(bf16[8,128,256]{2,1,0:T(8,128)(2,1)} %broadcast_in_dim.4), calls=%async_computation | async-start | bytes 1048576 | tf_op jit(solution)/shard_map/all_to_all | solution.py:54
  48.6 4.6 %collective-permute-start = (bf16[1024,256]{1,0:T(8,128)(2,1)S(1)}, bf16[1024,256]{1,0:T(8,128)(2,1)S(1)}, u32[]{:S(2)}, u32[]{:S(2)}) collective-permute-start(bf16[1024,256]{1,0:T(8,128)(2,1)S(1)} %bitcast.38), channel_id=1, source_target_pairs={{8,0},{0,8},{24,16},{16,24},{40,32},{32,40},{56,48},{48,56},{72,64... | collective-permute-start | bytes 1572872 | tf_op jit(solution)/shard_map/ppermute | solution.py:25
  54.1 4.1 %collective-permute-start.3 = (bf16[1024,256]{1,0:T(8,128)(2,1)}, bf16[1024,256]{1,0:T(8,128)(2,1)S(1)}, u32[]{:S(2)}, u32[]{:S(2)}) collective-permute-start(bf16[1024,256]{1,0:T(8,128)(2,1)} %broadcast_select_fusion.1), channel_id=1, source_target_pairs={{8,0},{0,8},{24,16},{16,24},{40,32},{32,40},{56,48},{48,56},{72,64... | collective-permute-start | bytes 1572872 | tf_op jit(solution)/shard_map/ppermute | solution.py:25
  58.3 4.8 %all-to-all-done = bf16[8,128,256]{2,1,0:T(8,128)(2,1)S(1)} async-done(((bf16[8,128,256]{2,1,0:T(8,128)(2,1)}), bf16[8,128,256]{2,1,0:T(8,128)(2,1)S(1)}, u32[]{:S(2)}, u32[]{:S(2)}) %all-to-all-start) | async-done | bytes 524320 | tf_op jit(solution)/shard_map/all_to_all | solution.py:54
  63.8 14.2 %first_step.1 = (f32[1024,5120]{1,0:T(8,128)S(1)}, f32[8,1024]{1,0:T(8,128)S(1)}, f32[1024,128]{1,0:T(8,128)S(1)}, f32[8,1024]{1,0:T(8,128)S(1)}) custom-call(s32[1,5]{1,0:T(1,128)S(1)} %copy-done.2, bf16[1024,256]{1,0:T(8,128)(2,1)S(1)} %bitcast.43, bf16[1024,256]{1,0:T(8,128)(2,1)S(1)} %bitcast.39, bf16[1024,256]{1,0:T(8,128)(2,1)S(1)} %collective-permute-done.t1, ...), custom_call_target="tpu_custom_call" | custom-call | flops 2684354560 | bytes 3145728 | tf_op jit(solution)/shard_map/first_step/pallas_call | solution.py:342
  78.0 26.5 %collective-permute-start.4 = (f32[6,1024]{1,0:T(8,128)S(1)}, f32[6,1024]{1,0:T(8,128)S(1)}, u32[]{:S(2)}, u32[]{:S(2)}) collective-permute-start(f32[6,1024]{1,0:T(8,128)S(1)} %bitcast.50), channel_id=1, source_target_pairs={{8,0},{0,8},{24,16},{16,24},{40,32},{32,40},{56,48},{48,56},{72,64... | collective-permute-start | bytes 73736 | tf_op jit(solution)/shard_map/ppermute | solution.py:25
  105.4 1.9 collective-permute-start.5
  109.3 4.8 %collective-permute-done.5 = f32[4,1024]{1,0:T(4,128)S(1)} collective-permute-done((f32[4,1024]{1,0:T(4,128)S(1)}, f32[4,1024]{1,0:T(4,128)S(1)}, u32[]{:S(2)}, u32[]{:S(2)}) %collective-permute-start.5) | collective-permute-done | bytes 16416 | tf_op jit(solution)/shard_map/ppermute | solution.py:25
  114.3 2.4 collective-permute-start.7
  118.7 6.7 %collective-permute-start.9 = (bf16[1024,256]{1,0:T(8,128)(2,1)S(1)}, bf16[1024,256]{1,0:T(8,128)(2,1)S(1)}, u32[]{:S(2)}, u32[]{:S(2)}) collective-permute-start(bf16[1024,256]{1,0:T(8,128)(2,1)S(1)} %bitcast.45), channel_id=1, source_target_pairs={{16,0},{24,8},{32,16},{40,24},{48,32},{56,40},{64,48},{72,56},{80,... | collective-permute-start | bytes 1572872 | tf_op jit(solution)/shard_map/ppermute | solution.py:25
  125.5 43.8 %later_step.2 = (f32[8,1024]{1,0:T(8,128)S(1)}, f32[1024,128]{1,0:T(8,128)}) custom-call(s32[1,5]{1,0:T(1,128)S(1)} %copy-done.2, f32[1024,5120]{1,0:T(8,128)S(1)} %get-tuple-element.23.entries, f32[5,1024]{1,0:T(8,128)S(1)} %fusion.pot, f32[8,1024]{1,0:T(8,128)S(1)} %get-tuple-element.27.base, f32[1024,128]{1,0:T(8,128)S(1)} %get-tuple-element.28.top, ...), custom_call_target="tpu_custom_call" | custom-call | flops 20971520 | bytes 3145728 | tf_op jit(solution)/shard_map/later_step/pallas_call | solution.py:366
  169.4 23.6 %collective-permute-start.8 = (f32[6,1024]{1,0:T(8,128)S(1)}, f32[6,1024]{1,0:T(8,128)S(1)}, u32[]{:S(2)}, u32[]{:S(2)}) collective-permute-start(f32[6,1024]{1,0:T(8,128)S(1)} %bitcast.51), channel_id=1, source_target_pairs={{8,0},{0,8},{24,16},{16,24},{40,32},{32,40},{56,48},{48,56},{72,64... | collective-permute-start | bytes 73736 | tf_op jit(solution)/shard_map/ppermute | solution.py:25
  197.8 2.3 collective-permute-start.15
  200.0 2.1 collective-permute-start.14
  202.8 2.4 collective-permute-start.13
  206.2 42.9 %later_step.3 = (f32[8,1024]{1,0:T(8,128)S(1)}, f32[1024,128]{1,0:T(8,128)S(1)}) custom-call(s32[1,5]{1,0:T(1,128)S(1)} %copy-done.2, f32[1024,5120]{1,0:T(8,128)S(1)} %get-tuple-element.23.entries, f32[5,1024]{1,0:T(8,128)S(1)} %fusion.1.pot, f32[8,1024]{1,0:T(8,128)S(1)} %get-tuple-element.27.base, f32[1024,128]{1,0:T(8,128)S(1)} %get-tuple-element.28.top, ...), custom_call_target="tpu_custom_call" | custom-call | flops 20971520 | bytes 3145728 | tf_op jit(solution)/shard_map/later_step/pallas_call | solution.py:366
  249.0 23.5 %collective-permute-start.16 = (f32[8,1024]{1,0:T(8,128)S(1)}, f32[8,1024]{1,0:T(8,128)S(1)}, u32[]{:S(2)}, u32[]{:S(2)}) collective-permute-start(f32[8,1024]{1,0:T(8,128)S(1)} %get-tuple-element.36), channel_id=1, source_target_pairs={{8,0},{0,8},{24,16},{16,24},{40,32},{32,40},{56,48},{48,56},{72,64... | collective-permute-start | bytes 98312 | tf_op jit(solution)/shard_map/ppermute | solution.py:25
  273.5 2.5 collective-permute-start.17
  277.9 4.5 %collective-permute-done.17 = f32[8,1024]{1,0:T(8,128)S(1)} collective-permute-done((f32[8,1024]{1,0:T(8,128)S(1)}, f32[8,1024]{1,0:T(8,128)S(1)}, u32[]{:S(2)}, u32[]{:S(2)}) %collective-permute-start.17) | collective-permute-done | bytes 32800 | tf_op jit(solution)/shard_map/ppermute | solution.py:25
  282.7 3.1 %collective-permute-start.19 = (f32[14,1024]{1,0:T(8,128)S(1)}, f32[14,1024]{1,0:T(8,128)S(1)}, u32[]{:S(2)}, u32[]{:S(2)}) collective-permute-start(f32[14,1024]{1,0:T(8,128)S(1)} %pad_maximum_fusion), channel_id=1, source_target_pairs={{8,0},{0,8},{24,16},{16,24},{40,32},{32,40},{56,48},{48,56},{72,64... | collective-permute-start | bytes 172040 | tf_op jit(solution)/shard_map/ppermute | solution.py:25
  286.9 3.9 %plan_gradients.1 = (f32[128,256]{1,0:T(8,128)}, f32[128,256]{1,0:T(8,128)}) custom-call(s32[1,5]{1,0:T(1,128)S(1)} %copy-done.2, f32[5,1024]{1,0:T(8,128)S(1)} %fusion.2.pot, f32[1024,128]{1,0:T(8,128)S(1)} %get-tuple-element.37.dual, f32[5,2,1024]{2,1,0:T(2,128)S(1)} %broadcast_select_fusion.2.around, bf16[128,256]{1,0:T(8,128)(2,1)S(1)} %copy-done, ...), custom_call_target="tpu_custom_call" | custom-call | flops 1342177280 | bytes 5242880 | tf_op jit(solution)/shard_map/plan_gradients/pallas_call | solution.py:426
  (76 shorter events, 19.7 us)
Async XLA Ops:
  21.2 32.1 %collective-permute-start.2 = (bf16[1024,256]{1,0:T(8,128)(2,1)S(1)}, bf16[1024,256]{1,0:T(8,128)(2,1)S(1)}, u32[]{:S(2)}, u32[]{:S(2)}) collective-permute-start(bf16[1024,256]{1,0:T(8,128)(2,1)S(1)} %bitcast.36), channel_id=1, source_target_pairs={{752,0},{760,8},{0,16},{8,24},{16,32},{24,40},{32,48},{40,56},{48,... | collective-permute-start | bytes 1572872 | tf_op jit(solution)/shard_map/ppermute | solution.py:25
  28.9 24.3 %collective-permute-start.1 = (bf16[1024,256]{1,0:T(8,128)(2,1)S(1)}, bf16[1024,256]{1,0:T(8,128)(2,1)S(1)}, u32[]{:S(2)}, u32[]{:S(2)}) collective-permute-start(bf16[1024,256]{1,0:T(8,128)(2,1)S(1)} %bitcast.37), channel_id=1, source_target_pairs={{16,0},{24,8},{32,16},{40,24},{48,32},{56,40},{64,48},{72,56},{80,... | collective-permute-start | bytes 1572872 | tf_op jit(solution)/shard_map/ppermute | solution.py:25
  45.0 18.1 %all-to-all-start = ((bf16[8,128,256]{2,1,0:T(8,128)(2,1)}), bf16[8,128,256]{2,1,0:T(8,128)(2,1)S(1)}, u32[]{:S(2)}, u32[]{:S(2)}) async-start(bf16[8,128,256]{2,1,0:T(8,128)(2,1)} %broadcast_in_dim.4), calls=%async_computation | async-start | bytes 1048576 | tf_op jit(solution)/shard_map/all_to_all | solution.py:54
  48.6 14.6 %collective-permute-start = (bf16[1024,256]{1,0:T(8,128)(2,1)S(1)}, bf16[1024,256]{1,0:T(8,128)(2,1)S(1)}, u32[]{:S(2)}, u32[]{:S(2)}) collective-permute-start(bf16[1024,256]{1,0:T(8,128)(2,1)S(1)} %bitcast.38), channel_id=1, source_target_pairs={{8,0},{0,8},{24,16},{16,24},{40,32},{32,40},{56,48},{48,56},{72,64... | collective-permute-start | bytes 1572872 | tf_op jit(solution)/shard_map/ppermute | solution.py:25
  54.1 9.0 %collective-permute-start.3 = (bf16[1024,256]{1,0:T(8,128)(2,1)}, bf16[1024,256]{1,0:T(8,128)(2,1)S(1)}, u32[]{:S(2)}, u32[]{:S(2)}) collective-permute-start(bf16[1024,256]{1,0:T(8,128)(2,1)} %broadcast_select_fusion.1), channel_id=1, source_target_pairs={{8,0},{0,8},{24,16},{16,24},{40,32},{32,40},{56,48},{48,56},{72,64... | collective-permute-start | bytes 1572872 | tf_op jit(solution)/shard_map/ppermute | solution.py:25
  63.1 0.7 copy-start.2
  78.0 27.4 %collective-permute-start.4 = (f32[6,1024]{1,0:T(8,128)S(1)}, f32[6,1024]{1,0:T(8,128)S(1)}, u32[]{:S(2)}, u32[]{:S(2)}) collective-permute-start(f32[6,1024]{1,0:T(8,128)S(1)} %bitcast.50), channel_id=1, source_target_pairs={{8,0},{0,8},{24,16},{16,24},{40,32},{32,40},{56,48},{48,56},{72,64... | collective-permute-start | bytes 73736 | tf_op jit(solution)/shard_map/ppermute | solution.py:25
  105.4 8.8 %collective-permute-start.5 = (f32[4,1024]{1,0:T(4,128)S(1)}, f32[4,1024]{1,0:T(4,128)S(1)}, u32[]{:S(2)}, u32[]{:S(2)}) collective-permute-start(f32[4,1024]{1,0:T(4,128)S(1)} %get-tuple-element.84), channel_id=1, source_target_pairs={{752,0},{744,8},{32,16},{760,24},{16,32},{72,40},{64,48},{88,56},{... | collective-permute-start | bytes 49160 | tf_op jit(solution)/shard_map/ppermute | solution.py:25
  107.3 6.9 %collective-permute-start.6 = (f32[4,1024]{1,0:T(4,128)S(1)}, f32[4,1024]{1,0:T(4,128)S(1)}, u32[]{:S(2)}, u32[]{:S(2)}) collective-permute-start(f32[4,1024]{1,0:T(4,128)S(1)} %get-tuple-element.85), channel_id=1, source_target_pairs={{16,0},{40,8},{0,16},{56,24},{48,32},{8,40},{32,48},{24,56},{80,64... | collective-permute-start | bytes 49160 | tf_op jit(solution)/shard_map/ppermute | solution.py:25
  114.3 11.1 %collective-permute-start.7 = (f32[6,1024]{1,0:T(8,128)S(1)}, f32[6,1024]{1,0:T(8,128)S(1)}, u32[]{:S(2)}, u32[]{:S(2)}) collective-permute-start(f32[6,1024]{1,0:T(8,128)S(1)} %maximum_select_fusion), channel_id=1, source_target_pairs={{8,0},{0,8},{24,16},{16,24},{40,32},{32,40},{56,48},{48,56},{72,64... | collective-permute-start | bytes 73736 | tf_op jit(solution)/shard_map/ppermute | solution.py:25
  116.7 77.1 %collective-permute-start.10 = (bf16[1024,256]{1,0:T(8,128)(2,1)S(1)}, bf16[1024,256]{1,0:T(8,128)(2,1)S(1)}, u32[]{:S(2)}, u32[]{:S(2)}) collective-permute-start(bf16[1024,256]{1,0:T(8,128)(2,1)S(1)} %bitcast.44), channel_id=1, source_target_pairs={{752,0},{760,8},{0,16},{8,24},{16,32},{24,40},{32,48},{40,56},{48,... | collective-permute-start | bytes 1572872 | tf_op jit(solution)/shard_map/ppermute | solution.py:25
  118.7 75.1 %collective-permute-start.9 = (bf16[1024,256]{1,0:T(8,128)(2,1)S(1)}, bf16[1024,256]{1,0:T(8,128)(2,1)S(1)}, u32[]{:S(2)}, u32[]{:S(2)}) collective-permute-start(bf16[1024,256]{1,0:T(8,128)(2,1)S(1)} %bitcast.45), channel_id=1, source_target_pairs={{16,0},{24,8},{32,16},{40,24},{48,32},{56,40},{64,48},{72,56},{80,... | collective-permute-start | bytes 1572872 | tf_op jit(solution)/shard_map/ppermute | solution.py:25
  125.5 161.4 %copy-start = (bf16[128,256]{1,0:T(8,128)(2,1)S(1)}, bf16[128,256]{1,0:T(8,128)(2,1)}, u32[]{:S(2)}) copy-start(bf16[128,256]{1,0:T(8,128)(2,1)} %mine.1) | copy-start | bytes 196612
  125.5 161.4 %copy-start.1 = (bf16[128,256]{1,0:T(8,128)(2,1)S(1)}, bf16[128,256]{1,0:T(8,128)(2,1)}, u32[]{:S(2)}) copy-start(bf16[128,256]{1,0:T(8,128)(2,1)} %own.1) | copy-start | bytes 196612
  169.4 24.4 %collective-permute-start.8 = (f32[6,1024]{1,0:T(8,128)S(1)}, f32[6,1024]{1,0:T(8,128)S(1)}, u32[]{:S(2)}, u32[]{:S(2)}) collective-permute-start(f32[6,1024]{1,0:T(8,128)S(1)} %bitcast.51), channel_id=1, source_target_pairs={{8,0},{0,8},{24,16},{16,24},{40,32},{32,40},{56,48},{48,56},{72,64... | collective-permute-start | bytes 73736 | tf_op jit(solution)/shard_map/ppermute | solution.py:25
  193.8 8.8 %collective-permute-start.11 = (f32[4,1024]{1,0:T(4,128)S(1)}, f32[4,1024]{1,0:T(4,128)S(1)}, u32[]{:S(2)}, u32[]{:S(2)}) collective-permute-start(f32[4,1024]{1,0:T(4,128)S(1)} %get-tuple-element.73), channel_id=1, source_target_pairs={{752,0},{744,8},{32,16},{760,24},{16,32},{72,40},{64,48},{88,56},{... | collective-permute-start | bytes 49160 | tf_op jit(solution)/shard_map/ppermute | solution.py:25
  195.8 6.9 %collective-permute-start.12 = (f32[4,1024]{1,0:T(4,128)S(1)}, f32[4,1024]{1,0:T(4,128)S(1)}, u32[]{:S(2)}, u32[]{:S(2)}) collective-permute-start(f32[4,1024]{1,0:T(4,128)S(1)} %get-tuple-element.74), channel_id=1, source_target_pairs={{16,0},{40,8},{0,16},{56,24},{48,32},{8,40},{32,48},{24,56},{80,64... | collective-permute-start | bytes 49160 | tf_op jit(solution)/shard_map/ppermute | solution.py:25
  197.8 8.3 %collective-permute-start.15 = (bf16[1024,256]{1,0:T(8,128)(2,1)S(1)}, bf16[1024,256]{1,0:T(8,128)(2,1)S(1)}, u32[]{:S(2)}, u32[]{:S(2)}) collective-permute-start(bf16[1024,256]{1,0:T(8,128)(2,1)S(1)} %broadcast_select_fusion), channel_id=1, source_target_pairs={{8,0},{0,8},{24,16},{16,24},{40,32},{32,40},{56,48},{48,56},{72,64... | collective-permute-start | bytes 1572872 | tf_op jit(solution)/shard_map/ppermute | solution.py:25
  200.0 6.1 %collective-permute-start.14 = (bf16[1024,256]{1,0:T(8,128)(2,1)S(1)}, bf16[1024,256]{1,0:T(8,128)(2,1)S(1)}, u32[]{:S(2)}, u32[]{:S(2)}) collective-permute-start(bf16[1024,256]{1,0:T(8,128)(2,1)S(1)} %bitcast.47), channel_id=1, source_target_pairs={{8,0},{0,8},{24,16},{16,24},{40,32},{32,40},{56,48},{48,56},{72,64... | collective-permute-start | bytes 1572872 | tf_op jit(solution)/shard_map/ppermute | solution.py:25
  202.8 3.3 %collective-permute-start.13 = (f32[6,1024]{1,0:T(8,128)S(1)}, f32[6,1024]{1,0:T(8,128)S(1)}, u32[]{:S(2)}, u32[]{:S(2)}) collective-permute-start(f32[6,1024]{1,0:T(8,128)S(1)} %maximum_select_fusion.2), channel_id=1, source_target_pairs={{8,0},{0,8},{24,16},{16,24},{40,32},{32,40},{56,48},{48,56},{72,64... | collective-permute-start | bytes 73736 | tf_op jit(solution)/shard_map/ppermute | solution.py:25
  249.0 24.3 %collective-permute-start.16 = (f32[8,1024]{1,0:T(8,128)S(1)}, f32[8,1024]{1,0:T(8,128)S(1)}, u32[]{:S(2)}, u32[]{:S(2)}) collective-permute-start(f32[8,1024]{1,0:T(8,128)S(1)} %get-tuple-element.36), channel_id=1, source_target_pairs={{8,0},{0,8},{24,16},{16,24},{40,32},{32,40},{56,48},{48,56},{72,64... | collective-permute-start | bytes 98312 | tf_op jit(solution)/shard_map/ppermute | solution.py:25
  273.5 9.0 %collective-permute-start.17 = (f32[8,1024]{1,0:T(8,128)S(1)}, f32[8,1024]{1,0:T(8,128)S(1)}, u32[]{:S(2)}, u32[]{:S(2)}) collective-permute-start(f32[8,1024]{1,0:T(8,128)S(1)} %get-tuple-element.42), channel_id=1, source_target_pairs={{752,0},{744,8},{32,16},{760,24},{16,32},{72,40},{64,48},{88,56},{... | collective-permute-start | bytes 98312 | tf_op jit(solution)/shard_map/ppermute | solution.py:25
  276.0 6.5 %collective-permute-start.18 = (f32[8,1024]{1,0:T(8,128)S(1)}, f32[8,1024]{1,0:T(8,128)S(1)}, u32[]{:S(2)}, u32[]{:S(2)}) collective-permute-start(f32[8,1024]{1,0:T(8,128)S(1)} %get-tuple-element.43), channel_id=1, source_target_pairs={{16,0},{40,8},{0,16},{56,24},{48,32},{8,40},{32,48},{24,56},{80,64... | collective-permute-start | bytes 98312 | tf_op jit(solution)/shard_map/ppermute | solution.py:25
  282.7 4.0 %collective-permute-start.19 = (f32[14,1024]{1,0:T(8,128)S(1)}, f32[14,1024]{1,0:T(8,128)S(1)}, u32[]{:S(2)}, u32[]{:S(2)}) collective-permute-start(f32[14,1024]{1,0:T(8,128)S(1)} %pad_maximum_fusion), channel_id=1, source_target_pairs={{8,0},{0,8},{24,16},{16,24},{40,32},{32,40},{56,48},{48,56},{72,64... | collective-permute-start | bytes 172040 | tf_op jit(solution)/shard_map/ppermute | solution.py:25

commit v5 on v4

--- a/solution.py
+++ b/solution.py
@@ -14,6 +14,7 @@
 TWO_KAPPA = 2.0 * KAPPA
 SAFE_SUM = 2.0 ** -60
 SAFE_ROW = 2.0 ** -28
+HIGH_ROW = 2.0 ** 60
 SAFE_SHIFT = 60.0
 SCOPED = 16 * 1024 * 1024
 LANES = 128
@@ -59,7 +60,7 @@
     return top + jnp.log2(jnp.exp2(a - top) + jnp.exp2(b - top))
 
 
-def column_totals(partial, even, up, extra=False, cargo=None, movers=(), late=False):
+def column_totals(partial, even, up, extra=False, cargo=None, movers=()):
     count = 2 if extra else 0
     other = swap_mate(partial[: 6 + count])
     chip = lse2(partial[:6], other[:6])
@@ -88,8 +89,7 @@
     total = lse2(chip, lse2(outer, got[:6]))
     if movers:
         moved = [move(*cargo) for move in movers]
-        if not late:
-            total, moved = lax.optimization_barrier((total, moved))
+        total, moved = lax.optimization_barrier((total, moved))
 
     def placed(rows):
         return jnp.where(
@@ -165,17 +165,54 @@
             sums_out[place(p), :] = exact_columns(*fetch(p), dual)
 
 
+def note_range(good, total):
+    inside = jnp.logical_and(total >= SAFE_ROW, total <= HIGH_ROW)
+    good[...] = jnp.minimum(good[...], jnp.where(inside, 1.0, 0.0))
+
+
+def put_exact_rows(mask, fetch, bias, dual, total):
+    count = dual.shape[0]
+
+    def value(block, p, here):
+        rows, target = block
+        shift = jnp.where(is_listed(mask, p), bias[p : p + 1, :], NEG)
+        return dot_nt(rows[here, :], target[...]) * TWO_KAPPA + shift
+
+    dual[...] = jnp.full(dual.shape, NEG, jnp.float32)
+    for p in range(WINDOW):
+        block = fetch(p)
+
+        def find(r, carry, p=p, block=block):
+            here = pl.ds(pl.multiple_of(r * LANES, LANES), LANES)
+            best = jnp.max(value(block, p, here), axis=1, keepdims=True)
+            dual[here, :] = jnp.maximum(dual[here, :], best)
+            return carry
+
+        lax.fori_loop(0, count // LANES, find, 0)
+    total[...] = jnp.zeros(total.shape, jnp.float32)
+    for p in range(WINDOW):
+        block = fetch(p)
+
+        def add(r, carry, p=p, block=block):
+            here = pl.ds(pl.multiple_of(r * LANES, LANES), LANES)
+            e = jnp.exp2(value(block, p, here) - dual[here, 0:1])
+            total[here, :] += jnp.sum(e, axis=1, keepdims=True)
+            return carry
+
+        lax.fori_loop(0, count // LANES, add, 0)
+    dual[...] = -(dual[...] + jnp.log2(total[...]))
+
+
 def add_columns(entries, here, scale, col, width):
     for q in range(width):
         e = entries[here, q * LANES : (q + 1) * LANES] * scale
         col[:, q * LANES : (q + 1) * LANES] += jnp.sum(e.reshape(LANES // 8, 8, LANES), axis=0)
 
 
-def first_kernel(mask, rows, t0, t1, t2, t3, t4, entries, sums_out, top_out, base, dual, peak, col):
+def first_kernel(mask, rows, t0, t1, t2, t3, t4, entries, sums_out, top_out, base, dual, mass, good, col):
     targets = (t0, t1, t2, t3, t4)
     count = rows.shape[0]
     base[...] = jnp.zeros(base.shape, jnp.float32)
-    peak[...] = jnp.full(peak.shape, NEG, jnp.float32)
     for p in range(WINDOW):
         sq = jnp.square(targets[p][...].astype(jnp.float32))
         sq = sum(sq[:, q * LANES : (q + 1) * LANES] for q in range(sq.shape[1] // LANES))
@@ -186,56 +223,63 @@
             ],
             axis=1,
         )
-        bias = -KAPPA * bias
-        bias = jnp.where(is_listed(mask, p), bias, NEG)
+        bias = jnp.where(is_listed(mask, p), -KAPPA * bias, NEG)
         base[p : p + 1, :] = bias
 
-        block = dot_nt(rows[...], targets[p][...]) * TWO_KAPPA + bias
-        entries[:, p * count : (p + 1) * count] = block
-        best = peak[...]
+    block = dot_nt(rows[...], targets[0][...]) * TWO_KAPPA + base[0:1, :]
+    entries[:, 0:count] = block
+    best = block[:, 0:LANES]
+    for q in range(1, count // LANES):
+        best = jnp.maximum(best, block[:, q * LANES : (q + 1) * LANES])
+    top_out[...] = jnp.broadcast_to(jnp.max(best, axis=1, keepdims=True), (count, LANES))
+    for p in (1, 2, 3, 4, 0):
+        if p:
+            block = dot_nt(rows[...], targets[p][...]) * TWO_KAPPA + base[p : p + 1, :]
+        else:
+            block = entries[:, 0:count]
+        acc = jnp.zeros((count, LANES), jnp.float32) if p == 1 else mass[...]
+        top = top_out[...]
         for q in range(count // LANES):
-            best = jnp.maximum(best, block[:, q * LANES : (q + 1) * LANES])
-        peak[...] = best
+            e = jnp.exp2(block[:, q * LANES : (q + 1) * LANES] - top)
+            entries[:, p * count + q * LANES : p * count + (q + 1) * LANES] = e
+            acc = acc + e
+        mass[...] = acc
 
     col[...] = jnp.zeros(col.shape, jnp.float32)
+    good[...] = jnp.ones(good.shape, jnp.float32)
     width = WINDOW * count // LANES
 
     def rows_of(r):
         return pl.ds(pl.multiple_of(r * LANES, LANES), LANES)
 
-    def exponentials(r, meanwhile):
+    def invert(r, carry):
         here = rows_of(r)
-        top = jnp.broadcast_to(jnp.max(peak[here, :], axis=1, keepdims=True), (LANES, LANES))
-        acc = jnp.zeros((LANES, LANES), jnp.float32)
-        for q in range(width):
-            e = jnp.exp2(entries[here, q * LANES : (q + 1) * LANES] - top)
-            entries[here, q * LANES : (q + 1) * LANES] = e
-            acc = acc + e
-        total = jnp.broadcast_to(jnp.sum(acc, axis=1, keepdims=True), (LANES, LANES))
-        meanwhile()
-        top_out[here, :] = top
-        dual[here, :] = -(top + jnp.log2(total))
-        peak[here, :] = 1.0 / total
-
-    def columns(r):
-        add_columns(entries, rows_of(r), peak[rows_of(r), :], col, width)
-
-    def both(r, carry):
-        exponentials(r, lambda: columns(r - 1))
+        total = jnp.broadcast_to(jnp.sum(mass[here, :], axis=1, keepdims=True), (LANES, LANES))
+        note_range(good, total)
+        dual[here, :] = -(top_out[here, :] + jnp.log2(total))
+        mass[here, :] = 1.0 / total
         return carry
 
-    exponentials(0, lambda: None)
-    lax.fori_loop(1, count // LANES, both, 0)
-    columns(count // LANES - 1)
-    fine = put_columns(mask, base, col, sums_out, jnp.ones((1, LANES), jnp.float32))
+    lax.fori_loop(0, count // LANES, invert, 0)
+
+    def columns(r, carry):
+        add_columns(entries, rows_of(r), mass[rows_of(r), :], col, width)
+        return carry
+
+    lax.fori_loop(0, count // LANES, columns, 0)
+    fine = put_columns(mask, base, col, sums_out, jnp.min(good[...], axis=0, keepdims=True))
 
     @pl.when(jnp.logical_not(fine))
     def _():
-        put_exact_columns(mask, lambda p: (rows, targets[p]), dual, sums_out)
+        def fetch(p):
+            return rows, targets[p]
+
+        put_exact_rows(mask, fetch, base, dual, mass)
+        put_exact_columns(mask, fetch, dual, sums_out)
 
 
 def later_kernel(
-    mask, entries, pot, base, top, rows_far, t0, t1, t2, t3, t4, sums_out, dual_out, gain, col, low, total, rows, target
+    mask, entries, pot, base, top, rows_far, t0, t1, t2, t3, t4, sums_out, dual_out, gain, col, good, total, rows, target
 ):
     targets = (t0, t1, t2, t3, t4)
     count = rows.shape[0]
@@ -255,7 +299,7 @@
         gain[:, p * count : (p + 1) * count] = jnp.broadcast_to(
             jnp.where(taken, jnp.exp2(shift), 0.0), (8, count)
         )
-    low[...] = jnp.full(low.shape, 1.0, jnp.float32)
+    good[...] = jnp.ones(good.shape, jnp.float32)
 
     def rows_of(r):
         return pl.ds(pl.multiple_of(r * LANES, LANES), LANES)
@@ -268,7 +312,7 @@
             acc = acc + entries[here, at] * gain[0:1, at]
         mass = jnp.broadcast_to(jnp.sum(acc, axis=1, keepdims=True), (LANES, LANES))
         meanwhile()
-        low[...] = jnp.minimum(low[...], mass)
+        note_range(good, mass)
         dual_out[here, :] = -(top[here, :] + jnp.log2(mass))
         total[here, :] = 1.0 / mass
 
@@ -282,41 +326,14 @@
     weigh(0, lambda: None)
     lax.fori_loop(1, count // LANES, both, 0)
     columns(count // LANES - 1)
-    fine = jnp.where(jnp.min(low[...], axis=0, keepdims=True) >= SAFE_ROW, 1.0, 0.0)
+    fine = jnp.min(good[...], axis=0, keepdims=True)
     for q in range(count // LANES):
         fine = jnp.minimum(fine, jnp.where(worst[:, q * LANES : (q + 1) * LANES] <= SAFE_SHIFT, 1.0, 0.0))
     fine = put_columns(mask, base, col, sums_out, fine)
 
     @pl.when(jnp.logical_not(fine))
     def _():
-        def value(p, here):
-            bias = jnp.where(is_listed(mask, p), pot[p : p + 1, :], NEG)
-            return dot_nt(rows[here, :], target[...]) * TWO_KAPPA + bias
-
-        dual_out[...] = jnp.full(dual_out.shape, NEG, jnp.float32)
-        for p in range(WINDOW):
-            fetch(p)
-
-            def find(r, carry, p=p):
-                here = pl.ds(pl.multiple_of(r * LANES, LANES), LANES)
-                best = jnp.max(value(p, here), axis=1, keepdims=True)
-                dual_out[here, :] = jnp.maximum(dual_out[here, :], best)
-                return carry
-
-            lax.fori_loop(0, count // LANES, find, 0)
-        total[...] = jnp.zeros(total.shape, jnp.float32)
-        for p in range(WINDOW):
-            fetch(p)
-
-            def add(r, carry, p=p):
-                here = pl.ds(pl.multiple_of(r * LANES, LANES), LANES)
-                e = jnp.exp2(value(p, here) - dual_out[here, 0:1])
-                total[here, :] += jnp.sum(e, axis=1, keepdims=True)
-                return carry
-
-            lax.fori_loop(0, count // LANES, add, 0)
-        dual_out[...] = -(dual_out[...] + jnp.log2(total[...]))
-
+        put_exact_rows(mask, fetch, pot, dual_out, total)
         put_exact_columns(mask, fetch, dual_out, sums_out)
 
     for r in range(count // LANES):
@@ -347,6 +364,7 @@
         scratch_shapes=[
             pltpu.VMEM((count, LANES), jnp.float32),
             pltpu.VMEM((count, LANES), jnp.float32),
+            pltpu.VMEM((LANES, LANES), jnp.float32),
             pltpu.VMEM((8, WINDOW * count), jnp.float32),
         ],
         compiler_params=pltpu.CompilerParams(vmem_limit_bytes=SCOPED),
@@ -357,18 +375,21 @@
     )(mask, rows, *targets)
 
 
-def later_step(mask, entries, pot, base, top, rows, targets):
+def later_step(last, mask, entries, pot, base, top, rows, targets):
     count, width = rows.shape
     pairs = WINDOW * count * count
     row = jax.ShapeDtypeStruct((8, count), jnp.float32)
     column = jax.ShapeDtypeStruct((count, LANES), jnp.float32)
     entries = pltpu.with_memory_space_constraint(entries, pltpu.VMEM)
+    out_shape = (row, column) if last else (row,)
+    dual = [] if last else [pltpu.VMEM((count, LANES), jnp.float32)]
     return pl.pallas_call(
         later_kernel,
-        out_shape=(row, column),
+        out_shape=out_shape,
         in_specs=[SMEM] + [VMEM] * 4 + [ANY] * 6,
-        out_specs=(VMEM, VMEM),
-        scratch_shapes=[
+        out_specs=(VMEM,) * len(out_shape),
+        scratch_shapes=dual
+        + [
             pltpu.VMEM((8, WINDOW * count), jnp.float32),
             pltpu.VMEM((8, WINDOW * count), jnp.float32),
             pltpu.VMEM((LANES, LANES), jnp.float32),
@@ -453,9 +474,9 @@
     rows, even, up = lax.optimization_barrier((rows, even, up))
     entries, partial, top, base = first_step(pair_mask, rows, targets)
     total, (above, below) = column_totals(
-        partial, even, up, False, (rows,), (lambda x: shifted(x, -2), lambda x: shifted(x, 2)), True
+        partial, even, up, False, (rows,), (lambda x: shifted(x, -2), lambda x: shifted(x, 2))
     )
-    partial, dual = later_step(pair_mask, entries, -total, base, top, rows, targets)
+    (partial,) = later_step(False, pair_mask, entries, -total, base, top, rows, targets)
     total, (mate, cross) = column_totals(
         partial,
         even,
@@ -464,7 +485,7 @@
         (rows, above, below),
         (lambda x, a, b: swap_mate(x), lambda x, a, b: swap_mate(jnp.where(even, a, b))),
     )
-    partial, dual = later_step(pair_mask, entries, -total, base, top, rows, targets)
+    partial, dual = later_step(True, pair_mask, entries, -total, base, top, rows, targets)
     total, around = column_totals(partial, even, up, True)
     sources = (rows, mate, cross, above, below)
     return gradients(pair_mask, -total, dual, around, source, target, targets, sources)

time: 292 us -> 330 us (1.13)
  Pallas kernels: 105 us -> 198 us
  starting transfers between devices: 141 us -> 82.3 us
  waiting for transfers between devices: 18.9 us -> 22.8 us
    ppermute x20, starting transfers between devices: 137 us -> 78.8 us  [from_row(): return lax.ppermute(block, 'row', [(source_of(i), i) for i in range(count)])]
    pallas_call x1, Pallas kernels: 14.2 us -> 65.6 us  [first_step(): pl.pallas_call(first_kernel, out_shape=(pltpu.VMEM((count, WINDOW * count...]
    pallas_call x2, Pallas kernels: 86.7 us -> 128 us  [later_step(): pl.pallas_call(later_kernel, out_shape=out_shape, in_specs=[SMEM] + [VMEM...]
    ppermute x20, waiting for transfers between devices: 14.1 us -> 18.1 us  [from_row(): return lax.ppermute(block, 'row', [(source_of(i), i) for i in range(count)])]
  transfers between devices with their start and end apart: 21 -> 21, of which waited for: 9 -> 11; matrix products, arithmetic and copies ran while one was open for 1% -> 1% of each run, Pallas kernels for 15% -> 0%
where the time goes in v5:
time: 330 us; the launch traced here: 329 us
  Pallas kernels  198 us (60%)
  starting transfers between devices  82.3 us (25%)
  waiting for transfers between devices  22.8 us (7%)
  blocking collectives  19.7 us (6%)
  local copies, waits for them, and re-layouts  3.48 us (1%)
    pallas_call x2, Pallas kernels, later_step(): pl.pallas_call(later_kernel, out_shape=out_shape, in_specs=[SMEM] + [VMEM...  128 us
    ppermute x20, starting transfers between devices, from_row(): return lax.ppermute(block, 'row', [(source_of(i), i) for i in range(count)])  78.8 us
    pallas_call x1, Pallas kernels, first_step(): pl.pallas_call(first_kernel, out_shape=(pltpu.VMEM((count, WINDOW * count...  65.6 us
    all_to_all x1, blocking collectives, gathered(): lax.all_to_all(copies, 'grp', 0, 0, tiled=True).reshape(-1, shard.shape[1])  19.7 us
    ppermute x20, waiting for transfers between devices, from_row(): return lax.ppermute(block, 'row', [(source_of(i), i) for i in range(count)])  18.1 us
  transfers between devices with their start and end apart: 21, of which 11 were waited for; matrix products, arithmetic and copies ran while one was open for 1% of the time, Pallas kernels for 0%

profile of v5, /device:TPU:1, one launch (start us, length us, event | category | flops | bytes accessed | tf_op | source)
XLA Modules:
  0.0 329.2 jit_solution(5813519321700604150)
XLA Ops:
  1.5 19.7 %all_to_all.10 = bf16[8,128,256]{2,1,0:T(8,128)(2,1)S(1)} all-to-all(bf16[8,128,256]{2,1,0:T(8,128)(2,1)S(1)} %broadcast_in_dim.5), channel_id=1, replica_groups=mesh['row'=96,'grp'=8] {'grp'}, dimensions={0} | all-to-all | bytes 1048576 | tf_op jit(solution)/shard_map/all_to_all | solution.py:55
  21.2 7.8 %collective-permute-start.2 = (bf16[1024,256]{1,0:T(8,128)(2,1)S(1)}, bf16[1024,256]{1,0:T(8,128)(2,1)S(1)}, u32[]{:S(2)}, u32[]{:S(2)}) collective-permute-start(bf16[1024,256]{1,0:T(8,128)(2,1)S(1)} %bitcast.36), channel_id=1, source_target_pairs={{752,0},{760,8},{0,16},{8,24},{16,32},{24,40},{32,48},{40,56},{48,... | collective-permute-start | bytes 1572872 | tf_op jit(solution)/shard_map/ppermute | solution.py:26
  28.9 14.4 %collective-permute-start.1 = (bf16[1024,256]{1,0:T(8,128)(2,1)S(1)}, bf16[1024,256]{1,0:T(8,128)(2,1)S(1)}, u32[]{:S(2)}, u32[]{:S(2)}) collective-permute-start(bf16[1024,256]{1,0:T(8,128)(2,1)S(1)} %bitcast.37), channel_id=1, source_target_pairs={{16,0},{24,8},{32,16},{40,24},{48,32},{56,40},{64,48},{72,56},{80,... | collective-permute-start | bytes 1572872 | tf_op jit(solution)/shard_map/ppermute | solution.py:26
  45.1 3.5 %all-to-all-start = ((bf16[8,128,256]{2,1,0:T(8,128)(2,1)}), bf16[8,128,256]{2,1,0:T(8,128)(2,1)S(1)}, u32[]{:S(2)}, u32[]{:S(2)}) async-start(bf16[8,128,256]{2,1,0:T(8,128)(2,1)} %broadcast_in_dim.4), calls=%async_computation | async-start | bytes 1048576 | tf_op jit(solution)/shard_map/all_to_all | solution.py:55
  48.6 4.6 %collective-permute-start = (bf16[1024,256]{1,0:T(8,128)(2,1)S(1)}, bf16[1024,256]{1,0:T(8,128)(2,1)S(1)}, u32[]{:S(2)}, u32[]{:S(2)}) collective-permute-start(bf16[1024,256]{1,0:T(8,128)(2,1)S(1)} %bitcast.38), channel_id=1, source_target_pairs={{8,0},{0,8},{24,16},{16,24},{40,32},{32,40},{56,48},{48,56},{72,64... | collective-permute-start | bytes 1572872 | tf_op jit(solution)/shard_map/ppermute | solution.py:26
  54.1 4.1 %collective-permute-start.3 = (bf16[1024,256]{1,0:T(8,128)(2,1)}, bf16[1024,256]{1,0:T(8,128)(2,1)S(1)}, u32[]{:S(2)}, u32[]{:S(2)}) collective-permute-start(bf16[1024,256]{1,0:T(8,128)(2,1)} %broadcast_select_fusion.1), channel_id=1, source_target_pairs={{8,0},{0,8},{24,16},{16,24},{40,32},{32,40},{56,48},{48,56},{72,64... | collective-permute-start | bytes 1572872 | tf_op jit(solution)/shard_map/ppermute | solution.py:26
  58.3 4.8 %all-to-all-done = bf16[8,128,256]{2,1,0:T(8,128)(2,1)S(1)} async-done(((bf16[8,128,256]{2,1,0:T(8,128)(2,1)}), bf16[8,128,256]{2,1,0:T(8,128)(2,1)S(1)}, u32[]{:S(2)}, u32[]{:S(2)}) %all-to-all-start) | async-done | bytes 524320 | tf_op jit(solution)/shard_map/all_to_all | solution.py:55
  63.8 65.6 %first_step.1 = (f32[1024,5120]{1,0:T(8,128)S(1)}, f32[8,1024]{1,0:T(8,128)S(1)}, f32[1024,128]{1,0:T(8,128)S(1)}, f32[8,1024]{1,0:T(8,128)S(1)}) custom-call(s32[1,5]{1,0:T(1,128)S(1)} %copy-done.2, bf16[1024,256]{1,0:T(8,128)(2,1)S(1)} %bitcast.43, bf16[1024,256]{1,0:T(8,128)(2,1)S(1)} %bitcast.39, bf16[1024,256]{1,0:T(8,128)(2,1)S(1)} %collective-permute-done.t1, ...), custom_call_target="tpu_custom_call" | custom-call | flops 2684354560 | bytes 3145728 | tf_op jit(solution)/shard_map/first_step/pallas_call | solution.py:359
  129.4 5.7 %collective-permute-start.4 = (f32[6,1024]{1,0:T(8,128)S(1)}, f32[6,1024]{1,0:T(8,128)S(1)}, u32[]{:S(2)}, u32[]{:S(2)}) collective-permute-start(f32[6,1024]{1,0:T(8,128)S(1)} %bitcast.51), channel_id=1, source_target_pairs={{8,0},{0,8},{24,16},{16,24},{40,32},{32,40},{56,48},{48,56},{72,64... | collective-permute-start | bytes 73736 | tf_op jit(solution)/shard_map/ppermute | solution.py:26
  136.0 3.3 %collective-permute-start.5 = (f32[4,1024]{1,0:T(4,128)S(1)}, f32[4,1024]{1,0:T(4,128)S(1)}, u32[]{:S(2)}, u32[]{:S(2)}) collective-permute-start(f32[4,1024]{1,0:T(4,128)S(1)} %get-tuple-element.88), channel_id=1, source_target_pairs={{752,0},{744,8},{32,16},{760,24},{16,32},{72,40},{64,48},{88,56},{... | collective-permute-start | bytes 49160 | tf_op jit(solution)/shard_map/ppermute | solution.py:26
  139.4 1.9 collective-permute-start.6
  143.3 6.7 %collective-permute-start.8 = (bf16[1024,256]{1,0:T(8,128)(2,1)S(1)}, bf16[1024,256]{1,0:T(8,128)(2,1)S(1)}, u32[]{:S(2)}, u32[]{:S(2)}) collective-permute-start(bf16[1024,256]{1,0:T(8,128)(2,1)S(1)} %bitcast.45), channel_id=1, source_target_pairs={{16,0},{24,8},{32,16},{40,24},{48,32},{56,40},{64,48},{72,56},{80,... | collective-permute-start | bytes 1572872 | tf_op jit(solution)/shard_map/ppermute | solution.py:26
  150.2 2.1 collective-permute-start.7
  153.3 6.3 %collective-permute-done.9.x4 = bf16[1024,256]{1,0:T(8,128)(2,1)S(1)} collective-permute-done((bf16[1024,256]{1,0:T(8,128)(2,1)S(1)}, bf16[1024,256]{1,0:T(8,128)(2,1)S(1)}, u32[]{:S(2)}, u32[]{:S(2)}) %collective-permute-start.9) | collective-permute-done | bytes 524320 | tf_op jit(solution)/shard_map/ppermute | solution.py:26
  161.5 63.9 %later_step.2 = f32[8,1024]{1,0:T(8,128)S(1)} custom-call(s32[1,5]{1,0:T(1,128)S(1)} %copy-done.2, f32[1024,5120]{1,0:T(8,128)S(1)} %get-tuple-element.25.entries, f32[5,1024]{1,0:T(8,128)S(1)} %fusion.pot, f32[8,1024]{1,0:T(8,128)S(1)} %get-tuple-element.31.base, f32[1024,128]{1,0:T(8,128)S(1)} %get-tuple-element.32.top, bf16[1024,256]{1,0:T(8,128)(2,1)S(1)} %bitcast.46, ...), custom_call_target="tpu_custom_call" | custom-call | flops 20971520 | bytes 3145728 | tf_op jit(solution)/shard_map/later_step/pallas_call | solution.py:386
  225.4 2.0 collective-permute-start.10
  228.6 4.2 %collective-permute-start.11 = (f32[4,1024]{1,0:T(4,128)S(1)}, f32[4,1024]{1,0:T(4,128)S(1)}, u32[]{:S(2)}, u32[]{:S(2)}) collective-permute-start(f32[4,1024]{1,0:T(4,128)S(1)} %get-tuple-element.77), channel_id=1, source_target_pairs={{752,0},{744,8},{32,16},{760,24},{16,32},{72,40},{64,48},{88,56},{... | collective-permute-start | bytes 49160 | tf_op jit(solution)/shard_map/ppermute | solution.py:26
  232.8 1.9 collective-permute-start.12
  236.8 2.4 collective-permute-start.14
  242.6 64.4 %later_step.3 = (f32[8,1024]{1,0:T(8,128)S(1)}, f32[1024,128]{1,0:T(8,128)S(1)}) custom-call(s32[1,5]{1,0:T(1,128)S(1)} %copy-done.2, f32[1024,5120]{1,0:T(8,128)S(1)} %get-tuple-element.25.entries, f32[5,1024]{1,0:T(8,128)S(1)} %fusion.1.pot, f32[8,1024]{1,0:T(8,128)S(1)} %get-tuple-element.31.base, f32[1024,128]{1,0:T(8,128)S(1)} %get-tuple-element.32.top, ...), custom_call_target="tpu_custom_call" | custom-call | flops 20971520 | bytes 3145728 | tf_op jit(solution)/shard_map/later_step/pallas_call | solution.py:386
  307.0 2.1 collective-permute-start.16
  310.2 5.9 %collective-permute-start.17 = (f32[8,1024]{1,0:T(8,128)S(1)}, f32[8,1024]{1,0:T(8,128)S(1)}, u32[]{:S(2)}, u32[]{:S(2)}) collective-permute-start(f32[8,1024]{1,0:T(8,128)S(1)} %get-tuple-element.46), channel_id=1, source_target_pairs={{752,0},{744,8},{32,16},{760,24},{16,32},{72,40},{64,48},{88,56},{... | collective-permute-start | bytes 98312 | tf_op jit(solution)/shard_map/ppermute | solution.py:26
  319.2 2.5 collective-permute-done.18
  325.3 3.9 %plan_gradients.1 = (f32[128,256]{1,0:T(8,128)}, f32[128,256]{1,0:T(8,128)}) custom-call(s32[1,5]{1,0:T(1,128)S(1)} %copy-done.2, f32[5,1024]{1,0:T(8,128)S(1)} %fusion.2.pot, f32[1024,128]{1,0:T(8,128)S(1)} %get-tuple-element.41.dual, f32[5,2,1024]{2,1,0:T(2,128)S(1)} %broadcast_select_fusion.2.around, bf16[128,256]{1,0:T(8,128)(2,1)S(1)} %copy-done, ...), custom_call_target="tpu_custom_call" | custom-call | flops 1342177280 | bytes 5242880 | tf_op jit(solution)/shard_map/plan_gradients/pallas_call | solution.py:447
  (76 shorter events, 24.1 us)
Async XLA Ops:
  21.2 32.1 %collective-permute-start.2 = (bf16[1024,256]{1,0:T(8,128)(2,1)S(1)}, bf16[1024,256]{1,0:T(8,128)(2,1)S(1)}, u32[]{:S(2)}, u32[]{:S(2)}) collective-permute-start(bf16[1024,256]{1,0:T(8,128)(2,1)S(1)} %bitcast.36), channel_id=1, source_target_pairs={{752,0},{760,8},{0,16},{8,24},{16,32},{24,40},{32,48},{40,56},{48,... | collective-permute-start | bytes 1572872 | tf_op jit(solution)/shard_map/ppermute | solution.py:26
  28.9 24.3 %collective-permute-start.1 = (bf16[1024,256]{1,0:T(8,128)(2,1)S(1)}, bf16[1024,256]{1,0:T(8,128)(2,1)S(1)}, u32[]{:S(2)}, u32[]{:S(2)}) collective-permute-start(bf16[1024,256]{1,0:T(8,128)(2,1)S(1)} %bitcast.37), channel_id=1, source_target_pairs={{16,0},{24,8},{32,16},{40,24},{48,32},{56,40},{64,48},{72,56},{80,... | collective-permute-start | bytes 1572872 | tf_op jit(solution)/shard_map/ppermute | solution.py:26
  45.1 18.1 %all-to-all-start = ((bf16[8,128,256]{2,1,0:T(8,128)(2,1)}), bf16[8,128,256]{2,1,0:T(8,128)(2,1)S(1)}, u32[]{:S(2)}, u32[]{:S(2)}) async-start(bf16[8,128,256]{2,1,0:T(8,128)(2,1)} %broadcast_in_dim.4), calls=%async_computation | async-start | bytes 1048576 | tf_op jit(solution)/shard_map/all_to_all | solution.py:55
  48.6 14.6 %collective-permute-start = (bf16[1024,256]{1,0:T(8,128)(2,1)S(1)}, bf16[1024,256]{1,0:T(8,128)(2,1)S(1)}, u32[]{:S(2)}, u32[]{:S(2)}) collective-permute-start(bf16[1024,256]{1,0:T(8,128)(2,1)S(1)} %bitcast.38), channel_id=1, source_target_pairs={{8,0},{0,8},{24,16},{16,24},{40,32},{32,40},{56,48},{48,56},{72,64... | collective-permute-start | bytes 1572872 | tf_op jit(solution)/shard_map/ppermute | solution.py:26
  54.1 9.0 %collective-permute-start.3 = (bf16[1024,256]{1,0:T(8,128)(2,1)}, bf16[1024,256]{1,0:T(8,128)(2,1)S(1)}, u32[]{:S(2)}, u32[]{:S(2)}) collective-permute-start(bf16[1024,256]{1,0:T(8,128)(2,1)} %broadcast_select_fusion.1), channel_id=1, source_target_pairs={{8,0},{0,8},{24,16},{16,24},{40,32},{32,40},{56,48},{48,56},{72,64... | collective-permute-start | bytes 1572872 | tf_op jit(solution)/shard_map/ppermute | solution.py:26
  63.1 0.7 copy-start.2
  129.4 6.5 %collective-permute-start.4 = (f32[6,1024]{1,0:T(8,128)S(1)}, f32[6,1024]{1,0:T(8,128)S(1)}, u32[]{:S(2)}, u32[]{:S(2)}) collective-permute-start(f32[6,1024]{1,0:T(8,128)S(1)} %bitcast.51), channel_id=1, source_target_pairs={{8,0},{0,8},{24,16},{16,24},{40,32},{32,40},{56,48},{48,56},{72,64... | collective-permute-start | bytes 73736 | tf_op jit(solution)/shard_map/ppermute | solution.py:26
  136.0 14.0 %collective-permute-start.5 = (f32[4,1024]{1,0:T(4,128)S(1)}, f32[4,1024]{1,0:T(4,128)S(1)}, u32[]{:S(2)}, u32[]{:S(2)}) collective-permute-start(f32[4,1024]{1,0:T(4,128)S(1)} %get-tuple-element.88), channel_id=1, source_target_pairs={{752,0},{744,8},{32,16},{760,24},{16,32},{72,40},{64,48},{88,56},{... | collective-permute-start | bytes 49160 | tf_op jit(solution)/shard_map/ppermute | solution.py:26
  139.4 10.6 %collective-permute-start.6 = (f32[4,1024]{1,0:T(4,128)S(1)}, f32[4,1024]{1,0:T(4,128)S(1)}, u32[]{:S(2)}, u32[]{:S(2)}) collective-permute-start(f32[4,1024]{1,0:T(4,128)S(1)} %get-tuple-element.89), channel_id=1, source_target_pairs={{16,0},{40,8},{0,16},{56,24},{48,32},{8,40},{32,48},{24,56},{80,64... | collective-permute-start | bytes 49160 | tf_op jit(solution)/shard_map/ppermute | solution.py:26
  141.4 18.2 %collective-permute-start.9 = (bf16[1024,256]{1,0:T(8,128)(2,1)S(1)}, bf16[1024,256]{1,0:T(8,128)(2,1)S(1)}, u32[]{:S(2)}, u32[]{:S(2)}) collective-permute-start(bf16[1024,256]{1,0:T(8,128)(2,1)S(1)} %bitcast.44), channel_id=1, source_target_pairs={{752,0},{760,8},{0,16},{8,24},{16,32},{24,40},{32,48},{40,56},{48,... | collective-permute-start | bytes 1572872 | tf_op jit(solution)/shard_map/ppermute | solution.py:26
  143.3 18.1 %collective-permute-start.8 = (bf16[1024,256]{1,0:T(8,128)(2,1)S(1)}, bf16[1024,256]{1,0:T(8,128)(2,1)S(1)}, u32[]{:S(2)}, u32[]{:S(2)}) collective-permute-start(bf16[1024,256]{1,0:T(8,128)(2,1)S(1)} %bitcast.45), channel_id=1, source_target_pairs={{16,0},{24,8},{32,16},{40,24},{48,32},{56,40},{64,48},{72,56},{80,... | collective-permute-start | bytes 1572872 | tf_op jit(solution)/shard_map/ppermute | solution.py:26
  150.2 3.1 collective-permute-start.7
  161.5 163.8 %copy-start = (bf16[128,256]{1,0:T(8,128)(2,1)S(1)}, bf16[128,256]{1,0:T(8,128)(2,1)}, u32[]{:S(2)}) copy-start(bf16[128,256]{1,0:T(8,128)(2,1)} %mine.1) | copy-start | bytes 196612
  161.5 163.8 %copy-start.1 = (bf16[128,256]{1,0:T(8,128)(2,1)S(1)}, bf16[128,256]{1,0:T(8,128)(2,1)}, u32[]{:S(2)}) copy-start(bf16[128,256]{1,0:T(8,128)(2,1)} %own.1) | copy-start | bytes 196612
  225.4 3.1 collective-permute-start.10
  228.6 10.6 %collective-permute-start.11 = (f32[4,1024]{1,0:T(4,128)S(1)}, f32[4,1024]{1,0:T(4,128)S(1)}, u32[]{:S(2)}, u32[]{:S(2)}) collective-permute-start(f32[4,1024]{1,0:T(4,128)S(1)} %get-tuple-element.77), channel_id=1, source_target_pairs={{752,0},{744,8},{32,16},{760,24},{16,32},{72,40},{64,48},{88,56},{... | collective-permute-start | bytes 49160 | tf_op jit(solution)/shard_map/ppermute | solution.py:26
  232.8 6.3 %collective-permute-start.12 = (f32[4,1024]{1,0:T(4,128)S(1)}, f32[4,1024]{1,0:T(4,128)S(1)}, u32[]{:S(2)}, u32[]{:S(2)}) collective-permute-start(f32[4,1024]{1,0:T(4,128)S(1)} %get-tuple-element.78), channel_id=1, source_target_pairs={{16,0},{40,8},{0,16},{56,24},{48,32},{8,40},{32,48},{24,56},{80,64... | collective-permute-start | bytes 49160 | tf_op jit(solution)/shard_map/ppermute | solution.py:26
  234.8 7.7 %collective-permute-start.15 = (bf16[1024,256]{1,0:T(8,128)(2,1)S(1)}, bf16[1024,256]{1,0:T(8,128)(2,1)S(1)}, u32[]{:S(2)}, u32[]{:S(2)}) collective-permute-start(bf16[1024,256]{1,0:T(8,128)(2,1)S(1)} %broadcast_select_fusion), channel_id=1, source_target_pairs={{8,0},{0,8},{24,16},{16,24},{40,32},{32,40},{56,48},{48,56},{72,64... | collective-permute-start | bytes 1572872 | tf_op jit(solution)/shard_map/ppermute | solution.py:26
  236.8 5.7 %collective-permute-start.14 = (bf16[1024,256]{1,0:T(8,128)(2,1)S(1)}, bf16[1024,256]{1,0:T(8,128)(2,1)S(1)}, u32[]{:S(2)}, u32[]{:S(2)}) collective-permute-start(bf16[1024,256]{1,0:T(8,128)(2,1)S(1)} %bitcast.47), channel_id=1, source_target_pairs={{8,0},{0,8},{24,16},{16,24},{40,32},{32,40},{56,48},{48,56},{72,64... | collective-permute-start | bytes 1572872 | tf_op jit(solution)/shard_map/ppermute | solution.py:26
  239.3 3.1 collective-permute-start.13
  307.0 3.1 collective-permute-start.16
  310.2 9.0 %collective-permute-start.17 = (f32[8,1024]{1,0:T(8,128)S(1)}, f32[8,1024]{1,0:T(8,128)S(1)}, u32[]{:S(2)}, u32[]{:S(2)}) collective-permute-start(f32[8,1024]{1,0:T(8,128)S(1)} %get-tuple-element.46), channel_id=1, source_target_pairs={{752,0},{744,8},{32,16},{760,24},{16,32},{72,40},{64,48},{88,56},{... | collective-permute-start | bytes 98312 | tf_op jit(solution)/shard_map/ppermute | solution.py:26
  316.1 5.6 %collective-permute-start.18 = (f32[8,1024]{1,0:T(8,128)S(1)}, f32[8,1024]{1,0:T(8,128)S(1)}, u32[]{:S(2)}, u32[]{:S(2)}) collective-permute-start(f32[8,1024]{1,0:T(8,128)S(1)} %get-tuple-element.47), channel_id=1, source_target_pairs={{16,0},{40,8},{0,16},{56,24},{48,32},{8,40},{32,48},{24,56},{80,64... | collective-permute-start | bytes 98312 | tf_op jit(solution)/shard_map/ppermute | solution.py:26
  321.9 3.1 collective-permute-start.19

commit v6 on v5

--- a/solution.py
+++ b/solution.py
@@ -60,7 +60,7 @@
     return top + jnp.log2(jnp.exp2(a - top) + jnp.exp2(b - top))
 
 
-def column_totals(partial, even, up, extra=False, cargo=None, movers=()):
+def column_totals(partial, even, up, extra=False, cargo=None, movers=(), late=False):
     count = 2 if extra else 0
     other = swap_mate(partial[: 6 + count])
     chip = lse2(partial[:6], other[:6])
@@ -89,7 +89,8 @@
     total = lse2(chip, lse2(outer, got[:6]))
     if movers:
         moved = [move(*cargo) for move in movers]
-        total, moved = lax.optimization_barrier((total, moved))
+        if not late:
+            total, moved = lax.optimization_barrier((total, moved))
 
     def placed(rows):
         return jnp.where(
@@ -474,7 +475,7 @@
     rows, even, up = lax.optimization_barrier((rows, even, up))
     entries, partial, top, base = first_step(pair_mask, rows, targets)
     total, (above, below) = column_totals(
-        partial, even, up, False, (rows,), (lambda x: shifted(x, -2), lambda x: shifted(x, 2))
+        partial, even, up, False, (rows,), (lambda x: shifted(x, -2), lambda x: shifted(x, 2)), True
     )
     (partial,) = later_step(False, pair_mask, entries, -total, base, top, rows, targets)
     total, (mate, cross) = column_totals(

time: 330 us -> 321 us (0.973)
  Pallas kernels: 198 us -> 166 us
  starting transfers between devices: 82.3 us -> 111 us
  waiting for transfers between devices: 22.8 us -> 16.7 us
    ppermute x20, starting transfers between devices: 78.8 us -> 107 us  [from_row(): return lax.ppermute(block, 'row', [(source_of(i), i) for i in range(count)])]
    pallas_call x2, Pallas kernels: 128 us -> 107 us  [later_step(): pl.pallas_call(later_kernel, out_shape=out_shape, in_specs=[SMEM] + [VMEM...]
    pallas_call x1, Pallas kernels: 65.6 us -> 55.2 us  [first_step(): pl.pallas_call(first_kernel, out_shape=(pltpu.VMEM((count, WINDOW * count...]
    ppermute x20, waiting for transfers between devices: 18.1 us -> 11.9 us  [from_row(): return lax.ppermute(block, 'row', [(source_of(i), i) for i in range(count)])]
  transfers between devices with their start and end apart: 21 -> 21, of which waited for: 11 -> 8; matrix products, arithmetic and copies ran while one was open for 1% -> 1% of each run, Pallas kernels for 0% -> 17%
where the time goes in v6:
time: 321 us; the launch traced here: 320 us
  Pallas kernels  166 us (52%)
  starting transfers between devices  111 us (35%)
  blocking collectives  19.7 us (6%)
  waiting for transfers between devices  16.7 us (5%)
  local copies, waits for them, and re-layouts  3.48 us (1%)
    pallas_call x2, Pallas kernels, later_step(): pl.pallas_call(later_kernel, out_shape=out_shape, in_specs=[SMEM] + [VMEM...  107 us
    ppermute x20, starting transfers between devices, from_row(): return lax.ppermute(block, 'row', [(source_of(i), i) for i in range(count)])  107 us
    pallas_call x1, Pallas kernels, first_step(): pl.pallas_call(first_kernel, out_shape=(pltpu.VMEM((count, WINDOW * count...  55.2 us
    all_to_all x1, blocking collectives, gathered(): lax.all_to_all(copies, 'grp', 0, 0, tiled=True).reshape(-1, shard.shape[1])  19.7 us
    ppermute x20, waiting for transfers between devices, from_row(): return lax.ppermute(block, 'row', [(source_of(i), i) for i in range(count)])  11.9 us
  transfers between devices with their start and end apart: 21, of which 8 were waited for; matrix products, arithmetic and copies ran while one was open for 1% of the time, Pallas kernels for 17%

profile of v6, /device:TPU:1, one launch (start us, length us, event | category | flops | bytes accessed | tf_op | source)
XLA Modules:
  0.0 319.8 jit_solution(412088110377149727)
XLA Ops:
  1.5 19.7 %all_to_all.10 = bf16[8,128,256]{2,1,0:T(8,128)(2,1)S(1)} all-to-all(bf16[8,128,256]{2,1,0:T(8,128)(2,1)S(1)} %broadcast_in_dim.5), channel_id=1, replica_groups=mesh['row'=96,'grp'=8] {'grp'}, dimensions={0} | all-to-all | bytes 1048576 | tf_op jit(solution)/shard_map/all_to_all | solution.py:55
  21.2 7.8 %collective-permute-start.2 = (bf16[1024,256]{1,0:T(8,128)(2,1)S(1)}, bf16[1024,256]{1,0:T(8,128)(2,1)S(1)}, u32[]{:S(2)}, u32[]{:S(2)}) collective-permute-start(bf16[1024,256]{1,0:T(8,128)(2,1)S(1)} %bitcast.36), channel_id=1, source_target_pairs={{752,0},{760,8},{0,16},{8,24},{16,32},{24,40},{32,48},{40,56},{48,... | collective-permute-start | bytes 1572872 | tf_op jit(solution)/shard_map/ppermute | solution.py:26
  28.9 14.4 %collective-permute-start.1 = (bf16[1024,256]{1,0:T(8,128)(2,1)S(1)}, bf16[1024,256]{1,0:T(8,128)(2,1)S(1)}, u32[]{:S(2)}, u32[]{:S(2)}) collective-permute-start(bf16[1024,256]{1,0:T(8,128)(2,1)S(1)} %bitcast.37), channel_id=1, source_target_pairs={{16,0},{24,8},{32,16},{40,24},{48,32},{56,40},{64,48},{72,56},{80,... | collective-permute-start | bytes 1572872 | tf_op jit(solution)/shard_map/ppermute | solution.py:26
  45.1 3.5 %all-to-all-start = ((bf16[8,128,256]{2,1,0:T(8,128)(2,1)}), bf16[8,128,256]{2,1,0:T(8,128)(2,1)S(1)}, u32[]{:S(2)}, u32[]{:S(2)}) async-start(bf16[8,128,256]{2,1,0:T(8,128)(2,1)} %broadcast_in_dim.4), calls=%async_computation | async-start | bytes 1048576 | tf_op jit(solution)/shard_map/all_to_all | solution.py:55
  48.6 4.6 %collective-permute-start = (bf16[1024,256]{1,0:T(8,128)(2,1)S(1)}, bf16[1024,256]{1,0:T(8,128)(2,1)S(1)}, u32[]{:S(2)}, u32[]{:S(2)}) collective-permute-start(bf16[1024,256]{1,0:T(8,128)(2,1)S(1)} %bitcast.38), channel_id=1, source_target_pairs={{8,0},{0,8},{24,16},{16,24},{40,32},{32,40},{56,48},{48,56},{72,64... | collective-permute-start | bytes 1572872 | tf_op jit(solution)/shard_map/ppermute | solution.py:26
  54.1 4.1 %collective-permute-start.3 = (bf16[1024,256]{1,0:T(8,128)(2,1)}, bf16[1024,256]{1,0:T(8,128)(2,1)S(1)}, u32[]{:S(2)}, u32[]{:S(2)}) collective-permute-start(bf16[1024,256]{1,0:T(8,128)(2,1)} %broadcast_select_fusion.1), channel_id=1, source_target_pairs={{8,0},{0,8},{24,16},{16,24},{40,32},{32,40},{56,48},{48,56},{72,64... | collective-permute-start | bytes 1572872 | tf_op jit(solution)/shard_map/ppermute | solution.py:26
  58.3 4.8 %all-to-all-done = bf16[8,128,256]{2,1,0:T(8,128)(2,1)S(1)} async-done(((bf16[8,128,256]{2,1,0:T(8,128)(2,1)}), bf16[8,128,256]{2,1,0:T(8,128)(2,1)S(1)}, u32[]{:S(2)}, u32[]{:S(2)}) %all-to-all-start) | async-done | bytes 524320 | tf_op jit(solution)/shard_map/all_to_all | solution.py:55
  63.8 55.2 %first_step.1 = (f32[1024,5120]{1,0:T(8,128)S(1)}, f32[8,1024]{1,0:T(8,128)S(1)}, f32[1024,128]{1,0:T(8,128)S(1)}, f32[8,1024]{1,0:T(8,128)S(1)}) custom-call(s32[1,5]{1,0:T(1,128)S(1)} %copy-done.2, bf16[1024,256]{1,0:T(8,128)(2,1)S(1)} %bitcast.43, bf16[1024,256]{1,0:T(8,128)(2,1)S(1)} %bitcast.39, bf16[1024,256]{1,0:T(8,128)(2,1)S(1)} %collective-permute-done.t1, ...), custom_call_target="tpu_custom_call" | custom-call | flops 2684354560 | bytes 3145728 | tf_op jit(solution)/shard_map/first_step/pallas_call | solution.py:360
  119.0 5.7 %collective-permute-start.4 = (f32[6,1024]{1,0:T(8,128)S(1)}, f32[6,1024]{1,0:T(8,128)S(1)}, u32[]{:S(2)}, u32[]{:S(2)}) collective-permute-start(f32[6,1024]{1,0:T(8,128)S(1)} %bitcast.51), channel_id=1, source_target_pairs={{8,0},{0,8},{24,16},{16,24},{40,32},{32,40},{56,48},{48,56},{72,64... | collective-permute-start | bytes 73736 | tf_op jit(solution)/shard_map/ppermute | solution.py:26
  125.6 13.8 %collective-permute-start.5 = (f32[4,1024]{1,0:T(4,128)S(1)}, f32[4,1024]{1,0:T(4,128)S(1)}, u32[]{:S(2)}, u32[]{:S(2)}) collective-permute-start(f32[4,1024]{1,0:T(4,128)S(1)} %get-tuple-element.82), channel_id=1, source_target_pairs={{752,0},{744,8},{32,16},{760,24},{16,32},{72,40},{64,48},{88,56},{... | collective-permute-start | bytes 49160 | tf_op jit(solution)/shard_map/ppermute | solution.py:26
  141.4 3.4 %collective-permute-done.6 = f32[4,1024]{1,0:T(4,128)S(1)} collective-permute-done((f32[4,1024]{1,0:T(4,128)S(1)}, f32[4,1024]{1,0:T(4,128)S(1)}, u32[]{:S(2)}, u32[]{:S(2)}) %collective-permute-start.6) | collective-permute-done | bytes 16416 | tf_op jit(solution)/shard_map/ppermute | solution.py:26
  144.9 2.8 collective-permute-start.7
  147.7 2.2 collective-permute-start.10
  149.9 6.6 %collective-permute-start.9 = (bf16[1024,256]{1,0:T(8,128)(2,1)S(1)}, bf16[1024,256]{1,0:T(8,128)(2,1)S(1)}, u32[]{:S(2)}, u32[]{:S(2)}) collective-permute-start(bf16[1024,256]{1,0:T(8,128)(2,1)S(1)} %bitcast.45), channel_id=1, source_target_pairs={{16,0},{24,8},{32,16},{40,24},{48,32},{56,40},{64,48},{72,56},{80,... | collective-permute-start | bytes 1572872 | tf_op jit(solution)/shard_map/ppermute | solution.py:26
  156.7 53.4 %later_step.2 = f32[8,1024]{1,0:T(8,128)S(1)} custom-call(s32[1,5]{1,0:T(1,128)S(1)} %copy-done.2, f32[1024,5120]{1,0:T(8,128)S(1)} %get-tuple-element.22.entries, f32[5,1024]{1,0:T(8,128)S(1)} %fusion.pot, f32[8,1024]{1,0:T(8,128)S(1)} %get-tuple-element.26.base, f32[1024,128]{1,0:T(8,128)S(1)} %get-tuple-element.27.top, bf16[1024,256]{1,0:T(8,128)(2,1)S(1)} %bitcast.46, ...), custom_call_target="tpu_custom_call" | custom-call | flops 20971520 | bytes 3145728 | tf_op jit(solution)/shard_map/later_step/pallas_call | solution.py:387
  210.1 2.5 collective-permute-start.8
  213.5 10.2 %collective-permute-start.11 = (f32[4,1024]{1,0:T(4,128)S(1)}, f32[4,1024]{1,0:T(4,128)S(1)}, u32[]{:S(2)}, u32[]{:S(2)}) collective-permute-start(f32[4,1024]{1,0:T(4,128)S(1)} %get-tuple-element.71), channel_id=1, source_target_pairs={{752,0},{744,8},{32,16},{760,24},{16,32},{72,40},{64,48},{88,56},{... | collective-permute-start | bytes 49160 | tf_op jit(solution)/shard_map/ppermute | solution.py:26
  225.8 4.4 %collective-permute-start.15 = (bf16[1024,256]{1,0:T(8,128)(2,1)S(1)}, bf16[1024,256]{1,0:T(8,128)(2,1)S(1)}, u32[]{:S(2)}, u32[]{:S(2)}) collective-permute-start(bf16[1024,256]{1,0:T(8,128)(2,1)S(1)} %broadcast_select_fusion), channel_id=1, source_target_pairs={{8,0},{0,8},{24,16},{16,24},{40,32},{32,40},{56,48},{48,56},{72,64... | collective-permute-start | bytes 1572872 | tf_op jit(solution)/shard_map/ppermute | solution.py:26
  232.3 2.4 collective-permute-start.13
  235.7 53.8 %later_step.3 = (f32[8,1024]{1,0:T(8,128)S(1)}, f32[1024,128]{1,0:T(8,128)S(1)}) custom-call(s32[1,5]{1,0:T(1,128)S(1)} %copy-done.2, f32[1024,5120]{1,0:T(8,128)S(1)} %get-tuple-element.22.entries, f32[5,1024]{1,0:T(8,128)S(1)} %fusion.1.pot, f32[8,1024]{1,0:T(8,128)S(1)} %get-tuple-element.26.base, f32[1024,128]{1,0:T(8,128)S(1)} %get-tuple-element.27.top, ...), custom_call_target="tpu_custom_call" | custom-call | flops 20971520 | bytes 3145728 | tf_op jit(solution)/shard_map/later_step/pallas_call | solution.py:387
  289.5 2.3 collective-permute-start.16
  292.8 13.6 %collective-permute-start.17 = (f32[8,1024]{1,0:T(8,128)S(1)}, f32[8,1024]{1,0:T(8,128)S(1)}, u32[]{:S(2)}, u32[]{:S(2)}) collective-permute-start(f32[8,1024]{1,0:T(8,128)S(1)} %get-tuple-element.40), channel_id=1, source_target_pairs={{752,0},{744,8},{32,16},{760,24},{16,32},{72,40},{64,48},{88,56},{... | collective-permute-start | bytes 98312 | tf_op jit(solution)/shard_map/ppermute | solution.py:26
  308.3 4.0 %collective-permute-done.18 = f32[8,1024]{1,0:T(8,128)S(1)} collective-permute-done((f32[8,1024]{1,0:T(8,128)S(1)}, f32[8,1024]{1,0:T(8,128)S(1)}, u32[]{:S(2)}, u32[]{:S(2)}) %collective-permute-start.18) | collective-permute-done | bytes 32800 | tf_op jit(solution)/shard_map/ppermute | solution.py:26
  315.9 3.9 %plan_gradients.1 = (f32[128,256]{1,0:T(8,128)}, f32[128,256]{1,0:T(8,128)}) custom-call(s32[1,5]{1,0:T(1,128)S(1)} %copy-done.2, f32[5,1024]{1,0:T(8,128)S(1)} %fusion.2.pot, f32[1024,128]{1,0:T(8,128)S(1)} %get-tuple-element.35.dual, f32[5,2,1024]{2,1,0:T(2,128)S(1)} %broadcast_select_fusion.2.around, bf16[128,256]{1,0:T(8,128)(2,1)S(1)} %copy-done, ...), custom_call_target="tpu_custom_call" | custom-call | flops 1342177280 | bytes 5242880 | tf_op jit(solution)/shard_map/plan_gradients/pallas_call | solution.py:448
  (76 shorter events, 19.6 us)
Async XLA Ops:
  21.2 32.1 %collective-permute-start.2 = (bf16[1024,256]{1,0:T(8,128)(2,1)S(1)}, bf16[1024,256]{1,0:T(8,128)(2,1)S(1)}, u32[]{:S(2)}, u32[]{:S(2)}) collective-permute-start(bf16[1024,256]{1,0:T(8,128)(2,1)S(1)} %bitcast.36), channel_id=1, source_target_pairs={{752,0},{760,8},{0,16},{8,24},{16,32},{24,40},{32,48},{40,56},{48,... | collective-permute-start | bytes 1572872 | tf_op jit(solution)/shard_map/ppermute | solution.py:26
  28.9 24.3 %collective-permute-start.1 = (bf16[1024,256]{1,0:T(8,128)(2,1)S(1)}, bf16[1024,256]{1,0:T(8,128)(2,1)S(1)}, u32[]{:S(2)}, u32[]{:S(2)}) collective-permute-start(bf16[1024,256]{1,0:T(8,128)(2,1)S(1)} %bitcast.37), channel_id=1, source_target_pairs={{16,0},{24,8},{32,16},{40,24},{48,32},{56,40},{64,48},{72,56},{80,... | collective-permute-start | bytes 1572872 | tf_op jit(solution)/shard_map/ppermute | solution.py:26
  45.1 18.1 %all-to-all-start = ((bf16[8,128,256]{2,1,0:T(8,128)(2,1)}), bf16[8,128,256]{2,1,0:T(8,128)(2,1)S(1)}, u32[]{:S(2)}, u32[]{:S(2)}) async-start(bf16[8,128,256]{2,1,0:T(8,128)(2,1)} %broadcast_in_dim.4), calls=%async_computation | async-start | bytes 1048576 | tf_op jit(solution)/shard_map/all_to_all | solution.py:55
  48.6 14.6 %collective-permute-start = (bf16[1024,256]{1,0:T(8,128)(2,1)S(1)}, bf16[1024,256]{1,0:T(8,128)(2,1)S(1)}, u32[]{:S(2)}, u32[]{:S(2)}) collective-permute-start(bf16[1024,256]{1,0:T(8,128)(2,1)S(1)} %bitcast.38), channel_id=1, source_target_pairs={{8,0},{0,8},{24,16},{16,24},{40,32},{32,40},{56,48},{48,56},{72,64... | collective-permute-start | bytes 1572872 | tf_op jit(solution)/shard_map/ppermute | solution.py:26
  54.1 9.0 %collective-permute-start.3 = (bf16[1024,256]{1,0:T(8,128)(2,1)}, bf16[1024,256]{1,0:T(8,128)(2,1)S(1)}, u32[]{:S(2)}, u32[]{:S(2)}) collective-permute-start(bf16[1024,256]{1,0:T(8,128)(2,1)} %broadcast_select_fusion.1), channel_id=1, source_target_pairs={{8,0},{0,8},{24,16},{16,24},{40,32},{32,40},{56,48},{48,56},{72,64... | collective-permute-start | bytes 1572872 | tf_op jit(solution)/shard_map/ppermute | solution.py:26
  63.1 0.7 copy-start.2
  119.0 6.5 %collective-permute-start.4 = (f32[6,1024]{1,0:T(8,128)S(1)}, f32[6,1024]{1,0:T(8,128)S(1)}, u32[]{:S(2)}, u32[]{:S(2)}) collective-permute-start(f32[6,1024]{1,0:T(8,128)S(1)} %bitcast.51), channel_id=1, source_target_pairs={{8,0},{0,8},{24,16},{16,24},{40,32},{32,40},{56,48},{48,56},{72,64... | collective-permute-start | bytes 73736 | tf_op jit(solution)/shard_map/ppermute | solution.py:26
  125.6 15.8 %collective-permute-start.5 = (f32[4,1024]{1,0:T(4,128)S(1)}, f32[4,1024]{1,0:T(4,128)S(1)}, u32[]{:S(2)}, u32[]{:S(2)}) collective-permute-start(f32[4,1024]{1,0:T(4,128)S(1)} %get-tuple-element.82), channel_id=1, source_target_pairs={{752,0},{744,8},{32,16},{760,24},{16,32},{72,40},{64,48},{88,56},{... | collective-permute-start | bytes 49160 | tf_op jit(solution)/shard_map/ppermute | solution.py:26
  139.4 5.4 %collective-permute-start.6 = (f32[4,1024]{1,0:T(4,128)S(1)}, f32[4,1024]{1,0:T(4,128)S(1)}, u32[]{:S(2)}, u32[]{:S(2)}) collective-permute-start(f32[4,1024]{1,0:T(4,128)S(1)} %get-tuple-element.83), channel_id=1, source_target_pairs={{16,0},{40,8},{0,16},{56,24},{48,32},{8,40},{32,48},{24,56},{80,64... | collective-permute-start | bytes 49160 | tf_op jit(solution)/shard_map/ppermute | solution.py:26
  144.9 11.6 %collective-permute-start.7 = (f32[6,1024]{1,0:T(8,128)S(1)}, f32[6,1024]{1,0:T(8,128)S(1)}, u32[]{:S(2)}, u32[]{:S(2)}) collective-permute-start(f32[6,1024]{1,0:T(8,128)S(1)} %maximum_select_fusion), channel_id=1, source_target_pairs={{8,0},{0,8},{24,16},{16,24},{40,32},{32,40},{56,48},{48,56},{72,64... | collective-permute-start | bytes 73736 | tf_op jit(solution)/shard_map/ppermute | solution.py:26
  147.7 65.7 %collective-permute-start.10 = (bf16[1024,256]{1,0:T(8,128)(2,1)S(1)}, bf16[1024,256]{1,0:T(8,128)(2,1)S(1)}, u32[]{:S(2)}, u32[]{:S(2)}) collective-permute-start(bf16[1024,256]{1,0:T(8,128)(2,1)S(1)} %bitcast.44), channel_id=1, source_target_pairs={{752,0},{760,8},{0,16},{8,24},{16,32},{24,40},{32,48},{40,56},{48,... | collective-permute-start | bytes 1572872 | tf_op jit(solution)/shard_map/ppermute | solution.py:26
  149.9 63.5 %collective-permute-start.9 = (bf16[1024,256]{1,0:T(8,128)(2,1)S(1)}, bf16[1024,256]{1,0:T(8,128)(2,1)S(1)}, u32[]{:S(2)}, u32[]{:S(2)}) collective-permute-start(bf16[1024,256]{1,0:T(8,128)(2,1)S(1)} %bitcast.45), channel_id=1, source_target_pairs={{16,0},{24,8},{32,16},{40,24},{48,32},{56,40},{64,48},{72,56},{80,... | collective-permute-start | bytes 1572872 | tf_op jit(solution)/shard_map/ppermute | solution.py:26
  156.6 159.3 %copy-start = (bf16[128,256]{1,0:T(8,128)(2,1)S(1)}, bf16[128,256]{1,0:T(8,128)(2,1)}, u32[]{:S(2)}) copy-start(bf16[128,256]{1,0:T(8,128)(2,1)} %mine.1) | copy-start | bytes 196612
  156.6 159.3 %copy-start.1 = (bf16[128,256]{1,0:T(8,128)(2,1)S(1)}, bf16[128,256]{1,0:T(8,128)(2,1)}, u32[]{:S(2)}) copy-start(bf16[128,256]{1,0:T(8,128)(2,1)} %own.1) | copy-start | bytes 196612
  210.1 3.3 %collective-permute-start.8 = (f32[6,1024]{1,0:T(8,128)S(1)}, f32[6,1024]{1,0:T(8,128)S(1)}, u32[]{:S(2)}, u32[]{:S(2)}) collective-permute-start(f32[6,1024]{1,0:T(8,128)S(1)} %bitcast.50), channel_id=1, source_target_pairs={{8,0},{0,8},{24,16},{16,24},{40,32},{32,40},{56,48},{48,56},{72,64... | collective-permute-start | bytes 73736 | tf_op jit(solution)/shard_map/ppermute | solution.py:26
  213.5 18.7 %collective-permute-start.11 = (f32[4,1024]{1,0:T(4,128)S(1)}, f32[4,1024]{1,0:T(4,128)S(1)}, u32[]{:S(2)}, u32[]{:S(2)}) collective-permute-start(f32[4,1024]{1,0:T(4,128)S(1)} %get-tuple-element.71), channel_id=1, source_target_pairs={{752,0},{744,8},{32,16},{760,24},{16,32},{72,40},{64,48},{88,56},{... | collective-permute-start | bytes 49160 | tf_op jit(solution)/shard_map/ppermute | solution.py:26
  223.6 8.5 %collective-permute-start.12 = (f32[4,1024]{1,0:T(4,128)S(1)}, f32[4,1024]{1,0:T(4,128)S(1)}, u32[]{:S(2)}, u32[]{:S(2)}) collective-permute-start(f32[4,1024]{1,0:T(4,128)S(1)} %get-tuple-element.72), channel_id=1, source_target_pairs={{16,0},{40,8},{0,16},{56,24},{48,32},{8,40},{32,48},{24,56},{80,64... | collective-permute-start | bytes 49160 | tf_op jit(solution)/shard_map/ppermute | solution.py:26
  225.8 9.8 %collective-permute-start.15 = (bf16[1024,256]{1,0:T(8,128)(2,1)S(1)}, bf16[1024,256]{1,0:T(8,128)(2,1)S(1)}, u32[]{:S(2)}, u32[]{:S(2)}) collective-permute-start(bf16[1024,256]{1,0:T(8,128)(2,1)S(1)} %broadcast_select_fusion), channel_id=1, source_target_pairs={{8,0},{0,8},{24,16},{16,24},{40,32},{32,40},{56,48},{48,56},{72,64... | collective-permute-start | bytes 1572872 | tf_op jit(solution)/shard_map/ppermute | solution.py:26
  230.2 5.4 %collective-permute-start.14 = (bf16[1024,256]{1,0:T(8,128)(2,1)S(1)}, bf16[1024,256]{1,0:T(8,128)(2,1)S(1)}, u32[]{:S(2)}, u32[]{:S(2)}) collective-permute-start(bf16[1024,256]{1,0:T(8,128)(2,1)S(1)} %bitcast.47), channel_id=1, source_target_pairs={{8,0},{0,8},{24,16},{16,24},{40,32},{32,40},{56,48},{48,56},{72,64... | collective-permute-start | bytes 1572872 | tf_op jit(solution)/shard_map/ppermute | solution.py:26
  232.3 3.2 %collective-permute-start.13 = (f32[6,1024]{1,0:T(8,128)S(1)}, f32[6,1024]{1,0:T(8,128)S(1)}, u32[]{:S(2)}, u32[]{:S(2)}) collective-permute-start(f32[6,1024]{1,0:T(8,128)S(1)} %maximum_select_fusion.2), channel_id=1, source_target_pairs={{8,0},{0,8},{24,16},{16,24},{40,32},{32,40},{56,48},{48,56},{72,64... | collective-permute-start | bytes 73736 | tf_op jit(solution)/shard_map/ppermute | solution.py:26
  289.5 3.1 collective-permute-start.16
  292.8 15.6 %collective-permute-start.17 = (f32[8,1024]{1,0:T(8,128)S(1)}, f32[8,1024]{1,0:T(8,128)S(1)}, u32[]{:S(2)}, u32[]{:S(2)}) collective-permute-start(f32[8,1024]{1,0:T(8,128)S(1)} %get-tuple-element.40), channel_id=1, source_target_pairs={{752,0},{744,8},{32,16},{760,24},{16,32},{72,40},{64,48},{88,56},{... | collective-permute-start | bytes 98312 | tf_op jit(solution)/shard_map/ppermute | solution.py:26
  306.4 5.9 %collective-permute-start.18 = (f32[8,1024]{1,0:T(8,128)S(1)}, f32[8,1024]{1,0:T(8,128)S(1)}, u32[]{:S(2)}, u32[]{:S(2)}) collective-permute-start(f32[8,1024]{1,0:T(8,128)S(1)} %get-tuple-element.41), channel_id=1, source_target_pairs={{16,0},{40,8},{0,16},{56,24},{48,32},{8,40},{32,48},{24,56},{80,64... | collective-permute-start | bytes 98312 | tf_op jit(solution)/shard_map/ppermute | solution.py:26
  312.5 3.1 collective-permute-start.19

commit v7 on v5

--- a/solution.py
+++ b/solution.py
@@ -60,10 +60,12 @@
     return top + jnp.log2(jnp.exp2(a - top) + jnp.exp2(b - top))
 
 
-def column_totals(partial, even, up, extra=False, cargo=None, movers=()):
+def column_totals(partial, even, up, extra=False, cargo=None, movers=(), landed=None):
     count = 2 if extra else 0
     other = swap_mate(partial[: 6 + count])
     chip = lse2(partial[:6], other[:6])
+    if landed is not None:
+        chip, landed = lax.optimization_barrier((chip, landed))
     if movers:
         chip, cargo = lax.optimization_barrier((chip, cargo))
     to_above, to_below = chip[2:6], chip[0:4]
@@ -100,6 +102,8 @@
 
     if movers:
         return placed(total), moved
+    if landed is not None:
+        return placed(total), landed
     if not count:
         return placed(total)
     near = jnp.where(even, sent[6:], got[6:])
@@ -474,7 +478,7 @@
     rows, even, up = lax.optimization_barrier((rows, even, up))
     entries, partial, top, base = first_step(pair_mask, rows, targets)
     total, (above, below) = column_totals(
-        partial, even, up, False, (rows,), (lambda x: shifted(x, -2), lambda x: shifted(x, 2))
+        partial, even, up, landed=(shifted(rows, -2), shifted(rows, 2))
     )
     (partial,) = later_step(False, pair_mask, entries, -total, base, top, rows, targets)
     total, (mate, cross) = column_totals(

time: 330 us -> 325 us (0.985)
  waiting for transfers between devices: 22.8 us -> 18 us
    ppermute x20, waiting for transfers between devices: 18.1 us -> 13.2 us  [from_row(): return lax.ppermute(block, 'row', [(source_of(i), i) for i in range(count)])]
  transfers between devices with their start and end apart: 21 -> 21, of which waited for: 11 -> 11; matrix products, arithmetic and copies ran while one was open for 1% -> 1% of each run, Pallas kernels for 0% -> 20%
where the time goes in v7:
time: 325 us; the launch traced here: 324 us
  Pallas kernels  198 us (61%)
  starting transfers between devices  81.8 us (25%)
  blocking collectives  19.7 us (6%)
  waiting for transfers between devices  18 us (6%)
  local copies, waits for them, and re-layouts  3.48 us (1%)
    pallas_call x2, Pallas kernels, later_step(): pl.pallas_call(later_kernel, out_shape=out_shape, in_specs=[SMEM] + [VMEM...  128 us
    ppermute x20, starting transfers between devices, from_row(): return lax.ppermute(block, 'row', [(source_of(i), i) for i in range(count)])  78.3 us
    pallas_call x1, Pallas kernels, first_step(): pl.pallas_call(first_kernel, out_shape=(pltpu.VMEM((count, WINDOW * count...  65.6 us
    all_to_all x1, blocking collectives, gathered(): lax.all_to_all(copies, 'grp', 0, 0, tiled=True).reshape(-1, shard.shape[1])  19.7 us
    ppermute x20, waiting for transfers between devices, from_row(): return lax.ppermute(block, 'row', [(source_of(i), i) for i in range(count)])  13.2 us
  transfers between devices with their start and end apart: 21, of which 11 were waited for; matrix products, arithmetic and copies ran while one was open for 1% of the time, Pallas kernels for 20%

profile of v7, /device:TPU:1, one launch (start us, length us, event | category | flops | bytes accessed | tf_op | source)
XLA Modules:
  0.0 323.8 jit_solution(13349540254737291873)
XLA Ops:
  1.5 19.7 %all_to_all.10 = bf16[8,128,256]{2,1,0:T(8,128)(2,1)S(1)} all-to-all(bf16[8,128,256]{2,1,0:T(8,128)(2,1)S(1)} %broadcast_in_dim.5), channel_id=1, replica_groups=mesh['row'=96,'grp'=8] {'grp'}, dimensions={0} | all-to-all | bytes 1048576 | tf_op jit(solution)/shard_map/all_to_all | solution.py:55
  21.2 7.8 %collective-permute-start.2 = (bf16[1024,256]{1,0:T(8,128)(2,1)S(1)}, bf16[1024,256]{1,0:T(8,128)(2,1)S(1)}, u32[]{:S(2)}, u32[]{:S(2)}) collective-permute-start(bf16[1024,256]{1,0:T(8,128)(2,1)S(1)} %bitcast.36), channel_id=1, source_target_pairs={{752,0},{760,8},{0,16},{8,24},{16,32},{24,40},{32,48},{40,56},{48,... | collective-permute-start | bytes 1572872 | tf_op jit(solution)/shard_map/ppermute | solution.py:26
  28.9 14.4 %collective-permute-start.1 = (bf16[1024,256]{1,0:T(8,128)(2,1)S(1)}, bf16[1024,256]{1,0:T(8,128)(2,1)S(1)}, u32[]{:S(2)}, u32[]{:S(2)}) collective-permute-start(bf16[1024,256]{1,0:T(8,128)(2,1)S(1)} %bitcast.37), channel_id=1, source_target_pairs={{16,0},{24,8},{32,16},{40,24},{48,32},{56,40},{64,48},{72,56},{80,... | collective-permute-start | bytes 1572872 | tf_op jit(solution)/shard_map/ppermute | solution.py:26
  45.1 3.5 %all-to-all-start = ((bf16[8,128,256]{2,1,0:T(8,128)(2,1)}), bf16[8,128,256]{2,1,0:T(8,128)(2,1)S(1)}, u32[]{:S(2)}, u32[]{:S(2)}) async-start(bf16[8,128,256]{2,1,0:T(8,128)(2,1)} %broadcast_in_dim.4), calls=%async_computation | async-start | bytes 1048576 | tf_op jit(solution)/shard_map/all_to_all | solution.py:55
  48.6 4.6 %collective-permute-start = (bf16[1024,256]{1,0:T(8,128)(2,1)S(1)}, bf16[1024,256]{1,0:T(8,128)(2,1)S(1)}, u32[]{:S(2)}, u32[]{:S(2)}) collective-permute-start(bf16[1024,256]{1,0:T(8,128)(2,1)S(1)} %bitcast.38), channel_id=1, source_target_pairs={{8,0},{0,8},{24,16},{16,24},{40,32},{32,40},{56,48},{48,56},{72,64... | collective-permute-start | bytes 1572872 | tf_op jit(solution)/shard_map/ppermute | solution.py:26
  54.1 4.1 %collective-permute-start.3 = (bf16[1024,256]{1,0:T(8,128)(2,1)}, bf16[1024,256]{1,0:T(8,128)(2,1)S(1)}, u32[]{:S(2)}, u32[]{:S(2)}) collective-permute-start(bf16[1024,256]{1,0:T(8,128)(2,1)} %broadcast_select_fusion.1), channel_id=1, source_target_pairs={{8,0},{0,8},{24,16},{16,24},{40,32},{32,40},{56,48},{48,56},{72,64... | collective-permute-start | bytes 1572872 | tf_op jit(solution)/shard_map/ppermute | solution.py:26
  58.3 4.8 %all-to-all-done = bf16[8,128,256]{2,1,0:T(8,128)(2,1)S(1)} async-done(((bf16[8,128,256]{2,1,0:T(8,128)(2,1)}), bf16[8,128,256]{2,1,0:T(8,128)(2,1)S(1)}, u32[]{:S(2)}, u32[]{:S(2)}) %all-to-all-start) | async-done | bytes 524320 | tf_op jit(solution)/shard_map/all_to_all | solution.py:55
  65.1 6.7 %collective-permute-start.5 = (bf16[1024,256]{1,0:T(8,128)(2,1)S(1)}, bf16[1024,256]{1,0:T(8,128)(2,1)S(1)}, u32[]{:S(2)}, u32[]{:S(2)}) collective-permute-start(bf16[1024,256]{1,0:T(8,128)(2,1)S(1)} %bitcast.44), channel_id=1, source_target_pairs={{16,0},{24,8},{32,16},{40,24},{48,32},{56,40},{64,48},{72,56},{80,... | collective-permute-start | bytes 1572872 | tf_op jit(solution)/shard_map/ppermute | solution.py:26
  72.4 65.6 %first_step.1 = (f32[1024,5120]{1,0:T(8,128)S(1)}, f32[8,1024]{1,0:T(8,128)S(1)}, f32[1024,128]{1,0:T(8,128)S(1)}, f32[8,1024]{1,0:T(8,128)S(1)}) custom-call(s32[1,5]{1,0:T(1,128)S(1)} %copy-done.2, bf16[1024,256]{1,0:T(8,128)(2,1)S(1)} %bitcast.45, bf16[1024,256]{1,0:T(8,128)(2,1)S(1)} %bitcast.39, bf16[1024,256]{1,0:T(8,128)(2,1)S(1)} %collective-permute-done.t1, ...), custom_call_target="tpu_custom_call" | custom-call | flops 2684354560 | bytes 3145728 | tf_op jit(solution)/shard_map/first_step/pallas_call | solution.py:363
  141.2 4.0 %collective-permute-start.7 = (f32[4,1024]{1,0:T(4,128)S(1)}, f32[4,1024]{1,0:T(4,128)S(1)}, u32[]{:S(2)}, u32[]{:S(2)}) collective-permute-start(f32[4,1024]{1,0:T(4,128)S(1)} %get-tuple-element.84), channel_id=1, source_target_pairs={{752,0},{744,8},{32,16},{760,24},{16,32},{72,40},{64,48},{88,56},{... | collective-permute-start | bytes 49160 | tf_op jit(solution)/shard_map/ppermute | solution.py:26
  145.3 1.9 collective-permute-start.8
  147.3 2.6 collective-permute-done.7
  150.8 4.5 %collective-permute-start.9 = (f32[6,1024]{1,0:T(8,128)S(1)}, f32[6,1024]{1,0:T(8,128)S(1)}, u32[]{:S(2)}, u32[]{:S(2)}) collective-permute-start(f32[6,1024]{1,0:T(8,128)S(1)} %maximum_select_fusion), channel_id=1, source_target_pairs={{8,0},{0,8},{24,16},{16,24},{40,32},{32,40},{56,48},{48,56},{72,64... | collective-permute-start | bytes 73736 | tf_op jit(solution)/shard_map/ppermute | solution.py:26
  156.2 64.0 %later_step.2 = f32[8,1024]{1,0:T(8,128)S(1)} custom-call(s32[1,5]{1,0:T(1,128)S(1)} %copy-done.2, f32[1024,5120]{1,0:T(8,128)S(1)} %get-tuple-element.23.entries, f32[5,1024]{1,0:T(8,128)S(1)} %fusion.pot, f32[8,1024]{1,0:T(8,128)S(1)} %get-tuple-element.27.base, f32[1024,128]{1,0:T(8,128)S(1)} %get-tuple-element.28.top, bf16[1024,256]{1,0:T(8,128)(2,1)S(1)} %bitcast.46, ...), custom_call_target="tpu_custom_call" | custom-call | flops 20971520 | bytes 3145728 | tf_op jit(solution)/shard_map/later_step/pallas_call | solution.py:390
  220.1 1.9 collective-permute-start.10
  223.3 3.2 collective-permute-start.11
  226.4 1.9 collective-permute-start.12
  228.4 2.4 collective-permute-start.15
  232.9 2.4 collective-permute-start.13
  236.4 64.4 %later_step.3 = (f32[8,1024]{1,0:T(8,128)S(1)}, f32[1024,128]{1,0:T(8,128)S(1)}) custom-call(s32[1,5]{1,0:T(1,128)S(1)} %copy-done.2, f32[1024,5120]{1,0:T(8,128)S(1)} %get-tuple-element.23.entries, f32[5,1024]{1,0:T(8,128)S(1)} %fusion.1.pot, f32[8,1024]{1,0:T(8,128)S(1)} %get-tuple-element.27.base, f32[1024,128]{1,0:T(8,128)S(1)} %get-tuple-element.28.top, ...), custom_call_target="tpu_custom_call" | custom-call | flops 20971520 | bytes 3145728 | tf_op jit(solution)/shard_map/later_step/pallas_call | solution.py:390
  300.7 1.9 collective-permute-start.16
  304.0 6.8 %collective-permute-start.17 = (f32[8,1024]{1,0:T(8,128)S(1)}, f32[8,1024]{1,0:T(8,128)S(1)}, u32[]{:S(2)}, u32[]{:S(2)}) collective-permute-start(f32[8,1024]{1,0:T(8,128)S(1)} %get-tuple-element.42), channel_id=1, source_target_pairs={{752,0},{744,8},{32,16},{760,24},{16,32},{72,40},{64,48},{88,56},{... | collective-permute-start | bytes 98312 | tf_op jit(solution)/shard_map/ppermute | solution.py:26
  312.9 3.4 %collective-permute-done.18 = f32[8,1024]{1,0:T(8,128)S(1)} collective-permute-done((f32[8,1024]{1,0:T(8,128)S(1)}, f32[8,1024]{1,0:T(8,128)S(1)}, u32[]{:S(2)}, u32[]{:S(2)}) %collective-permute-start.18) | collective-permute-done | bytes 32800 | tf_op jit(solution)/shard_map/ppermute | solution.py:26
  320.0 3.9 %plan_gradients.1 = (f32[128,256]{1,0:T(8,128)}, f32[128,256]{1,0:T(8,128)}) custom-call(s32[1,5]{1,0:T(1,128)S(1)} %copy-done.2, f32[5,1024]{1,0:T(8,128)S(1)} %fusion.2.pot, f32[1024,128]{1,0:T(8,128)S(1)} %get-tuple-element.37.dual, f32[5,2,1024]{2,1,0:T(2,128)S(1)} %broadcast_select_fusion.2.around, bf16[128,256]{1,0:T(8,128)(2,1)S(1)} %copy-done, ...), custom_call_target="tpu_custom_call" | custom-call | flops 1342177280 | bytes 5242880 | tf_op jit(solution)/shard_map/plan_gradients/pallas_call | solution.py:451
  (76 shorter events, 22.0 us)
Async XLA Ops:
  21.2 32.1 %collective-permute-start.2 = (bf16[1024,256]{1,0:T(8,128)(2,1)S(1)}, bf16[1024,256]{1,0:T(8,128)(2,1)S(1)}, u32[]{:S(2)}, u32[]{:S(2)}) collective-permute-start(bf16[1024,256]{1,0:T(8,128)(2,1)S(1)} %bitcast.36), channel_id=1, source_target_pairs={{752,0},{760,8},{0,16},{8,24},{16,32},{24,40},{32,48},{40,56},{48,... | collective-permute-start | bytes 1572872 | tf_op jit(solution)/shard_map/ppermute | solution.py:26
  28.9 24.3 %collective-permute-start.1 = (bf16[1024,256]{1,0:T(8,128)(2,1)S(1)}, bf16[1024,256]{1,0:T(8,128)(2,1)S(1)}, u32[]{:S(2)}, u32[]{:S(2)}) collective-permute-start(bf16[1024,256]{1,0:T(8,128)(2,1)S(1)} %bitcast.37), channel_id=1, source_target_pairs={{16,0},{24,8},{32,16},{40,24},{48,32},{56,40},{64,48},{72,56},{80,... | collective-permute-start | bytes 1572872 | tf_op jit(solution)/shard_map/ppermute | solution.py:26
  45.1 18.1 %all-to-all-start = ((bf16[8,128,256]{2,1,0:T(8,128)(2,1)}), bf16[8,128,256]{2,1,0:T(8,128)(2,1)S(1)}, u32[]{:S(2)}, u32[]{:S(2)}) async-start(bf16[8,128,256]{2,1,0:T(8,128)(2,1)} %broadcast_in_dim.4), calls=%async_computation | async-start | bytes 1048576 | tf_op jit(solution)/shard_map/all_to_all | solution.py:55
  48.6 23.2 %collective-permute-start = (bf16[1024,256]{1,0:T(8,128)(2,1)S(1)}, bf16[1024,256]{1,0:T(8,128)(2,1)S(1)}, u32[]{:S(2)}, u32[]{:S(2)}) collective-permute-start(bf16[1024,256]{1,0:T(8,128)(2,1)S(1)} %bitcast.38), channel_id=1, source_target_pairs={{8,0},{0,8},{24,16},{16,24},{40,32},{32,40},{56,48},{48,56},{72,64... | collective-permute-start | bytes 1572872 | tf_op jit(solution)/shard_map/ppermute | solution.py:26
  54.1 17.6 %collective-permute-start.3 = (bf16[1024,256]{1,0:T(8,128)(2,1)}, bf16[1024,256]{1,0:T(8,128)(2,1)S(1)}, u32[]{:S(2)}, u32[]{:S(2)}) collective-permute-start(bf16[1024,256]{1,0:T(8,128)(2,1)} %broadcast_select_fusion.1), channel_id=1, source_target_pairs={{8,0},{0,8},{24,16},{16,24},{40,32},{32,40},{56,48},{48,56},{72,64... | collective-permute-start | bytes 1572872 | tf_op jit(solution)/shard_map/ppermute | solution.py:26
  63.1 78.0 %collective-permute-start.6 = (bf16[1024,256]{1,0:T(8,128)(2,1)S(1)}, bf16[1024,256]{1,0:T(8,128)(2,1)S(1)}, u32[]{:S(2)}, u32[]{:S(2)}) collective-permute-start(bf16[1024,256]{1,0:T(8,128)(2,1)S(1)} %bitcast.43), channel_id=1, source_target_pairs={{752,0},{760,8},{0,16},{8,24},{16,32},{24,40},{32,48},{40,56},{48,... | collective-permute-start | bytes 1572872 | tf_op jit(solution)/shard_map/ppermute | solution.py:26
  65.1 76.1 %collective-permute-start.5 = (bf16[1024,256]{1,0:T(8,128)(2,1)S(1)}, bf16[1024,256]{1,0:T(8,128)(2,1)S(1)}, u32[]{:S(2)}, u32[]{:S(2)}) collective-permute-start(bf16[1024,256]{1,0:T(8,128)(2,1)S(1)} %bitcast.44), channel_id=1, source_target_pairs={{16,0},{24,8},{32,16},{40,24},{48,32},{56,40},{64,48},{72,56},{80,... | collective-permute-start | bytes 1572872 | tf_op jit(solution)/shard_map/ppermute | solution.py:26
  71.8 0.7 copy-start.2
  138.0 3.1 collective-permute-start.4
  141.2 8.7 %collective-permute-start.7 = (f32[4,1024]{1,0:T(4,128)S(1)}, f32[4,1024]{1,0:T(4,128)S(1)}, u32[]{:S(2)}, u32[]{:S(2)}) collective-permute-start(f32[4,1024]{1,0:T(4,128)S(1)} %get-tuple-element.84), channel_id=1, source_target_pairs={{752,0},{744,8},{32,16},{760,24},{16,32},{72,40},{64,48},{88,56},{... | collective-permute-start | bytes 49160 | tf_op jit(solution)/shard_map/ppermute | solution.py:26
  145.3 5.4 %collective-permute-start.8 = (f32[4,1024]{1,0:T(4,128)S(1)}, f32[4,1024]{1,0:T(4,128)S(1)}, u32[]{:S(2)}, u32[]{:S(2)}) collective-permute-start(f32[4,1024]{1,0:T(4,128)S(1)} %get-tuple-element.85), channel_id=1, source_target_pairs={{16,0},{40,8},{0,16},{56,24},{48,32},{8,40},{32,48},{24,56},{80,64... | collective-permute-start | bytes 49160 | tf_op jit(solution)/shard_map/ppermute | solution.py:26
  150.8 5.2 %collective-permute-start.9 = (f32[6,1024]{1,0:T(8,128)S(1)}, f32[6,1024]{1,0:T(8,128)S(1)}, u32[]{:S(2)}, u32[]{:S(2)}) collective-permute-start(f32[6,1024]{1,0:T(8,128)S(1)} %maximum_select_fusion), channel_id=1, source_target_pairs={{8,0},{0,8},{24,16},{16,24},{40,32},{32,40},{56,48},{48,56},{72,64... | collective-permute-start | bytes 73736 | tf_op jit(solution)/shard_map/ppermute | solution.py:26
  156.1 163.8 %copy-start = (bf16[128,256]{1,0:T(8,128)(2,1)S(1)}, bf16[128,256]{1,0:T(8,128)(2,1)}, u32[]{:S(2)}) copy-start(bf16[128,256]{1,0:T(8,128)(2,1)} %mine.1) | copy-start | bytes 196612
  156.1 163.8 %copy-start.1 = (bf16[128,256]{1,0:T(8,128)(2,1)S(1)}, bf16[128,256]{1,0:T(8,128)(2,1)}, u32[]{:S(2)}) copy-start(bf16[128,256]{1,0:T(8,128)(2,1)} %own.1) | copy-start | bytes 196612
  220.1 3.1 collective-permute-start.10
  223.3 9.5 %collective-permute-start.11 = (f32[4,1024]{1,0:T(4,128)S(1)}, f32[4,1024]{1,0:T(4,128)S(1)}, u32[]{:S(2)}, u32[]{:S(2)}) collective-permute-start(f32[4,1024]{1,0:T(4,128)S(1)} %get-tuple-element.73), channel_id=1, source_target_pairs={{752,0},{744,8},{32,16},{760,24},{16,32},{72,40},{64,48},{88,56},{... | collective-permute-start | bytes 49160 | tf_op jit(solution)/shard_map/ppermute | solution.py:26
  226.4 6.4 %collective-permute-start.12 = (f32[4,1024]{1,0:T(4,128)S(1)}, f32[4,1024]{1,0:T(4,128)S(1)}, u32[]{:S(2)}, u32[]{:S(2)}) collective-permute-start(f32[4,1024]{1,0:T(4,128)S(1)} %get-tuple-element.74), channel_id=1, source_target_pairs={{16,0},{40,8},{0,16},{56,24},{48,32},{8,40},{32,48},{24,56},{80,64... | collective-permute-start | bytes 49160 | tf_op jit(solution)/shard_map/ppermute | solution.py:26
  228.4 7.8 %collective-permute-start.15 = (bf16[1024,256]{1,0:T(8,128)(2,1)S(1)}, bf16[1024,256]{1,0:T(8,128)(2,1)S(1)}, u32[]{:S(2)}, u32[]{:S(2)}) collective-permute-start(bf16[1024,256]{1,0:T(8,128)(2,1)S(1)} %broadcast_select_fusion), channel_id=1, source_target_pairs={{8,0},{0,8},{24,16},{16,24},{40,32},{32,40},{56,48},{48,56},{72,64... | collective-permute-start | bytes 1572872 | tf_op jit(solution)/shard_map/ppermute | solution.py:26
  230.9 5.4 %collective-permute-start.14 = (bf16[1024,256]{1,0:T(8,128)(2,1)S(1)}, bf16[1024,256]{1,0:T(8,128)(2,1)S(1)}, u32[]{:S(2)}, u32[]{:S(2)}) collective-permute-start(bf16[1024,256]{1,0:T(8,128)(2,1)S(1)} %bitcast.47), channel_id=1, source_target_pairs={{8,0},{0,8},{24,16},{16,24},{40,32},{32,40},{56,48},{48,56},{72,64... | collective-permute-start | bytes 1572872 | tf_op jit(solution)/shard_map/ppermute | solution.py:26
  232.9 3.2 %collective-permute-start.13 = (f32[6,1024]{1,0:T(8,128)S(1)}, f32[6,1024]{1,0:T(8,128)S(1)}, u32[]{:S(2)}, u32[]{:S(2)}) collective-permute-start(f32[6,1024]{1,0:T(8,128)S(1)} %maximum_select_fusion.2), channel_id=1, source_target_pairs={{8,0},{0,8},{24,16},{16,24},{40,32},{32,40},{56,48},{48,56},{72,64... | collective-permute-start | bytes 73736 | tf_op jit(solution)/shard_map/ppermute | solution.py:26
  300.7 3.1 collective-permute-start.16
  304.0 9.0 %collective-permute-start.17 = (f32[8,1024]{1,0:T(8,128)S(1)}, f32[8,1024]{1,0:T(8,128)S(1)}, u32[]{:S(2)}, u32[]{:S(2)}) collective-permute-start(f32[8,1024]{1,0:T(8,128)S(1)} %get-tuple-element.42), channel_id=1, source_target_pairs={{752,0},{744,8},{32,16},{760,24},{16,32},{72,40},{64,48},{88,56},{... | collective-permute-start | bytes 98312 | tf_op jit(solution)/shard_map/ppermute | solution.py:26
  310.8 5.6 %collective-permute-start.18 = (f32[8,1024]{1,0:T(8,128)S(1)}, f32[8,1024]{1,0:T(8,128)S(1)}, u32[]{:S(2)}, u32[]{:S(2)}) collective-permute-start(f32[8,1024]{1,0:T(8,128)S(1)} %get-tuple-element.43), channel_id=1, source_target_pairs={{16,0},{40,8},{0,16},{56,24},{48,32},{8,40},{32,48},{24,56},{80,64... | collective-permute-start | bytes 98312 | tf_op jit(solution)/shard_map/ppermute | solution.py:26
  316.5 3.1 collective-permute-start.19

commit v8 on v7

--- a/solution.py
+++ b/solution.py
@@ -101,7 +101,7 @@
         )
 
     if movers:
-        return placed(total), moved
+        return placed(total), moved + list(landed or ())
     if landed is not None:
         return placed(total), landed
     if not count:
@@ -477,17 +477,22 @@
     rows = gathered(source)
     rows, even, up = lax.optimization_barrier((rows, even, up))
     entries, partial, top, base = first_step(pair_mask, rows, targets)
-    total, (above, below) = column_totals(
-        partial, even, up, landed=(shifted(rows, -2), shifted(rows, 2))
+    total, (mate, above, below) = column_totals(
+        partial,
+        even,
+        up,
+        cargo=(rows,),
+        movers=(swap_mate,),
+        landed=(shifted(rows, -2), shifted(rows, 2)),
     )
     (partial,) = later_step(False, pair_mask, entries, -total, base, top, rows, targets)
-    total, (mate, cross) = column_totals(
+    total, (cross,) = column_totals(
         partial,
         even,
         up,
         False,
-        (rows, above, below),
-        (lambda x, a, b: swap_mate(x), lambda x, a, b: swap_mate(jnp.where(even, a, b))),
+        (above, below),
+        (lambda a, b: swap_mate(jnp.where(even, a, b)),),
     )
     partial, dual = later_step(True, pair_mask, entries, -total, base, top, rows, targets)
     total, around = column_totals(partial, even, up, True)

time: 325 us -> 320 us (0.985)
  Pallas kernels: 198 us -> 135 us
  starting transfers between devices: 81.8 us -> 141 us
    ppermute x20, starting transfers between devices: 78.3 us -> 138 us  [from_row(): return lax.ppermute(block, 'row', [(source_of(i), i) for i in range(count)])]
    pallas_call x2, Pallas kernels: 128 us -> 86 us  [later_step(): pl.pallas_call(later_kernel, out_shape=out_shape, in_specs=[SMEM] + [VMEM...]
    pallas_call x1, Pallas kernels: 65.6 us -> 44.8 us  [first_step(): pl.pallas_call(first_kernel, out_shape=(pltpu.VMEM((count, WINDOW * count...]
  transfers between devices with their start and end apart: 21 -> 21, of which waited for: 11 -> 10; matrix products, arithmetic and copies ran while one was open for 1% -> 1% of each run, Pallas kernels for 20% -> 14%
where the time goes in v8:
time: 320 us; the launch traced here: 322 us
  starting transfers between devices  141 us (44%)
  Pallas kernels  135 us (42%)
  blocking collectives  19.7 us (6%)
  waiting for transfers between devices  19.7 us (6%)
  local copies, waits for them, and re-layouts  3.48 us (1%)
    ppermute x20, starting transfers between devices, from_row(): return lax.ppermute(block, 'row', [(source_of(i), i) for i in range(count)])  138 us
    pallas_call x2, Pallas kernels, later_step(): pl.pallas_call(later_kernel, out_shape=out_shape, in_specs=[SMEM] + [VMEM...  86 us
    pallas_call x1, Pallas kernels, first_step(): pl.pallas_call(first_kernel, out_shape=(pltpu.VMEM((count, WINDOW * count...  44.8 us
    all_to_all x1, blocking collectives, gathered(): lax.all_to_all(copies, 'grp', 0, 0, tiled=True).reshape(-1, shard.shape[1])  19.7 us
    ppermute x20, waiting for transfers between devices, from_row(): return lax.ppermute(block, 'row', [(source_of(i), i) for i in range(count)])  14.9 us
  transfers between devices with their start and end apart: 21, of which 10 were waited for; matrix products, arithmetic and copies ran while one was open for 1% of the time, Pallas kernels for 14%

profile of v8, /device:TPU:1, one launch (start us, length us, event | category | flops | bytes accessed | tf_op | source)
XLA Modules:
  0.0 321.6 jit_solution(15790063588696963280)
XLA Ops:
  1.5 19.7 %all_to_all.10 = bf16[8,128,256]{2,1,0:T(8,128)(2,1)S(1)} all-to-all(bf16[8,128,256]{2,1,0:T(8,128)(2,1)S(1)} %broadcast_in_dim.5), channel_id=1, replica_groups=mesh['row'=96,'grp'=8] {'grp'}, dimensions={0} | all-to-all | bytes 1048576 | tf_op jit(solution)/shard_map/all_to_all | solution.py:55
  21.2 7.8 %collective-permute-start.2 = (bf16[1024,256]{1,0:T(8,128)(2,1)S(1)}, bf16[1024,256]{1,0:T(8,128)(2,1)S(1)}, u32[]{:S(2)}, u32[]{:S(2)}) collective-permute-start(bf16[1024,256]{1,0:T(8,128)(2,1)S(1)} %bitcast.36), channel_id=1, source_target_pairs={{752,0},{760,8},{0,16},{8,24},{16,32},{24,40},{32,48},{40,56},{48,... | collective-permute-start | bytes 1572872 | tf_op jit(solution)/shard_map/ppermute | solution.py:26
  28.9 14.4 %collective-permute-start.1 = (bf16[1024,256]{1,0:T(8,128)(2,1)S(1)}, bf16[1024,256]{1,0:T(8,128)(2,1)S(1)}, u32[]{:S(2)}, u32[]{:S(2)}) collective-permute-start(bf16[1024,256]{1,0:T(8,128)(2,1)S(1)} %bitcast.37), channel_id=1, source_target_pairs={{16,0},{24,8},{32,16},{40,24},{48,32},{56,40},{64,48},{72,56},{80,... | collective-permute-start | bytes 1572872 | tf_op jit(solution)/shard_map/ppermute | solution.py:26
  45.1 3.5 %all-to-all-start = ((bf16[8,128,256]{2,1,0:T(8,128)(2,1)}), bf16[8,128,256]{2,1,0:T(8,128)(2,1)S(1)}, u32[]{:S(2)}, u32[]{:S(2)}) async-start(bf16[8,128,256]{2,1,0:T(8,128)(2,1)} %broadcast_in_dim.4), calls=%async_computation | async-start | bytes 1048576 | tf_op jit(solution)/shard_map/all_to_all | solution.py:55
  48.6 4.6 %collective-permute-start = (bf16[1024,256]{1,0:T(8,128)(2,1)S(1)}, bf16[1024,256]{1,0:T(8,128)(2,1)S(1)}, u32[]{:S(2)}, u32[]{:S(2)}) collective-permute-start(bf16[1024,256]{1,0:T(8,128)(2,1)S(1)} %bitcast.38), channel_id=1, source_target_pairs={{8,0},{0,8},{24,16},{16,24},{40,32},{32,40},{56,48},{48,56},{72,64... | collective-permute-start | bytes 1572872 | tf_op jit(solution)/shard_map/ppermute | solution.py:26
  54.1 4.1 %collective-permute-start.3 = (bf16[1024,256]{1,0:T(8,128)(2,1)}, bf16[1024,256]{1,0:T(8,128)(2,1)S(1)}, u32[]{:S(2)}, u32[]{:S(2)}) collective-permute-start(bf16[1024,256]{1,0:T(8,128)(2,1)} %broadcast_select_fusion.1), channel_id=1, source_target_pairs={{8,0},{0,8},{24,16},{16,24},{40,32},{32,40},{56,48},{48,56},{72,64... | collective-permute-start | bytes 1572872 | tf_op jit(solution)/shard_map/ppermute | solution.py:26
  58.3 4.8 %all-to-all-done = bf16[8,128,256]{2,1,0:T(8,128)(2,1)S(1)} async-done(((bf16[8,128,256]{2,1,0:T(8,128)(2,1)}), bf16[8,128,256]{2,1,0:T(8,128)(2,1)S(1)}, u32[]{:S(2)}, u32[]{:S(2)}) %all-to-all-start) | async-done | bytes 524320 | tf_op jit(solution)/shard_map/all_to_all | solution.py:55
  65.1 6.7 %collective-permute-start.5 = (bf16[1024,256]{1,0:T(8,128)(2,1)S(1)}, bf16[1024,256]{1,0:T(8,128)(2,1)S(1)}, u32[]{:S(2)}, u32[]{:S(2)}) collective-permute-start(bf16[1024,256]{1,0:T(8,128)(2,1)S(1)} %bitcast.44), channel_id=1, source_target_pairs={{16,0},{24,8},{32,16},{40,24},{48,32},{56,40},{64,48},{72,56},{80,... | collective-permute-start | bytes 1572872 | tf_op jit(solution)/shard_map/ppermute | solution.py:26
  72.4 44.8 %first_step.1 = (f32[1024,5120]{1,0:T(8,128)S(1)}, f32[8,1024]{1,0:T(8,128)S(1)}, f32[1024,128]{1,0:T(8,128)S(1)}, f32[8,1024]{1,0:T(8,128)S(1)}) custom-call(s32[1,5]{1,0:T(1,128)S(1)} %copy-done.2, bf16[1024,256]{1,0:T(8,128)(2,1)S(1)} %bitcast.45, bf16[1024,256]{1,0:T(8,128)(2,1)S(1)} %bitcast.39, bf16[1024,256]{1,0:T(8,128)(2,1)S(1)} %collective-permute-done.t1, ...), custom_call_target="tpu_custom_call" | custom-call | flops 2684354560 | bytes 3145728 | tf_op jit(solution)/shard_map/first_step/pallas_call | solution.py:363
  117.2 27.1 %collective-permute-start.4 = (f32[6,1024]{1,0:T(8,128)S(1)}, f32[6,1024]{1,0:T(8,128)S(1)}, u32[]{:S(2)}, u32[]{:S(2)}) collective-permute-start(f32[6,1024]{1,0:T(8,128)S(1)} %bitcast.51), channel_id=1, source_target_pairs={{8,0},{0,8},{24,16},{16,24},{40,32},{32,40},{56,48},{48,56},{72,64... | collective-permute-start | bytes 73736 | tf_op jit(solution)/shard_map/ppermute | solution.py:26
  145.2 1.9 collective-permute-start.7
  149.2 2.2 collective-permute-start.10
  151.4 2.6 collective-permute-done.7
  154.1 2.6 collective-permute-start.9
  157.6 42.9 %later_step.2 = f32[8,1024]{1,0:T(8,128)S(1)} custom-call(s32[1,5]{1,0:T(1,128)S(1)} %copy-done.2, f32[1024,5120]{1,0:T(8,128)S(1)} %get-tuple-element.25.entries, f32[5,1024]{1,0:T(8,128)S(1)} %fusion.pot, f32[8,1024]{1,0:T(8,128)S(1)} %get-tuple-element.32.base, f32[1024,128]{1,0:T(8,128)S(1)} %get-tuple-element.33.top, bf16[1024,256]{1,0:T(8,128)(2,1)S(1)} %bitcast.47, ...), custom_call_target="tpu_custom_call" | custom-call | flops 20971520 | bytes 3145728 | tf_op jit(solution)/shard_map/later_step/pallas_call | solution.py:390
  200.4 23.4 %collective-permute-start.11 = (f32[6,1024]{1,0:T(8,128)S(1)}, f32[6,1024]{1,0:T(8,128)S(1)}, u32[]{:S(2)}, u32[]{:S(2)}) collective-permute-start(f32[6,1024]{1,0:T(8,128)S(1)} %bitcast.50), channel_id=1, source_target_pairs={{8,0},{0,8},{24,16},{16,24},{40,32},{32,40},{56,48},{48,56},{72,64... | collective-permute-start | bytes 73736 | tf_op jit(solution)/shard_map/ppermute | solution.py:26
  228.6 2.5 collective-permute-start.15
  231.1 2.4 collective-permute-done.12
  233.6 2.4 collective-permute-start.14
  237.0 43.2 %later_step.3 = (f32[8,1024]{1,0:T(8,128)S(1)}, f32[1024,128]{1,0:T(8,128)S(1)}) custom-call(s32[1,5]{1,0:T(1,128)S(1)} %copy-done.2, f32[1024,5120]{1,0:T(8,128)S(1)} %get-tuple-element.25.entries, f32[5,1024]{1,0:T(8,128)S(1)} %fusion.1.pot, f32[8,1024]{1,0:T(8,128)S(1)} %get-tuple-element.32.base, f32[1024,128]{1,0:T(8,128)S(1)} %get-tuple-element.33.top, ...), custom_call_target="tpu_custom_call" | custom-call | flops 20971520 | bytes 3145728 | tf_op jit(solution)/shard_map/later_step/pallas_call | solution.py:390
  280.2 23.5 %collective-permute-start.16 = (f32[8,1024]{1,0:T(8,128)S(1)}, f32[8,1024]{1,0:T(8,128)S(1)}, u32[]{:S(2)}, u32[]{:S(2)}) collective-permute-start(f32[8,1024]{1,0:T(8,128)S(1)} %get-tuple-element.40), channel_id=1, source_target_pairs={{8,0},{0,8},{24,16},{16,24},{40,32},{32,40},{56,48},{48,56},{72,64... | collective-permute-start | bytes 98312 | tf_op jit(solution)/shard_map/ppermute | solution.py:26
  308.5 5.1 %collective-permute-done.17 = f32[8,1024]{1,0:T(8,128)S(1)} collective-permute-done((f32[8,1024]{1,0:T(8,128)S(1)}, f32[8,1024]{1,0:T(8,128)S(1)}, u32[]{:S(2)}, u32[]{:S(2)}) %collective-permute-start.17) | collective-permute-done | bytes 32800 | tf_op jit(solution)/shard_map/ppermute | solution.py:26
  313.8 2.8 collective-permute-start.19
  317.7 3.9 %plan_gradients.1 = (f32[128,256]{1,0:T(8,128)}, f32[128,256]{1,0:T(8,128)}) custom-call(s32[1,5]{1,0:T(1,128)S(1)} %copy-done.2, f32[5,1024]{1,0:T(8,128)S(1)} %fusion.2.pot, f32[1024,128]{1,0:T(8,128)S(1)} %get-tuple-element.41.dual, f32[5,2,1024]{2,1,0:T(2,128)S(1)} %broadcast_select_fusion.2.around, bf16[128,256]{1,0:T(8,128)(2,1)S(1)} %copy-done, ...), custom_call_target="tpu_custom_call" | custom-call | flops 1342177280 | bytes 5242880 | tf_op jit(solution)/shard_map/plan_gradients/pallas_call | solution.py:451
  (76 shorter events, 21.7 us)
Async XLA Ops:
  21.2 32.1 %collective-permute-start.2 = (bf16[1024,256]{1,0:T(8,128)(2,1)S(1)}, bf16[1024,256]{1,0:T(8,128)(2,1)S(1)}, u32[]{:S(2)}, u32[]{:S(2)}) collective-permute-start(bf16[1024,256]{1,0:T(8,128)(2,1)S(1)} %bitcast.36), channel_id=1, source_target_pairs={{752,0},{760,8},{0,16},{8,24},{16,32},{24,40},{32,48},{40,56},{48,... | collective-permute-start | bytes 1572872 | tf_op jit(solution)/shard_map/ppermute | solution.py:26
  28.9 24.3 %collective-permute-start.1 = (bf16[1024,256]{1,0:T(8,128)(2,1)S(1)}, bf16[1024,256]{1,0:T(8,128)(2,1)S(1)}, u32[]{:S(2)}, u32[]{:S(2)}) collective-permute-start(bf16[1024,256]{1,0:T(8,128)(2,1)S(1)} %bitcast.37), channel_id=1, source_target_pairs={{16,0},{24,8},{32,16},{40,24},{48,32},{56,40},{64,48},{72,56},{80,... | collective-permute-start | bytes 1572872 | tf_op jit(solution)/shard_map/ppermute | solution.py:26
  45.1 18.1 %all-to-all-start = ((bf16[8,128,256]{2,1,0:T(8,128)(2,1)}), bf16[8,128,256]{2,1,0:T(8,128)(2,1)S(1)}, u32[]{:S(2)}, u32[]{:S(2)}) async-start(bf16[8,128,256]{2,1,0:T(8,128)(2,1)} %broadcast_in_dim.4), calls=%async_computation | async-start | bytes 1048576 | tf_op jit(solution)/shard_map/all_to_all | solution.py:55
  48.6 23.2 %collective-permute-start = (bf16[1024,256]{1,0:T(8,128)(2,1)S(1)}, bf16[1024,256]{1,0:T(8,128)(2,1)S(1)}, u32[]{:S(2)}, u32[]{:S(2)}) collective-permute-start(bf16[1024,256]{1,0:T(8,128)(2,1)S(1)} %bitcast.38), channel_id=1, source_target_pairs={{8,0},{0,8},{24,16},{16,24},{40,32},{32,40},{56,48},{48,56},{72,64... | collective-permute-start | bytes 1572872 | tf_op jit(solution)/shard_map/ppermute | solution.py:26
  54.1 17.6 %collective-permute-start.3 = (bf16[1024,256]{1,0:T(8,128)(2,1)}, bf16[1024,256]{1,0:T(8,128)(2,1)S(1)}, u32[]{:S(2)}, u32[]{:S(2)}) collective-permute-start(bf16[1024,256]{1,0:T(8,128)(2,1)} %broadcast_select_fusion.1), channel_id=1, source_target_pairs={{8,0},{0,8},{24,16},{16,24},{40,32},{32,40},{56,48},{48,56},{72,64... | collective-permute-start | bytes 1572872 | tf_op jit(solution)/shard_map/ppermute | solution.py:26
  63.1 82.0 %collective-permute-start.6 = (bf16[1024,256]{1,0:T(8,128)(2,1)S(1)}, bf16[1024,256]{1,0:T(8,128)(2,1)S(1)}, u32[]{:S(2)}, u32[]{:S(2)}) collective-permute-start(bf16[1024,256]{1,0:T(8,128)(2,1)S(1)} %bitcast.43), channel_id=1, source_target_pairs={{752,0},{760,8},{0,16},{8,24},{16,32},{24,40},{32,48},{40,56},{48,... | collective-permute-start | bytes 1572872 | tf_op jit(solution)/shard_map/ppermute | solution.py:26
  65.1 80.1 %collective-permute-start.5 = (bf16[1024,256]{1,0:T(8,128)(2,1)S(1)}, bf16[1024,256]{1,0:T(8,128)(2,1)S(1)}, u32[]{:S(2)}, u32[]{:S(2)}) collective-permute-start(bf16[1024,256]{1,0:T(8,128)(2,1)S(1)} %bitcast.44), channel_id=1, source_target_pairs={{16,0},{24,8},{32,16},{40,24},{48,32},{56,40},{64,48},{72,56},{80,... | collective-permute-start | bytes 1572872 | tf_op jit(solution)/shard_map/ppermute | solution.py:26
  71.8 0.7 copy-start.2
  117.2 27.9 %collective-permute-start.4 = (f32[6,1024]{1,0:T(8,128)S(1)}, f32[6,1024]{1,0:T(8,128)S(1)}, u32[]{:S(2)}, u32[]{:S(2)}) collective-permute-start(f32[6,1024]{1,0:T(8,128)S(1)} %bitcast.51), channel_id=1, source_target_pairs={{8,0},{0,8},{24,16},{16,24},{40,32},{32,40},{56,48},{48,56},{72,64... | collective-permute-start | bytes 73736 | tf_op jit(solution)/shard_map/ppermute | solution.py:26
  145.2 8.8 %collective-permute-start.7 = (f32[4,1024]{1,0:T(4,128)S(1)}, f32[4,1024]{1,0:T(4,128)S(1)}, u32[]{:S(2)}, u32[]{:S(2)}) collective-permute-start(f32[4,1024]{1,0:T(4,128)S(1)} %get-tuple-element.88), channel_id=1, source_target_pairs={{752,0},{744,8},{32,16},{760,24},{16,32},{72,40},{64,48},{88,56},{... | collective-permute-start | bytes 49160 | tf_op jit(solution)/shard_map/ppermute | solution.py:26
  147.1 6.9 %collective-permute-start.8 = (f32[4,1024]{1,0:T(4,128)S(1)}, f32[4,1024]{1,0:T(4,128)S(1)}, u32[]{:S(2)}, u32[]{:S(2)}) collective-permute-start(f32[4,1024]{1,0:T(4,128)S(1)} %get-tuple-element.89), channel_id=1, source_target_pairs={{16,0},{40,8},{0,16},{56,24},{48,32},{8,40},{32,48},{24,56},{80,64... | collective-permute-start | bytes 49160 | tf_op jit(solution)/shard_map/ppermute | solution.py:26
  149.2 8.3 %collective-permute-start.10 = (bf16[1024,256]{1,0:T(8,128)(2,1)S(1)}, bf16[1024,256]{1,0:T(8,128)(2,1)S(1)}, u32[]{:S(2)}, u32[]{:S(2)}) collective-permute-start(bf16[1024,256]{1,0:T(8,128)(2,1)S(1)} %bitcast.46), channel_id=1, source_target_pairs={{8,0},{0,8},{24,16},{16,24},{40,32},{32,40},{56,48},{48,56},{72,64... | collective-permute-start | bytes 1572872 | tf_op jit(solution)/shard_map/ppermute | solution.py:26
  154.1 3.3 %collective-permute-start.9 = (f32[6,1024]{1,0:T(8,128)S(1)}, f32[6,1024]{1,0:T(8,128)S(1)}, u32[]{:S(2)}, u32[]{:S(2)}) collective-permute-start(f32[6,1024]{1,0:T(8,128)S(1)} %maximum_select_fusion), channel_id=1, source_target_pairs={{8,0},{0,8},{24,16},{16,24},{40,32},{32,40},{56,48},{48,56},{72,64... | collective-permute-start | bytes 73736 | tf_op jit(solution)/shard_map/ppermute | solution.py:26
  157.6 160.2 %copy-start = (bf16[128,256]{1,0:T(8,128)(2,1)S(1)}, bf16[128,256]{1,0:T(8,128)(2,1)}, u32[]{:S(2)}) copy-start(bf16[128,256]{1,0:T(8,128)(2,1)} %mine.1) | copy-start | bytes 196612
  157.6 160.2 %copy-start.1 = (bf16[128,256]{1,0:T(8,128)(2,1)S(1)}, bf16[128,256]{1,0:T(8,128)(2,1)}, u32[]{:S(2)}) copy-start(bf16[128,256]{1,0:T(8,128)(2,1)} %own.1) | copy-start | bytes 196612
  200.4 24.2 %collective-permute-start.11 = (f32[6,1024]{1,0:T(8,128)S(1)}, f32[6,1024]{1,0:T(8,128)S(1)}, u32[]{:S(2)}, u32[]{:S(2)}) collective-permute-start(f32[6,1024]{1,0:T(8,128)S(1)} %bitcast.50), channel_id=1, source_target_pairs={{8,0},{0,8},{24,16},{16,24},{40,32},{32,40},{56,48},{48,56},{72,64... | collective-permute-start | bytes 73736 | tf_op jit(solution)/shard_map/ppermute | solution.py:26
  224.7 8.8 %collective-permute-start.12 = (f32[4,1024]{1,0:T(4,128)S(1)}, f32[4,1024]{1,0:T(4,128)S(1)}, u32[]{:S(2)}, u32[]{:S(2)}) collective-permute-start(f32[4,1024]{1,0:T(4,128)S(1)} %get-tuple-element.77), channel_id=1, source_target_pairs={{752,0},{744,8},{32,16},{760,24},{16,32},{72,40},{64,48},{88,56},{... | collective-permute-start | bytes 49160 | tf_op jit(solution)/shard_map/ppermute | solution.py:26
  226.6 6.9 %collective-permute-start.13 = (f32[4,1024]{1,0:T(4,128)S(1)}, f32[4,1024]{1,0:T(4,128)S(1)}, u32[]{:S(2)}, u32[]{:S(2)}) collective-permute-start(f32[4,1024]{1,0:T(4,128)S(1)} %get-tuple-element.78), channel_id=1, source_target_pairs={{16,0},{40,8},{0,16},{56,24},{48,32},{8,40},{32,48},{24,56},{80,64... | collective-permute-start | bytes 49160 | tf_op jit(solution)/shard_map/ppermute | solution.py:26
  228.6 8.3 %collective-permute-start.15 = (bf16[1024,256]{1,0:T(8,128)(2,1)S(1)}, bf16[1024,256]{1,0:T(8,128)(2,1)S(1)}, u32[]{:S(2)}, u32[]{:S(2)}) collective-permute-start(bf16[1024,256]{1,0:T(8,128)(2,1)S(1)} %broadcast_select_fusion), channel_id=1, source_target_pairs={{8,0},{0,8},{24,16},{16,24},{40,32},{32,40},{56,48},{48,56},{72,64... | collective-permute-start | bytes 1572872 | tf_op jit(solution)/shard_map/ppermute | solution.py:26
  233.6 3.3 %collective-permute-start.14 = (f32[6,1024]{1,0:T(8,128)S(1)}, f32[6,1024]{1,0:T(8,128)S(1)}, u32[]{:S(2)}, u32[]{:S(2)}) collective-permute-start(f32[6,1024]{1,0:T(8,128)S(1)} %maximum_select_fusion.2), channel_id=1, source_target_pairs={{8,0},{0,8},{24,16},{16,24},{40,32},{32,40},{56,48},{48,56},{72,64... | collective-permute-start | bytes 73736 | tf_op jit(solution)/shard_map/ppermute | solution.py:26
  280.2 24.3 %collective-permute-start.16 = (f32[8,1024]{1,0:T(8,128)S(1)}, f32[8,1024]{1,0:T(8,128)S(1)}, u32[]{:S(2)}, u32[]{:S(2)}) collective-permute-start(f32[8,1024]{1,0:T(8,128)S(1)} %get-tuple-element.40), channel_id=1, source_target_pairs={{8,0},{0,8},{24,16},{16,24},{40,32},{32,40},{56,48},{48,56},{72,64... | collective-permute-start | bytes 98312 | tf_op jit(solution)/shard_map/ppermute | solution.py:26
  304.6 9.0 %collective-permute-start.17 = (f32[8,1024]{1,0:T(8,128)S(1)}, f32[8,1024]{1,0:T(8,128)S(1)}, u32[]{:S(2)}, u32[]{:S(2)}) collective-permute-start(f32[8,1024]{1,0:T(8,128)S(1)} %get-tuple-element.46), channel_id=1, source_target_pairs={{752,0},{744,8},{32,16},{760,24},{16,32},{72,40},{64,48},{88,56},{... | collective-permute-start | bytes 98312 | tf_op jit(solution)/shard_map/ppermute | solution.py:26
  306.6 7.1 %collective-permute-start.18 = (f32[8,1024]{1,0:T(8,128)S(1)}, f32[8,1024]{1,0:T(8,128)S(1)}, u32[]{:S(2)}, u32[]{:S(2)}) collective-permute-start(f32[8,1024]{1,0:T(8,128)S(1)} %get-tuple-element.47), channel_id=1, source_target_pairs={{16,0},{40,8},{0,16},{56,24},{48,32},{8,40},{32,48},{24,56},{80,64... | collective-permute-start | bytes 98312 | tf_op jit(solution)/shard_map/ppermute | solution.py:26
  313.8 3.6 %collective-permute-start.19 = (f32[14,1024]{1,0:T(8,128)S(1)}, f32[14,1024]{1,0:T(8,128)S(1)}, u32[]{:S(2)}, u32[]{:S(2)}) collective-permute-start(f32[14,1024]{1,0:T(8,128)S(1)} %pad_maximum_fusion), channel_id=1, source_target_pairs={{8,0},{0,8},{24,16},{16,24},{40,32},{32,40},{56,48},{48,56},{72,64... | collective-permute-start | bytes 172040 | tf_op jit(solution)/shard_map/ppermute | solution.py:26
